TPU v7x, 32 devices: a whole 2x2x4 slice. The times are simulated.
32 devices in a mesh: dp: 4 (over y, x), fsdp: 8 (over z, core).
Axes of the slice: x: 2, y: 2, z: 4, core: 2. Of those that a mesh axis runs over, the one named last changes fastest.
Arguments:
- hidden_in: bfloat16 [16384, 768], P(('dp', 'fsdp')), may hold values from -6 to 6
- teacher_hidden: bfloat16 [16384, 768], P(('dp', 'fsdp')), may hold values from -6 to 6
- teacher_scores: bfloat16 [16384, 12, 256], P(('dp', 'fsdp')), may hold values from -8 to 8
- seq_lengths: int32 [32, 4], P(('dp', 'fsdp')), may hold values from 16 to 256, as said below
- live_counts: int32 [32, 3], P(('dp', 'fsdp')), may hold values from 0 to 2, as said below
- triple_latent: float32 [2, 768, 2304], P(None, 'fsdp'), may hold values from -1.5 to 1.5
- mixing_latent: float32 [2, 768, 768], P(None, 'fsdp'), may hold values from -1.5 to 1.5
- widen_latent: float32 [2, 768, 3072], P(None, 'fsdp'), may hold values from -1.5 to 1.5
- narrow_latent: float32 [2, 3072, 768], P(None, 'fsdp'), may hold values from -1.5 to 1.5
- triple_bias: float32 [3, 768], P(None, 'fsdp'), may hold values from -1.2 to 1.2
- mixing_bias: float32 [768], P('fsdp'), may hold values from -1.2 to 1.2
- widen_bias: float32 [3072], P('fsdp'), may hold values from -1.2 to 1.2
- narrow_bias: float32 [768], P('fsdp'), may hold values from -1.2 to 1.2
- norm_gain: float32 [2, 768], P(None, 'fsdp'), may hold values from 0.5 to 1.5
- norm_shift: float32 [2, 768], P(None, 'fsdp'), may hold values from -1.2 to 1.2
- clip_level: float32 [4], replicated, may hold values from 0.8 to 3
Outputs:
- layer_out: bfloat16 [16384, 768], P(('dp', 'fsdp'))
- loss: float32 [], replicated
- input_grad: float32 [16384, 768], P(('dp', 'fsdp'))
- triple_latent_grad: float32 [2, 768, 2304], P(None, 'fsdp')
- mixing_latent_grad: float32 [2, 768, 768], P(None, 'fsdp')
- widen_latent_grad: float32 [2, 768, 3072], P(None, 'fsdp')
- narrow_latent_grad: float32 [2, 3072, 768], P(None, 'fsdp')
- triple_bias_grad: float32 [3, 768], P(None, 'fsdp')
- mixing_bias_grad: float32 [768], P('fsdp')
- widen_bias_grad: float32 [3072], P('fsdp')
- narrow_bias_grad: float32 [768], P('fsdp')
- norm_gain_grad: float32 [2, 768], P(None, 'fsdp')
- norm_shift_grad: float32 [2, 768], P(None, 'fsdp')
- clip_level_grad: float32 [4], replicated
Inputs may be any that keep to these rules, and one draw needn't show every extreme that they name: `seq_lengths`: slot j of every device has at most its bucket's number of rows (256, 128 or 64) and at least a quarter of it; every slot column is full on some device. `live_counts`: columns are the long, middle and short bucket; each entry is at most that bucket's number of slots, the live slots are the first ones, and some device has all its slots live.
All inputs are finite; a program needn't handle non-finite values.
Results may differ from a plain program's by a relative error of at most 0.0074.
Values sent between devices are 32-bit elements; how exact they have to be, the bound alone decides.
A program may use at most 256 MiB of HBM per device.

v0:
```python
import math

import jax
import jax.numpy as jnp
from jax import lax
from jax.sharding import PartitionSpec as P

D = 768
HEADS = 12
HEAD_DIM = 64
FF = 3072
LONG_LEN = 256
MID_LEN = 128
SHORT_LEN = 64
LONG_SLOTS = 1
MID_SLOTS = 1
SHORT_SLOTS = 2


bit_count = 32
norm_epsilon = 1e-12
masked_fill = -1e30


def soft_clip(values, clip_at):
    return clip_at * jnp.tanh(values / clip_at)


def layer_norm(values, gain_row, shift_row):
    center = values - jnp.mean(values, axis=-1, keepdims=True)
    variance = jnp.mean(center * center, axis=-1, keepdims=True)
    return center * lax.rsqrt(variance + norm_epsilon) * gain_row + shift_row


def gelu_exact(values):
    return 0.5 * values * (1.0 + lax.erf(values * (1.0 / math.sqrt(2.0))))


def pack_signs(latent):
    halves, row_count, columns = latent.shape
    sign_bits = (
        (latent > 0).astype(jnp.int32).reshape(halves, row_count, columns // bit_count, bit_count)
    )
    places = jnp.arange(bit_count, dtype=jnp.int32)
    return jnp.sum(jnp.left_shift(sign_bits, places), axis=-1, dtype=jnp.int32)


def unpack_weight(sign_words, scales):
    halves, row_count, word_count = sign_words.shape
    places = jnp.arange(bit_count, dtype=jnp.int32)
    sign_bits = jnp.bitwise_and(jnp.right_shift(sign_words[..., None], places), 1)
    sign_values = (
        (2 * sign_bits - 1).astype(jnp.float32).reshape(halves, row_count, word_count * bit_count)
    )
    return (scales[0][:, None] * sign_values[0] + scales[1][:, None] * sign_values[1]).astype(
        jnp.bfloat16
    )


def bucket_shapes():
    return ((LONG_SLOTS, LONG_LEN), (MID_SLOTS, MID_LEN), (SHORT_SLOTS, SHORT_LEN))


def bucket_masks(lengths, live_count, slot_count, bucket_len):
    places = jnp.arange(bucket_len, dtype=jnp.int32)
    key_ok = places[None, :] < lengths[:, None]
    query_ok = jnp.logical_and(
        key_ok, jnp.arange(slot_count, dtype=jnp.int32)[:, None] < live_count
    )
    return (key_ok, query_ok)


def split_heads(block, slot_count, bucket_len):
    return block.reshape(slot_count, bucket_len, HEADS, HEAD_DIM)


def bucket_scores(qkv_rows, teacher_rows, key_ok, query_ok, slot_count, bucket_len):
    queries = split_heads(qkv_rows[:, :D], slot_count, bucket_len)
    keys_part = split_heads(qkv_rows[:, D : 2 * D], slot_count, bucket_len)
    scores = jnp.einsum(
        "sqhd,skhd->shqk", queries, keys_part, preferred_element_type=jnp.float32
    ) * HEAD_DIM ** (-0.5)
    masked = jnp.where(key_ok[:, None, None, :], scores, masked_fill)
    teacher = jnp.transpose(
        teacher_rows.reshape(slot_count, bucket_len, HEADS, LONG_LEN)[..., :bucket_len],
        (0, 2, 1, 3),
    ).astype(jnp.float32)
    pair_ok = jnp.logical_and(query_ok[:, None, :, None], key_ok[:, None, None, :])
    score_gap = jnp.where(pair_ok, scores - teacher, 0.0)
    return (queries, keys_part, masked, score_gap)


def attend(qkv_rows, teacher_rows, key_ok, query_ok, slot_count, bucket_len):
    queries, keys_part, masked, score_gap = bucket_scores(
        qkv_rows, teacher_rows, key_ok, query_ok, slot_count, bucket_len
    )
    values_part = split_heads(qkv_rows[:, 2 * D :], slot_count, bucket_len)
    row_top = jnp.max(masked, axis=-1, keepdims=True)
    exponent = jnp.exp(masked - row_top)
    exp_total = jnp.sum(exponent, axis=-1, keepdims=True)
    attention = exponent / exp_total
    context = jnp.einsum(
        "shqk,skhd->sqhd",
        attention.astype(jnp.bfloat16),
        values_part,
        preferred_element_type=jnp.float32,
    )
    distill = 0.5 / LONG_LEN * jnp.sum(score_gap * score_gap)
    return (context.reshape(slot_count * bucket_len, D), row_top + jnp.log(exp_total), distill)


def attend_back(
    qkv_rows, teacher_rows, key_ok, query_ok, slot_count, bucket_len, log_total, context_grad
):
    queries, keys_part, masked, score_gap = bucket_scores(
        qkv_rows, teacher_rows, key_ok, query_ok, slot_count, bucket_len
    )
    values_part = split_heads(qkv_rows[:, 2 * D :], slot_count, bucket_len)
    attention = jnp.exp(masked - log_total)
    grad_heads = split_heads(context_grad, slot_count, bucket_len)
    values_grad = jnp.einsum(
        "shqk,sqhd->skhd",
        attention.astype(jnp.bfloat16),
        grad_heads,
        preferred_element_type=jnp.float32,
    )
    weight_grad = jnp.einsum(
        "sqhd,skhd->shqk", grad_heads, values_part, preferred_element_type=jnp.float32
    )
    score_grad = attention * (
        weight_grad - jnp.sum(weight_grad * attention, axis=-1, keepdims=True)
    ) + score_gap * (1.0 / LONG_LEN)
    score_low = score_grad.astype(jnp.bfloat16)
    score_scale = HEAD_DIM ** (-0.5)
    queries_grad = (
        jnp.einsum("shqk,skhd->sqhd", score_low, keys_part, preferred_element_type=jnp.float32)
        * score_scale
    )
    keys_grad = (
        jnp.einsum("shqk,sqhd->skhd", score_low, queries, preferred_element_type=jnp.float32)
        * score_scale
    )
    row_count = slot_count * bucket_len
    return jnp.concatenate(
        [
            queries_grad.reshape(row_count, D),
            keys_grad.reshape(row_count, D),
            values_grad.reshape(row_count, D),
        ],
        axis=-1,
    )


def on_device(
    hidden_in,
    teacher_hidden,
    teacher_scores,
    seq_lengths,
    live_counts,
    triple_latent,
    mixing_latent,
    widen_latent,
    narrow_latent,
    triple_bias,
    mixing_bias,
    widen_bias,
    narrow_bias,
    norm_gain,
    norm_shift,
    clip_level,
):
    latents = (triple_latent, mixing_latent, widen_latent, narrow_latent)
    fan_ins = (D, D, D, FF)
    own_scales = tuple(
        (
            jnp.mean(jnp.abs(latent), axis=-1) / math.sqrt(fan_in)
            for latent, fan_in in zip(latents, fan_ins)
        )
    )
    packed = tuple((pack_signs(latent) for latent in latents))
    gathered = (
        lax.all_gather(packed[0], "fsdp", axis=1, tiled=True),
        lax.all_gather(packed[1], "fsdp", axis=1, tiled=True),
        lax.all_gather(packed[2], "fsdp", axis=1, tiled=True),
        lax.all_gather(packed[3], "fsdp", axis=1, tiled=True),
    )
    factors = (
        lax.all_gather(own_scales[0], "fsdp", axis=1, tiled=True),
        lax.all_gather(own_scales[1], "fsdp", axis=1, tiled=True),
        lax.all_gather(own_scales[2], "fsdp", axis=1, tiled=True),
        lax.all_gather(own_scales[3], "fsdp", axis=1, tiled=True),
        lax.all_gather(triple_bias, "fsdp", axis=1, tiled=True),
        lax.all_gather(mixing_bias, "fsdp", axis=0, tiled=True),
        lax.all_gather(widen_bias, "fsdp", axis=0, tiled=True),
        lax.all_gather(narrow_bias, "fsdp", axis=0, tiled=True),
        lax.all_gather(norm_gain, "fsdp", axis=1, tiled=True),
        lax.all_gather(norm_shift, "fsdp", axis=1, tiled=True),
    )
    scales = factors[:4]
    triple_rows, full_mixing_bias, full_widen_bias, full_narrow_bias, gains, shifts = factors[4:]
    full_triple_bias = triple_rows.reshape(3 * D)
    weights = tuple(
        (unpack_weight(words_part, scale_part) for words_part, scale_part in zip(gathered, scales))
    )
    inputs = hidden_in.astype(jnp.float32)
    inputs_low = soft_clip(inputs, clip_level[0]).astype(jnp.bfloat16)
    qkv_all = (
        jnp.dot(inputs_low, weights[0], preferred_element_type=jnp.float32) + full_triple_bias
    ).astype(jnp.bfloat16)
    lengths = seq_lengths[0]
    counts = live_counts[0]
    plans = []
    row_start = 0
    slot_start = 0
    for bucket, shape_pair in enumerate(bucket_shapes()):
        slot_count, bucket_len = shape_pair
        key_ok, query_ok = bucket_masks(
            lengths[slot_start : slot_start + slot_count], counts[bucket], slot_count, bucket_len
        )
        plans.append(
            (
                row_start,
                row_start + slot_count * bucket_len,
                slot_count,
                bucket_len,
                key_ok,
                query_ok,
            )
        )
        row_start = row_start + slot_count * bucket_len
        slot_start = slot_start + slot_count
    contexts = []
    log_totals = []
    distill_sum = 0.0
    for plan in plans:
        row_begin, row_end, slot_count, bucket_len, key_ok, query_ok = plan
        context, log_total, distill = attend(
            qkv_all[row_begin:row_end],
            teacher_scores[row_begin:row_end],
            key_ok,
            query_ok,
            slot_count,
            bucket_len,
        )
        contexts.append(context)
        log_totals.append(log_total)
        distill_sum = distill_sum + distill
    context = jnp.concatenate(contexts, axis=0)
    token_ok = jnp.concatenate([plan[5].reshape(-1) for plan in plans])
    context_low = soft_clip(context, clip_level[1]).astype(jnp.bfloat16)
    mixed = jnp.dot(context_low, weights[1], preferred_element_type=jnp.float32) + full_mixing_bias
    first_sum = inputs + mixed
    first_norm = layer_norm(first_sum, gains[0], shifts[0])
    widen_low = soft_clip(first_norm, clip_level[2]).astype(jnp.bfloat16)
    widened = jnp.dot(widen_low, weights[2], preferred_element_type=jnp.float32) + full_widen_bias
    activated = gelu_exact(widened)
    activated_low = soft_clip(activated, clip_level[3]).astype(jnp.bfloat16)
    narrowed = (
        jnp.dot(activated_low, weights[3], preferred_element_type=jnp.float32) + full_narrow_bias
    )
    second_sum = first_norm + narrowed
    out_full = layer_norm(second_sum, gains[1], shifts[1])
    out_gap = jnp.where(token_ok[:, None], out_full - teacher_hidden.astype(jnp.float32), 0.0)
    loss_local = 0.5 * jnp.sum(out_gap * out_gap) + distill_sum
    regathered = (
        lax.all_gather(packed[0], "fsdp", axis=1, tiled=True),
        lax.all_gather(packed[1], "fsdp", axis=1, tiled=True),
        lax.all_gather(packed[2], "fsdp", axis=1, tiled=True),
        lax.all_gather(packed[3], "fsdp", axis=1, tiled=True),
    )
    back_weights = tuple(
        (
            unpack_weight(words_part, scale_part)
            for words_part, scale_part in zip(regathered, scales)
        )
    )
    _, second_back = jax.vjp(layer_norm, second_sum, gains[1], shifts[1])
    second_grad, gain_two, shift_two = second_back(out_gap)
    narrow_low = second_grad.astype(jnp.bfloat16)
    narrow_weight_grad = jnp.einsum(
        "rf,rd->fd", activated_low, narrow_low, preferred_element_type=jnp.float32
    )
    act_low_grad = jnp.einsum(
        "rd,fd->rf", narrow_low, back_weights[3], preferred_element_type=jnp.float32
    )
    _, clip_three_back = jax.vjp(soft_clip, activated, clip_level[3])
    act_grad, clip_three = clip_three_back(act_low_grad)
    _, gelu_back = jax.vjp(gelu_exact, widened)
    (widened_grad,) = gelu_back(act_grad)
    widen_grad_low = widened_grad.astype(jnp.bfloat16)
    widen_weight_grad = jnp.einsum(
        "rd,rf->df", widen_low, widen_grad_low, preferred_element_type=jnp.float32
    )
    norm_low_grad = jnp.einsum(
        "rf,df->rd", widen_grad_low, back_weights[2], preferred_element_type=jnp.float32
    )
    _, clip_two_back = jax.vjp(soft_clip, first_norm, clip_level[2])
    norm_grad, clip_two = clip_two_back(norm_low_grad)
    norm_grad = norm_grad + second_grad
    _, first_back = jax.vjp(layer_norm, first_sum, gains[0], shifts[0])
    first_grad, gain_one, shift_one = first_back(norm_grad)
    mixed_low = first_grad.astype(jnp.bfloat16)
    mixing_weight_grad = jnp.einsum(
        "rc,rd->cd", context_low, mixed_low, preferred_element_type=jnp.float32
    )
    context_low_grad = jnp.einsum(
        "rd,cd->rc", mixed_low, back_weights[1], preferred_element_type=jnp.float32
    )
    _, clip_one_back = jax.vjp(soft_clip, context, clip_level[1])
    context_grad, clip_one = clip_one_back(context_low_grad)
    context_grad_low = context_grad.astype(jnp.bfloat16)
    qkv_grads = []
    for plan, log_total in zip(plans, log_totals):
        row_begin, row_end, slot_count, bucket_len, key_ok, query_ok = plan
        qkv_grads.append(
            attend_back(
                qkv_all[row_begin:row_end],
                teacher_scores[row_begin:row_end],
                key_ok,
                query_ok,
                slot_count,
                bucket_len,
                log_total,
                context_grad_low[row_begin:row_end],
            )
        )
    qkv_grad_low = jnp.concatenate(qkv_grads, axis=0).astype(jnp.bfloat16)
    triple_weight_grad = jnp.einsum(
        "rd,re->de", inputs_low, qkv_grad_low, preferred_element_type=jnp.float32
    )
    input_low_grad = jnp.einsum(
        "re,de->rd", qkv_grad_low, back_weights[0], preferred_element_type=jnp.float32
    )
    _, clip_zero_back = jax.vjp(soft_clip, inputs, clip_level[0])
    input_side, clip_zero = clip_zero_back(input_low_grad)
    input_grad = input_side + first_grad
    bias_sums = (
        jnp.sum(qkv_grad_low, axis=0, dtype=jnp.float32).reshape(3, D),
        jnp.sum(mixed_low, axis=0, dtype=jnp.float32),
        jnp.sum(widen_grad_low, axis=0, dtype=jnp.float32),
        jnp.sum(narrow_low, axis=0, dtype=jnp.float32),
    )
    row_shares = (
        lax.psum_scatter(triple_weight_grad, "fsdp", scatter_dimension=0, tiled=True),
        lax.psum_scatter(mixing_weight_grad, "fsdp", scatter_dimension=0, tiled=True),
        lax.psum_scatter(widen_weight_grad, "fsdp", scatter_dimension=0, tiled=True),
        lax.psum_scatter(narrow_weight_grad, "fsdp", scatter_dimension=0, tiled=True),
    )
    totals = lax.psum((row_shares[0], row_shares[1], row_shares[2], row_shares[3]), "dp")
    small_sums = lax.psum(
        (
            bias_sums[0],
            bias_sums[1],
            bias_sums[2],
            bias_sums[3],
            jnp.stack([gain_one, gain_two]),
            jnp.stack([shift_one, shift_two]),
            jnp.stack([clip_zero, clip_one, clip_two, clip_three]),
            loss_local,
        ),
        ("dp", "fsdp"),
    )
    shard_index = lax.axis_index("fsdp")
    shard_parts = lax.axis_size("fsdp")

    def own_part(vector, along):
        share_width = vector.shape[along] // shard_parts
        return lax.dynamic_slice_in_dim(vector, shard_index * share_width, share_width, along)

    latent_grads = tuple(
        (
            jnp.where(jnp.abs(latent) <= 1.0, (total / math.sqrt(fan_in))[None], 0.0)
            for latent, total, fan_in in zip(latents, totals, fan_ins)
        )
    )
    loss = small_sums[7] / (hidden_in.shape[0] * D * lax.axis_size("dp") * shard_parts)
    return (
        out_full.astype(jnp.bfloat16),
        loss,
        input_grad,
        latent_grads[0],
        latent_grads[1],
        latent_grads[2],
        latent_grads[3],
        own_part(small_sums[0], 1),
        own_part(small_sums[1], 0),
        own_part(small_sums[2], 0),
        own_part(small_sums[3], 0),
        own_part(small_sums[4], 1),
        own_part(small_sums[5], 1),
        small_sums[6],
    )


def solution(mesh):
    in_specs = (
        P(("dp", "fsdp"), None),
        P(("dp", "fsdp"), None),
        P(("dp", "fsdp"), None, None),
        P(("dp", "fsdp"), None),
        P(("dp", "fsdp"), None),
        P(None, "fsdp", None),
        P(None, "fsdp", None),
        P(None, "fsdp", None),
        P(None, "fsdp", None),
        P(None, "fsdp"),
        P("fsdp"),
        P("fsdp"),
        P("fsdp"),
        P(None, "fsdp"),
        P(None, "fsdp"),
        P(),
    )
    out_specs = (
        P(("dp", "fsdp"), None),
        P(),
        P(("dp", "fsdp"), None),
        P(None, "fsdp", None),
        P(None, "fsdp", None),
        P(None, "fsdp", None),
        P(None, "fsdp", None),
        P(None, "fsdp"),
        P("fsdp"),
        P("fsdp"),
        P("fsdp"),
        P(None, "fsdp"),
        P(None, "fsdp"),
        P(),
    )
    return jax.shard_map(
        on_device, mesh=mesh, in_specs=in_specs, out_specs=out_specs, check_vma=False
    )
```

profile of v0, /device:TPU:0, one launch (start us, length us, event | category | flops | bytes accessed | tf_op | source)
XLA Modules:
  0.0 904.2 jit_solution(6892277818581372955)
XLA Ops:
  11.8 2.2 copy.236
  25.7 17.2 %all_gather.47 = s32[2,768,72]{2,0,1:T(2,128)S(1)} all-gather(s32[2,96,72]{2,0,1:T(2,128)S(1)} %copy.207), channel_id=1, replica_groups=mesh['dp'=4,'fsdp'=8] {'fsdp'}, dimensions={1}, use_global_device_ids=true | all-gather | bytes 497664 | tf_op jit(solution)/shard_map/all_gather | solution.py:182
  43.4 7.5 add_convert_fusion.2
  50.9 12.2 %fusion.171 = (f32[1,768,72,32]{1,3,2,0:T(8,128)}, f32[1,768,72,32]{1,3,2,0:T(8,128)}) fusion(f32[2,768,72,32]{1,3,2,0:T(8,128)} %add_convert_fusion.2), kind=kLoop, calls=%fused_computation.275 | loop fusion | bytes 28311552 | tf_op jit(solution)/shard_map/slice | solution.py:55
  63.1 11.9 %all-gather = f32[8,96,2]{1,2,0:T(2,128)S(1)} all-gather(f32[1,96,2]{1,2,0:T(2,128)S(1)} %multiply_bitcast_fusion.2), channel_id=1, replica_groups=mesh['dp'=4,'fsdp'=8] {'fsdp'}, dimensions={0}, use_global_device_ids=true | all-gather | bytes 6912 | tf_op jit(solution)/shard_map/all_gather | solution.py:188
  75.1 12.7 %all-gather.1 = f32[8,96,3]{1,2,0:T(4,128)S(1)} all-gather(f32[1,96,3]{1,2,0:T(4,128)S(1)} %bitcast.400), channel_id=1, replica_groups=mesh['dp'=4,'fsdp'=8] {'fsdp'}, dimensions={0}, use_global_device_ids=true | all-gather | bytes 10368 | tf_op jit(solution)/shard_map/all_gather | solution.py:192
  87.9 6.1 fusion.8
  94.1 2.7 fusion.9
  98.8 8.7 all-gather.4
  108.2 10.6 %all-gather.3 = f32[8,96,2]{1,2,0:T(2,128)S(1)} all-gather(f32[1,96,2]{1,2,0:T(2,128)} %bitcast.402), channel_id=1, replica_groups=mesh['dp'=4,'fsdp'=8] {'fsdp'}, dimensions={0}, use_global_device_ids=true | all-gather | bytes 6912 | tf_op jit(solution)/shard_map/all_gather | solution.py:196
  119.7 15.3 %all_gather.58 = s32[2,3072,24]{1,2,0:T(8,128)S(1)} all-gather(s32[2,384,24]{1,2,0:T(8,128)S(1)} %shift-left_reduce_fusion.1), channel_id=1, replica_groups=mesh['dp'=4,'fsdp'=8] {'fsdp'}, dimensions={1}, use_global_device_ids=true | all-gather | bytes 663552 | tf_op jit(solution)/shard_map/all_gather | solution.py:185
  135.0 9.9 %add_convert_fusion = f32[2,3072,24,32]{1,3,2,0:T(8,128)} fusion(s32[2,3072,24]{1,2,0:T(8,128)S(1)} %all_gather.58), kind=kLoop, calls=%fused_computation.3 | loop fusion | flops 23592960 | bytes 19464192 | tf_op jit(solution)/shard_map/convert_element_type | solution.py:53
  145.0 12.8 %fusion.170 = (f32[1,3072,24,32]{1,3,2,0:T(8,128)}, f32[1,3072,24,32]{1,3,2,0:T(8,128)}) fusion(f32[2,3072,24,32]{1,3,2,0:T(8,128)} %add_convert_fusion), kind=kLoop, calls=%fused_computation.274 | loop fusion | bytes 37748736 | tf_op jit(solution)/shard_map/slice | solution.py:55
  157.7 13.9 %all_gather.57 = f32[2,3072]{1,0:T(2,128)S(1)} all-gather(f32[2,384]{1,0:T(2,128)S(1)} %broadcast_multiply_fusion.4), channel_id=1, replica_groups=mesh['dp'=4,'fsdp'=8] {'fsdp'}, dimensions={1}, use_global_device_ids=true | all-gather | bytes 27648 | tf_op jit(solution)/shard_map/all_gather | solution.py:191
  173.1 16.2 %all_gather.55 = s32[2,768,96]{2,0,1:T(2,128)S(1)} all-gather(s32[2,96,96]{2,0,1:T(2,128)S(1)} %copy.239), channel_id=1, replica_groups=mesh['dp'=4,'fsdp'=8] {'fsdp'}, dimensions={1}, use_global_device_ids=true | all-gather | bytes 663552 | tf_op jit(solution)/shard_map/all_gather | solution.py:184
  189.7 9.7 %add_convert_fusion.1 = f32[2,768,96,32]{1,3,2,0:T(8,128)} fusion(s32[2,768,96]{1,2,0:T(8,128)S(1)} %copy.240), kind=kLoop, calls=%fused_computation.4 | loop fusion | flops 23592960 | bytes 19464192 | tf_op jit(solution)/shard_map/convert_element_type | solution.py:53
  199.4 12.3 %fusion.169 = (f32[1,768,96,32]{1,3,2,0:T(8,128)}, f32[1,768,96,32]{1,3,2,0:T(8,128)}) fusion(f32[2,768,96,32]{1,3,2,0:T(8,128)} %add_convert_fusion.1), kind=kLoop, calls=%fused_computation.273 | loop fusion | bytes 37748736 | tf_op jit(solution)/shard_map/slice | solution.py:55
  211.8 8.7 all-gather.5
  221.5 16.2 %all_gather.50 = s32[2,768,24]{2,0,1:T(2,128)S(1)} all-gather(s32[2,96,24]{2,0,1:T(2,128)S(1)} %copy.232), channel_id=1, replica_groups=mesh['dp'=4,'fsdp'=8] {'fsdp'}, dimensions={1}, use_global_device_ids=true | all-gather | bytes 165888 | tf_op jit(solution)/shard_map/all_gather | solution.py:183
  238.9 2.7 fusion.172
  241.7 10.2 %all-gather.2 = f32[8,96,2]{1,2,0:T(2,128)S(1)} all-gather(f32[1,96,2]{1,2,0:T(2,128)S(1)} %multiply_bitcast_fusion.1), channel_id=1, replica_groups=mesh['dp'=4,'fsdp'=8] {'fsdp'}, dimensions={0}, use_global_device_ids=true | all-gather | bytes 6912 | tf_op jit(solution)/shard_map/all_gather | solution.py:189
  280.4 2.3 copy.226
  288.5 14.9 %all-reduce.3 = (f32[768]{0:T(1024)}, f32[768]{0:T(1024)}) all-reduce(f32[768]{0:T(1024)} %dynamic-update-slice, f32[768]{0:T(1024)} %dynamic-update-slice.1), channel_id=1, replica_groups=mesh['dp'=4,'fsdp'=8] {'fsdp'}, use_global_device_ids=true, to_apply=%add | all-reduce | flops 1536 | bytes 12288
  303.4 2.8 fusion.19
  310.1 13.6 %all-gather.6 = f32[8,1,384]{2,1,0:T(1,128)} all-gather(f32[1,1,384]{2,1,0:T(1,128)S(1)} %reshape.683), channel_id=1, replica_groups=mesh['dp'=4,'fsdp'=8] {'fsdp'}, dimensions={0}, use_global_device_ids=true | all-gather | bytes 13824 | tf_op jit(solution)/shard_map/all_gather | solution.py:194
  327.7 10.9 %fusion.4 = bf16[3072,768]{0,1:T(8,128)(2,1)} fusion(f32[1,3072,24,32]{1,3,2,0:T(8,128)} %get-tuple-element.115, f32[1,3072,24,32]{1,3,2,0:T(8,128)} %get-tuple-element.114, f32[3072]{0:T(1024)} %bitcast.390, f32[3072]{0:T(1024)} %bitcast.389), kind=kLoop, calls=%fused_computation.8 | loop fusion | flops 9437184 | bytes 23617536 | tf_op jit(solution)/shard_map/convert_element_type | solution.py:55
  338.6 9.8 %fusion.6 = bf16[768,3072]{0,1:T(8,128)(2,1)} fusion(f32[1,768,96,32]{1,3,2,0:T(8,128)} %get-tuple-element.113, f32[1,768,96,32]{1,3,2,0:T(8,128)} %get-tuple-element.112, f32[768]{0:T(1024)} %get-tuple-element.80, f32[768]{0:T(1024)} %get-tuple-element.79), kind=kLoop, calls=%fused_computation.12 | loop fusion | flops 9437184 | bytes 23599104 | tf_op jit(solution)/shard_map/convert_element_type | solution.py:55
  348.5 6.6 fusion.123
  355.2 4.9 fusion.182
  365.0 2.5 fusion.168
  368.2 2.2 convert_reduce_fusion.2
  370.4 13.2 %multiply_reduce_fusion = (f32[]{:T(128)}, f32[]{:T(128)}, f32[3072]{0:T(1024)}, bf16[512,3072]{1,0:T(8,128)(2,1)S(1)}) fusion(f32[]{:T(128)S(6)} %div.218, f32[512,3072]{1,0:T(8,128)} %copy-done.114, f32[3072]{0:T(1024)} %bitcast.397, f32[]{:T(128)} %bitcast.40, bf16[512,768]{1,0:T(8,128)(2,1)S(1)} %get-tuple-element.100, bf16[3072,768]{0,1:T(8,128)(2,1)} %fusion.4), kind=kOutput, calls=%fused_computation.18 | convolution fusion | flops 2461529088 | bytes 14966800 | tf_op jit(solution)/shard_map/rd,fd->rf/dot_general | solution.py:283
  383.7 7.8 multiply_reduce_fusion.10
  395.0 2.9 fusion.121
  398.0 2.7 slice.245
  403.3 4.3 multiply_reduce_fusion.6
  409.2 2.6 copy.292
  411.8 2.3 copy.293
  423.4 3.6 fusion.88
  430.8 3.6 fusion.89
  447.3 3.5 fusion.93
  450.8 3.4 fusion.92
  454.3 3.4 fusion.183
  457.7 6.7 fusion.71
  464.4 6.7 fusion.76
  474.8 7.7 convert_reduce_fusion.1
  483.9 5.7 fusion.120
  490.3 9.5 %fusion.122 = f32[768,3072]{1,0:T(8,128)} fusion(bf16[512,3072]{1,0:T(8,128)(2,1)} %copy-done.113, f32[]{:T(128)} %bitcast.41, f32[512,768]{1,0:T(8,128)} %copy-done.13, f32[768]{0:T(1024)S(1)} %copy-done.97, f32[768]{0:T(1024)S(1)} %copy-done.78, f32[512]{0:T(512)S(1)} %copy-done.85, f32[512]{0:T(512)S(1)} %copy-done.68), kind=kOutput, calls=%fused_computation.194 | convolution fusion | flops 2418671616 | bytes 14166020 | tf_op jit(solution)/shard_map/rd,rf->df/dot_general | solution.py:291
  500.5 8.4 fusion.91
  509.1 56.8 %reduce-scatter.5.cloned.1.call-done = f32[96,2304]{1,0:T(8,128)} async-done(((f32[768,2304]{1,0:T(8,128)}), f32[96,2304]{1,0:T(8,128)}) %reduce-scatter.5.cloned.1.call-update) | async-done | bytes 884752 | tf_op jit(solution)/shard_map/reduce_scatter | solution.py:344
  565.9 100.2 %reduce-scatter.9.cloned.1.call-done = f32[96,3072]{1,0:T(8,128)} async-done(((f32[768,3072]{1,0:T(8,128)}), f32[96,3072]{1,0:T(8,128)}) %reduce-scatter.9.cloned.1.call-update) | async-done | bytes 1179664 | tf_op jit(solution)/shard_map/reduce_scatter | solution.py:346
  666.1 100.1 %reduce-scatter.11.cloned.1.call-done = f32[384,768]{1,0:T(8,128)} async-done(((f32[3072,768]{1,0:T(8,128)}), f32[384,768]{1,0:T(8,128)}) %reduce-scatter.11.cloned.1.call-update) | async-done | bytes 1179664 | tf_op jit(solution)/shard_map/reduce_scatter | solution.py:347
  769.7 8.8 fusion.21
  781.9 2.8 multiply_reduce_fusion.3
  789.5 39.2 %all-reduce.2 = (f32[]{:T(128)}, f32[3,768]{1,0:T(4,128)S(1)}, f32[768]{0:T(1024)S(1)}, f32[3072]{0:T(1024)S(1)}, f32[768]{0:T(1024)S(1)}, /*index=5*/f32[2,768]{1,0:T(2,128)S(1)}, f32[2,768]{1,0:T(2,128)S(1)}, f32[4]{0:T(128)}) all-reduce(f32[]{:T(128)S(6)} %add.236, ...), channel_id=1, replica_groups=mesh['dp'=4,'fsdp'=8] {'dp','fsdp'}, use_global_device_ids=true, to_apply=%region_22.23 | all-reduce | flops 9989 | bytes 79912 | tf_op jit(solution)/shard_map/psum | solution.py:350
  833.1 29.8 %all-reduce.7.cloned.1.call-done = (f32[96,2304]{1,0:T(8,128)}, f32[96,768]{1,0:T(8,128)}, f32[96,3072]{1,0:T(8,128)}, f32[384,768]{1,0:T(8,128)}) async-done(((f32[96,2304]{1,0:T(8,128)}, f32[96,768]{1,0:T(8,128)}, f32[96,3072]{1,0:T(8,128)}, f32[384,768]{1,0:T(8,128)}), (f32[96,2304]{1,0:T(8,128)}, f32[96,768]{1,0:T(8,128)}, f32[96,3072]{1,0:T(8,128)}, f32[384,768]{1,0:T(8,128)})) %all-reduce.7.cloned.1.call-update) | async-done | bytes 3538960 | tf_op jit(solution)/shard_map/psum | solution.py:349
  868.3 3.0 copy.272
  872.6 2.4 copy.273
  874.9 2.4 broadcast_multiply_fusion.1
  877.3 2.9 copy.270
  880.2 3.5 compare_select_fusion
  883.7 3.4 copy.274
  890.0 3.0 compare_select_fusion.1
  893.0 3.0 copy.275
  (391 shorter events, 121.4 us)
Async XLA Ops:
  7.2 501.9 %reduce-scatter.7.cloned.1.call-start = ((), (), s32[]{:S(2)}) async-start(), calls=%async_computation.5 | async-start | bytes 2654208 | tf_op jit(solution)/shard_map/reduce_scatter | solution.py:345
  50.9 24.2 %copy-start.101 = (f32[3,96]{1,0:T(4,128)S(1)}, f32[3,96]{1,0:T(4,128)}, u32[]{:S(2)}) copy-start(f32[3,96]{1,0:T(4,128)} %param.25) | copy-start | bytes 3460
  87.9 6.1 copy-start.108
  96.8 22.5 %copy-start.10 = (s32[2,384,768]{1,2,0:T(8,128)S(1)}, s32[2,384,768]{1,2,0:T(8,128)}, u32[]{:S(2)}) copy-start(s32[2,384,768]{1,2,0:T(8,128)} %compare_convert_fusion.1) | copy-start | bytes 7077892
  145.0 27.3 %copy-start.6 = (s32[2,96,3072]{1,2,0:T(8,128)S(1)}, s32[2,96,3072]{1,2,0:T(8,128)}, u32[]{:S(2)}) copy-start(s32[2,96,3072]{1,2,0:T(8,128)} %compare_convert_fusion) | copy-start | bytes 7077892
  199.4 12.3 %copy-start.94 = (f32[2,96]{1,0:T(2,128)S(1)}, f32[2,96]{1,0:T(2,128)}, u32[]{:S(2)}) copy-start(f32[2,96]{1,0:T(2,128)} %abs_reduce_fusion) | copy-start | bytes 2308
  241.7 18.7 %copy-start.20 = (bf16[512,12,256]{2,0,1:T(8,128)(2,1)S(1)}, bf16[512,12,256]{2,0,1:T(8,128)(2,1)}, u32[]{:S(2)}) copy-start(bf16[512,12,256]{2,0,1:T(8,128)(2,1)} %param.18) | copy-start | bytes 9437188
  257.8 3.9 copy-start.106
  260.4 5.1 copy-start.23
  261.8 4.6 copy-start.29
  261.9 4.5 copy-start.79
  262.6 3.7 copy-start.59
  270.4 4.4 copy-start.27
  270.6 4.3 copy-start.26
  282.7 23.6 %copy-start.46 = (f32[128,768]{1,0:T(8,128)S(1)}, f32[128,768]{1,0:T(8,128)}, u32[]{:S(2)}) copy-start(f32[128,768]{1,0:T(8,128)} %copy.227) | copy-start | bytes 1179652
  306.3 3.7 copy-start.102
  348.5 6.6 copy-start.14
  348.5 6.6 copy-start.17
  348.5 6.7 copy-start.66
  348.5 6.7 copy-start.76
  348.5 6.7 copy-start.80
  348.5 6.7 copy-start.83
  348.5 6.7 copy-start.95
  348.5 6.7 copy-start.111
  355.1 5.1 copy-start.114
  355.2 7.9 copy-start.107
  355.2 7.9 copy-start.19
  355.2 7.9 copy-start.61
  355.2 7.9 copy-start.62
  370.4 13.2 %copy-start.38 = (bf16[512,768]{1,0:T(8,128)(2,1)}, bf16[512,768]{1,0:T(8,128)(2,1)S(1)}, u32[]{:S(2)}) copy-start(bf16[512,768]{1,0:T(8,128)(2,1)S(1)} %get-tuple-element.100) | copy-start | bytes 2359300
  370.4 13.2 %copy-start.12 = (f32[512,768]{1,0:T(8,128)S(1)}, f32[512,768]{1,0:T(8,128)}, u32[]{:S(2)}) copy-start(f32[512,768]{1,0:T(8,128)} %get-tuple-element.111) | copy-start | bytes 4718596
  370.4 13.2 %copy-start.15 = (f32[512,768]{1,0:T(8,128)S(1)}, f32[512,768]{1,0:T(8,128)}, u32[]{:S(2)}) copy-start(f32[512,768]{1,0:T(8,128)} %copy-done.13) | copy-start | bytes 4718596
  370.4 13.2 %copy-start.67 = (f32[512]{0:T(512)S(1)}, f32[512]{0:T(512)}, u32[]{:S(2)}) copy-start(f32[512]{0:T(512)} %copy-done.65) | copy-start | bytes 6148
  370.4 13.2 %copy-start.77 = (f32[768]{0:T(1024)S(1)}, f32[768]{0:T(1024)}, u32[]{:S(2)}) copy-start(f32[768]{0:T(1024)} %get-tuple-element.161) | copy-start | bytes 9220
  370.4 13.2 %copy-start.84 = (f32[512]{0:T(512)S(1)}, f32[512]{0:T(512)}, u32[]{:S(2)}) copy-start(f32[512]{0:T(512)} %fusion.131) | copy-start | bytes 6148
  370.4 13.2 %copy-start.91 = (f32[512]{0:T(512)S(1)}, f32[512]{0:T(512)}, u32[]{:S(2)}) copy-start(f32[512]{0:T(512)} %negate_multiply_fusion.1) | copy-start | bytes 6148
  370.4 13.2 %copy-start.96 = (f32[768]{0:T(1024)S(1)}, f32[768]{0:T(1024)}, u32[]{:S(2)}) copy-start(f32[768]{0:T(1024)} %get-tuple-element.78) | copy-start | bytes 9220
  383.6 7.9 copy-start.113
  383.6 7.8 copy-start.70
  397.9 168.0 %reduce-scatter.5.cloned.1.call-start = ((), (), s32[]{:S(2)}) async-start(), calls=%async_computation.4 | async-start | bytes 7962624 | tf_op jit(solution)/shard_map/reduce_scatter | solution.py:344
  423.4 7.4 copy-start.24
  436.7 14.1 %copy-start.42 = (bf16[128,768]{0,1:T(8,128)(2,1)S(1)}, bf16[128,768]{0,1:T(8,128)(2,1)}, u32[]{:S(2)}) copy-start(bf16[128,768]{0,1:T(8,128)(2,1)} %copy-done.41) | copy-start | bytes 589828
  443.7 7.1 copy-start.60
  464.4 6.7 copy-start.64
  464.4 6.7 copy-start.88
  471.1 3.6 copy-start.44
  471.1 3.6 copy-start.45
  471.1 3.6 copy-start.49
  471.1 3.6 copy-start.50
  471.1 3.6 copy-start.53
  474.7 9.2 %copy-start.110 = (bf16[512,768]{1,0:T(8,128)(2,1)S(1)}, bf16[512,768]{1,0:T(8,128)(2,1)}, u32[]{:S(2)}) copy-start(bf16[512,768]{1,0:T(8,128)(2,1)} %param.16) | copy-start | bytes 2359300
  489.6 176.5 %reduce-scatter.9.cloned.1.call-start = ((), (), s32[]{:S(2)}) async-start(), calls=%async_computation.6 | async-start | bytes 10616832 | tf_op jit(solution)/shard_map/reduce_scatter | solution.py:346
  499.8 266.3 %reduce-scatter.11.cloned.1.call-start = ((), (), s32[]{:S(2)}) async-start(), calls=%async_computation.7 | async-start | bytes 10616832 | tf_op jit(solution)/shard_map/reduce_scatter | solution.py:347
  508.9 258.5 %copy-start.74 = (f32[768]{0:T(1024)S(1)}, f32[768]{0:T(1024)}, u32[]{:S(2)}) copy-start(f32[768]{0:T(1024)} %get-tuple-element.65) | copy-start | bytes 9220
  509.0 258.5 %copy-start.99 = (f32[768]{0:T(1024)S(1)}, f32[768]{0:T(1024)}, u32[]{:S(2)}) copy-start(f32[768]{0:T(1024)} %get-tuple-element.60) | copy-start | bytes 9220
  509.0 258.6 %copy-start.73 = (f32[768]{0:T(1024)S(1)}, f32[768]{0:T(1024)}, u32[]{:S(2)}) copy-start(f32[768]{0:T(1024)} %get-tuple-element.64) | copy-start | bytes 9220
  509.0 258.6 %copy-start.98 = (f32[768]{0:T(1024)S(1)}, f32[768]{0:T(1024)}, u32[]{:S(2)}) copy-start(f32[768]{0:T(1024)} %get-tuple-element.72) | copy-start | bytes 9220
  509.0 260.7 %copy-start.90 = (f32[512]{0:T(512)S(1)}, f32[512]{0:T(512)}, u32[]{:S(2)}) copy-start(f32[512]{0:T(512)} %copy-done.89) | copy-start | bytes 6148
  509.0 353.9 %all-reduce.7.cloned.1.call-start = ((), (), s32[]{:S(2)}) async-start(), calls=%async_computation.8 | async-start | bytes 7077888 | tf_op jit(solution)/shard_map/psum | solution.py:349
  778.5 10.9 %copy-start.71 = (f32[768]{0:T(1024)S(1)}, f32[768]{0:T(1024)}, u32[]{:S(2)}) copy-start(f32[768]{0:T(1024)} %get-tuple-element.99) | copy-start | bytes 9220
  778.5 10.9 %copy-start.72 = (f32[768]{0:T(1024)S(1)}, f32[768]{0:T(1024)}, u32[]{:S(2)}) copy-start(f32[768]{0:T(1024)} %get-tuple-element.103) | copy-start | bytes 9220
  778.5 10.9 %copy-start.82 = (f32[3072]{0:T(1024)S(1)}, f32[3072]{0:T(1024)}, u32[]{:S(2)}) copy-start(f32[3072]{0:T(1024)} %get-tuple-element.118) | copy-start | bytes 36868
  784.7 81.9 %copy-start.5 = (f32[2,96,2304]{1,2,0:T(8,128)S(1)}, f32[2,96,2304]{1,2,0:T(8,128)}, u32[]{:S(2)}) copy-start(f32[2,96,2304]{1,2,0:T(8,128)} %copy-done.4) | copy-start | bytes 5308420
  872.6 7.6 copy-start.1
  (56 other events, 116.3 us)
Sparse Core Ops, SparseCore 0:
  398.0 35.0 reduce-scatter.6
  489.7 76.0 reduce-scatter.4
  568.2 97.8 reduce-scatter.8
  668.2 97.8 reduce-scatter.10
  769.4 93.4 all-reduce.6
where the time goes:
time: 915 us; the launch traced here: 904 us
  waiting for transfers between devices  287 us (31%)
  blocking collectives  209 us (23%)
  local copies, waits for them, and re-layouts  136 us (15%)
  matrix products  123 us (13%)
  other arithmetic  116 us (13%)
  between operations  32.8 us (4%)
    reduce_scatter x1, waiting for transfers between devices, on_device(): lax.psum_scatter(widen_weight_grad, 'fsdp', scatter_dimension=0, tiled=True)  100 us
    reduce_scatter x1, waiting for transfers between devices, on_device(): lax.psum_scatter(narrow_weight_grad, 'fsdp', scatter_dimension=0, tiled=T...  100 us
    reduce_scatter x1, waiting for transfers between devices, on_device(): lax.psum_scatter(triple_weight_grad, 'fsdp', scatter_dimension=0, tiled=T...  56.8 us
    unnamed x253, local copies, waits for them, and re-layouts  41.3 us
    slice x4, local copies, waits for them, and re-layouts, unpack_weight(): sign_values[0]  40 us
    psum x1, blocking collectives, on_device(): lax.psum((bias_sums[0], bias_sums[1], bias_sums[2], bias_sums[3], jnp.sta...  39.2 us
    psum x1, waiting for transfers between devices, on_device(): lax.psum((row_shares[0], row_shares[1], row_shares[2], row_shares[3]), 'dp')  29.8 us
    convert_element_type x4, other arithmetic, unpack_weight(): (scales[0][:, None] * sign_values[0] + scales[1][:, None] * sign_values[1...  29.7 us
  transfers between devices with their start and end apart: 5, of which 4 were waited for; matrix products, arithmetic and copies ran while one was open for 14% of the time, Pallas kernels for 0%

commit v1 on v0

--- a/solution.py
+++ b/solution.py
@@ -3,6 +3,8 @@
 import jax
 import jax.numpy as jnp
 from jax import lax
+from jax.experimental import pallas as pl
+from jax.experimental.pallas import tpu as pltpu
 from jax.sharding import PartitionSpec as P
 
 D = 768
@@ -392,6 +394,836 @@
     )
 
 
+bf16 = jnp.bfloat16
+f32 = jnp.float32
+MESH = pl.DeviceIdType.MESH
+VMEM_CAP = 60 * 1024 * 1024
+ROWS = LONG_SLOTS * LONG_LEN + MID_SLOTS * MID_LEN + SHORT_SLOTS * SHORT_LEN
+BLOCK = 96
+CHUNK = 512
+CHUNKS = 18
+SLOTS = 4
+
+
+def dot_nn(a, b):
+    return lax.dot_general(a, b, (((1,), (0,)), ((), ())), preferred_element_type=f32)
+
+
+def dot_nt(a, b):
+    return lax.dot_general(a, b, (((1,), (1,)), ((), ())), preferred_element_type=f32)
+
+
+def dot_tn(a, b):
+    return lax.dot_general(a, b, (((0,), (0,)), ((), ())), preferred_element_type=f32)
+
+
+def loop(count, step, body):
+    def run(i, carry):
+        body(pl.multiple_of(i * step, step))
+        return carry
+
+    lax.fori_loop(0, count, run, 0)
+
+
+def latent_piece(refs, block, half, group):
+    triple, mixing, widen, narrow = refs
+    rows = pl.ds(group * 8, 8)
+    if block < 3:
+        return triple[half, rows, block * D : (block + 1) * D]
+    if block == 3:
+        return mixing[half, rows, :]
+    if block < 8:
+        return widen[half, rows, (block - 4) * D : (block - 3) * D]
+    return narrow[half, pl.ds((block - 8) * BLOCK + group * 8, 8), :]
+
+
+def plane_of(block, half, group):
+    place = block * 24 + half * 12 + group
+    bit = place % 32
+    return place // 32, (1 << bit) if bit < 31 else -(1 << 31)
+
+
+def gather_kernel(
+    triple, mixing, widen, narrow, tb, mb, wb, nb, gain, shift,
+    words, small, spread, wsend, wrecv, ssend, srecv, cwsend, cwrecv, cssend, csrecv,
+):
+    dp = lax.axis_index("dp")
+    me = lax.axis_index("fsdp")
+    z = lax.div(me, 2)
+    core = lax.rem(me, 2)
+    refs = (triple, mixing, widen, narrow)
+    masks = [[] for _ in range(9)]
+    for block in range(12):
+        for half in range(2):
+            for group in range(12):
+                word, bit = plane_of(block, half, group)
+                masks[word].append((block, half, group, bit))
+    for word in range(9):
+        total = jnp.zeros((8, D), jnp.int32)
+        for block, half, group, bit in masks[word]:
+            piece = latent_piece(refs, block, half, group)
+            total = total | jnp.where(piece > 0, jnp.int32(bit), jnp.int32(0))
+        words[me, word * 8 : (word + 1) * 8, :] = total
+    lane = lax.broadcasted_iota(jnp.int32, (8, 128), 1)
+
+    def scale_rows(group, carry):
+        tile = jnp.zeros((8, 128), f32)
+        rows = pl.ds(pl.multiple_of(group * 8, 8), 8)
+        for half in range(2):
+            for index in range(7):
+                if index == 0:
+                    part = triple[half, rows, :]
+                elif index == 1:
+                    part = mixing[half, rows, :]
+                elif index == 2:
+                    part = widen[half, rows, :]
+                else:
+                    part = narrow[
+                        half, pl.ds(pl.multiple_of((index - 3) * BLOCK + group * 8, 8), 8), :
+                    ]
+                fan = FF if index >= 3 else D
+                mean = jnp.sum(jnp.abs(part), axis=1, keepdims=True) * (1.0 / part.shape[1])
+                tile = jnp.where(lane == index * 2 + half, mean / math.sqrt(fan), tile)
+        small[me, rows, :] = tile
+        return carry
+
+    lax.fori_loop(0, 12, scale_rows, 0)
+    spread[...] = jnp.zeros_like(spread)
+    spread[0:3, 0:BLOCK] = tb[...]
+    spread[3:4, 0:BLOCK] = mb[...]
+    spread[4:5, 0:BLOCK] = nb[...]
+    spread[5:7, 0:BLOCK] = gain[...]
+    spread[7:9, 0:BLOCK] = shift[...]
+    spread[16:17, 0 : 4 * BLOCK] = wb[...]
+    placed = pltpu.roll(spread[0:16, :], me * BLOCK, 1)
+    wide = pltpu.roll(spread[16:24, :], core * (4 * BLOCK), 1)
+    row = lax.broadcasted_iota(jnp.int32, (16, D), 0)
+    wide_rows = jnp.broadcast_to(wide[0:1, :], (16, D))
+    placed = placed + jnp.where(row == 9 + z, wide_rows, 0.0)
+    for part in range(6):
+        small[me, 96 + part * 16 : 112 + part * 16, :] = placed[:, part * 128 : (part + 1) * 128]
+
+    def over_z(hop, ref, send, recv):
+        peer = lax.rem(z + hop, 4) * 2 + core
+        return pltpu.make_async_remote_copy(
+            src_ref=ref.at[me], dst_ref=ref.at[me], send_sem=send.at[hop - 1],
+            recv_sem=recv.at[hop - 1], device_id=(dp, peer), device_id_type=MESH,
+        )
+
+    def over_core(hop, ref, send, recv):
+        owner = lax.rem(z + 4 - hop, 4) * 2 + core
+        return pltpu.make_async_remote_copy(
+            src_ref=ref.at[owner], dst_ref=ref.at[owner], send_sem=send.at[hop],
+            recv_sem=recv.at[hop], device_id=(dp, z * 2 + 1 - core), device_id_type=MESH,
+        )
+
+    for hop in (1, 2, 3):
+        over_z(hop, small, ssend, srecv).start()
+    for hop in (1, 2, 3):
+        over_z(hop, words, wsend, wrecv).start()
+    over_core(0, small, cssend, csrecv).start()
+    over_core(0, words, cwsend, cwrecv).start()
+    for hop in (1, 2, 3):
+        over_z(hop, small, ssend, srecv).wait()
+        over_core(hop, small, cssend, csrecv).start()
+    for hop in (1, 2, 3):
+        over_z(hop, words, wsend, wrecv).wait()
+        over_core(hop, words, cwsend, cwrecv).start()
+    for hop in range(4):
+        over_core(hop, small, cssend, csrecv).wait()
+        over_core(hop, words, cwsend, cwrecv).wait()
+
+
+def gather(triple, mixing, widen, narrow, tb, mb, wb, nb, gain, shift):
+    vm = pl.BlockSpec(memory_space=pltpu.VMEM)
+    return pl.pallas_call(
+        gather_kernel,
+        out_shape=(
+            jax.ShapeDtypeStruct((8, 72, D), jnp.int32),
+            jax.ShapeDtypeStruct((8, 192, 128), f32),
+        ),
+        in_specs=[vm] * 10,
+        out_specs=(vm, vm),
+        scratch_shapes=[pltpu.VMEM((24, D), f32)]
+        + [pltpu.SemaphoreType.DMA((3,))] * 4
+        + [pltpu.SemaphoreType.DMA((4,))] * 4,
+        compiler_params=pltpu.CompilerParams(has_side_effects=True, vmem_limit_bytes=VMEM_CAP),
+        name="gather_weights",
+    )(triple, mixing, widen, narrow, tb, mb, wb, nb, gain, shift)
+
+
+def unpack_block(words, small, block, dst):
+    index = 0 if block < 3 else 1 if block == 3 else 2 if block < 8 else block - 5
+
+    def one(owner, carry):
+        for pair in range(6):
+            parts = []
+            for group in (2 * pair, 2 * pair + 1):
+                total = None
+                for half in range(2):
+                    word, bit = plane_of(block, half, group)
+                    bits = words[owner, word * 8 : (word + 1) * 8, :] & jnp.int32(bit)
+                    column = index * 2 + half
+                    scale = jnp.broadcast_to(
+                        small[owner, group * 8 : (group + 1) * 8, column : column + 1], (8, D)
+                    )
+                    value = jnp.where(bits != 0, scale, -scale)
+                    total = value if total is None else total + value
+                parts.append(total)
+            tile = jnp.concatenate(parts, axis=0).astype(bf16)
+            if block < 8:
+                start = owner * BLOCK + pair * 16
+            else:
+                start = owner * (4 * BLOCK) + (block - 8) * BLOCK + pair * 16
+            rows = pl.ds(pl.multiple_of(start, 16), 16)
+            if block < 3:
+                dst[rows, block * D : (block + 1) * D] = tile
+            elif block < 8 and block > 3:
+                dst[rows, (block - 4) * D : (block - 3) * D] = tile
+            else:
+                dst[rows, :] = tile
+        return carry
+
+    lax.fori_loop(0, 8, one, 0)
+
+
+def clip_back(grad, value, level, inverse):
+    u = value * inverse
+    t = jnp.tanh(u)
+    slope = 1.0 - t * t
+    return grad * slope, jnp.sum(grad * (t - u * slope), axis=0, keepdims=True)
+
+
+def norm_rows(v):
+    center = v - jnp.mean(v, axis=1, keepdims=True)
+    variance = jnp.mean(center * center, axis=1, keepdims=True)
+    rstd = lax.rsqrt(variance + norm_epsilon)
+    return center * rstd, rstd
+
+
+def norm_rows_back(grad, hat, rstd, gain_row):
+    g = grad * gain_row
+    return rstd * (
+        g - jnp.mean(g, axis=1, keepdims=True) - hat * jnp.mean(g * hat, axis=1, keepdims=True)
+    )
+
+
+def colsum(v):
+    return jnp.sum(v, axis=0, keepdims=True)
+
+
+HALF_ROOT = 1.0 / math.sqrt(2.0)
+DENSITY = 1.0 / math.sqrt(2.0 * math.pi)
+
+
+def layer_kernel(
+    seq, live, level, words, small, hid, teach, teach_scores,
+    out, input_grad, xlT, clT, wlT, nlT, act, wg, mlow, qg, sums,
+    wt, wm, ww, wn, prm, bias, wbias, qkv, low, ctx, hat1, rstd1, widened, acc, gacc, sgrad,
+    cgrad, valid, pair,
+):
+    c0, c1, c2, c3 = level[0], level[1], level[2], level[3]
+    i0, i1, i2, i3 = 1.0 / c0, 1.0 / c1, 1.0 / c2, 1.0 / c3
+    for part in range(6):
+        total = small[0, 96 + part * 16 : 112 + part * 16, :]
+        for owner in range(1, 8):
+            total = total + small[owner, 96 + part * 16 : 112 + part * 16, :]
+        prm[:, part * 128 : (part + 1) * 128] = total
+    for part in range(3):
+        bias[0:1, part * D : (part + 1) * D] = prm[part : part + 1, :]
+    for part in range(4):
+        wbias[0:1, part * D : (part + 1) * D] = prm[9 + part : 10 + part, :]
+    sums[...] = jnp.zeros_like(sums)
+    row = lax.broadcasted_iota(jnp.int32, (256, 256), 0)
+    col = lax.broadcasted_iota(jnp.int32, (256, 256), 1)
+    key_ok = col < seq[0, 0]
+    query_ok = row < seq[0, 0] * live[0, 0]
+    valid[0] = jnp.where(key_ok, 1.0, 0.0)
+    pair[0] = jnp.where(key_ok & query_ok, 1.0, 0.0)
+
+    def in_slots(at):
+        mid = (at < 128) & (at < seq[0, 1])
+        one = (at >= 128) & (at < 192) & (at - 128 < seq[0, 2])
+        two = (at >= 192) & (at - 192 < seq[0, 3])
+        return mid, one, two
+
+    km, ko, kt = in_slots(col)
+    qm, qo, qt = in_slots(row)
+    key_ok = (km & (row < 128)) | (ko & (row >= 128) & (row < 192)) | (kt & (row >= 192))
+    live_mid = row * 0 + live[0, 1] > 0
+    live_one = row * 0 + live[0, 2] > 0
+    live_two = row * 0 + live[0, 2] > 1
+    query_ok = (qm & live_mid) | (qo & live_one) | (qt & live_two)
+    valid[1] = jnp.where(key_ok, 1.0, 0.0)
+    pair[1] = jnp.where(key_ok & query_ok, 1.0, 0.0)
+    ones = jnp.where(query_ok, 1.0, 0.0)
+
+    for block in range(12):
+        unpack_block(
+            words, small, block, wt if block < 3 else wm if block == 3 else ww if block < 8 else wn
+        )
+
+    def clip_in(r):
+        x = hid[pl.ds(r, 128), :].astype(f32)
+        lo = (c0 * jnp.tanh(x * i0)).astype(bf16)
+        low[pl.ds(r, 128), :] = lo
+        xlT[:, pl.ds(r, 128)] = lo.T
+
+    loop(4, 128, clip_in)
+
+    def qkv_cols(c):
+        cs = pl.ds(c, 256)
+        qkv[:, cs] = (dot_nn(low[...], wt[:, cs]) + bias[0:1, cs]).astype(bf16)
+
+    loop(9, 256, qkv_cols)
+    lane = lax.broadcasted_iota(jnp.int32, (256, 128), 1)
+    first = lane < 64
+
+    def pick(v, j):
+        return jnp.where(first, v, jnp.zeros_like(v)) if j == 0 else jnp.where(first, jnp.zeros_like(v), v)
+
+    def softmax(q, k, ok, j):
+        s = dot_nt(pick(q, j), k) * (HEAD_DIM**-0.5)
+        masked = jnp.where(ok, s, masked_fill)
+        e = jnp.exp(masked - jnp.max(masked, axis=1, keepdims=True))
+        return s, e / jnp.sum(e, axis=1, keepdims=True)
+
+    def attend_pair(u, carry):
+        g = lax.div(u, 6)
+        hp = lax.rem(u, 6)
+        rs = pl.ds(pl.multiple_of(g * 256, 256), 256)
+        qs = pl.multiple_of(hp * 128, 128)
+        q = qkv[rs, pl.ds(qs, 128)]
+        k = qkv[rs, pl.ds(pl.multiple_of(D + qs, 128), 128)]
+        v = qkv[rs, pl.ds(pl.multiple_of(2 * D + qs, 128), 128)]
+        ok = valid[g] > 0.5
+        parts = []
+        for j in range(2):
+            s, p = softmax(q, k, ok, j)
+            parts.append(dot_nn(p.astype(bf16), v))
+        ctx[rs, pl.ds(qs, 128)] = jnp.where(first, parts[0], parts[1])
+        return carry
+
+    lax.fori_loop(0, 12, attend_pair, 0)
+
+    def clip_ctx(r):
+        lo = (c1 * jnp.tanh(ctx[pl.ds(r, 128), :] * i1)).astype(bf16)
+        low[pl.ds(r, 128), :] = lo
+        clT[:, pl.ds(r, 128)] = lo.T
+
+    loop(4, 128, clip_ctx)
+
+    def mix_cols(c):
+        cs = pl.ds(c, 256)
+        acc[:, cs] = dot_nn(low[...], wm[:, cs]) + prm[3:4, cs] + hid[:, cs].astype(f32)
+
+    loop(3, 256, mix_cols)
+
+    def norm_one(r):
+        rs = pl.ds(r, 128)
+        hat, rstd = norm_rows(acc[rs, :])
+        hat1[rs, :] = hat
+        rstd1[rs, :] = jnp.broadcast_to(rstd, (128, 128))
+        normed = hat * prm[5:6, :] + prm[7:8, :]
+        lo = (c2 * jnp.tanh(normed * i2)).astype(bf16)
+        low[rs, :] = lo
+        wlT[:, rs] = lo.T
+        acc[rs, :] = normed + prm[4:5, :]
+
+    loop(4, 128, norm_one)
+
+    def feed(c):
+        cs = pl.ds(c, 512)
+        w = dot_nn(low[...], ww[:, cs]) + wbias[0:1, cs]
+        widened[:, cs] = w
+        a = 0.5 * w * (1.0 + lax.erf(w * HALF_ROOT))
+        lo = (c3 * jnp.tanh(a * i3)).astype(bf16)
+        act[:, cs] = lo
+        acc[...] += dot_nn(lo, wn[cs, :])
+
+    loop(6, 512, feed)
+
+    def norm_two(r):
+        rs = pl.ds(r, 128)
+        hat, rstd = norm_rows(acc[rs, :])
+        full = hat * prm[6:7, :] + prm[8:9, :]
+        out[rs, :] = full.astype(bf16)
+        at = lax.broadcasted_iota(jnp.int32, (128, D), 0) + r
+        l0, l1, l2, l3 = seq[0, 0] * live[0, 0], seq[0, 1], seq[0, 2], seq[0, 3]
+        l1 = jnp.where(live[0, 1] > 0, l1, 0)
+        l2 = jnp.where(live[0, 2] > 0, l2, 0)
+        l3 = jnp.where(live[0, 2] > 1, l3, 0)
+        ok = (at < l0) | ((at >= 256) & (at < 256 + l1)) | ((at >= 384) & (at < 384 + l2))
+        ok = ok | ((at >= 448) & (at < 448 + l3))
+        gap = jnp.where(ok, full - teach[rs, :].astype(f32), 0.0)
+        sums[15:16, :] += colsum(gap * gap) * 0.5
+        sums[6:7, :] += colsum(gap * hat)
+        sums[8:9, :] += colsum(gap)
+        grad = norm_rows_back(gap, hat, rstd, prm[6:7, :])
+        sgrad[rs, :] = grad
+        lo = grad.astype(bf16)
+        low[rs, :] = lo
+        nlT[:, rs] = lo.T
+        sums[4:5, :] += colsum(lo.astype(f32))
+
+    loop(4, 128, norm_two)
+    gacc[...] = sgrad[...] * 0.0
+
+    def feed_back(t, carry):
+        cs = pl.ds(pl.multiple_of(t * 512, 512), 512)
+        g = dot_nt(low[...], wn[cs, :])
+        w = widened[:, cs]
+        e = 0.5 * (1.0 + lax.erf(w * HALF_ROOT))
+        a = w * e
+        u = a * i3
+        th = jnp.tanh(u)
+        slope = 1.0 - th * th
+        clip_sum = colsum(g * (th - u * slope))
+        sums[14:15, 0:512] += clip_sum
+        back = g * slope * (e + w * (DENSITY * jnp.exp(-0.5 * w * w)))
+        lo = back.astype(bf16)
+        wg[:, cs] = lo
+        wbias[1:2, cs] = colsum(lo.astype(f32))
+        gacc[...] += dot_nt(lo, ww[:, cs])
+        return carry
+
+    lax.fori_loop(0, 6, feed_back, 0)
+    for part in range(4):
+        sums[9 + part : 10 + part, :] = wbias[1:2, part * D : (part + 1) * D]
+    def norm_one_back(r):
+        rs = pl.ds(r, 128)
+        hat = hat1[rs, :]
+        normed = hat * prm[5:6, :] + prm[7:8, :]
+        grad, clip_sum = clip_back(gacc[rs, :], normed, c2, i2)
+        sums[18:19, :] += clip_sum
+        grad = grad + sgrad[rs, :]
+        sums[5:6, :] += colsum(grad * hat)
+        sums[7:8, :] += colsum(grad)
+        grad = norm_rows_back(grad, hat, rstd1[rs, 0:1], prm[5:6, :])
+        acc[rs, :] = grad
+        lo = grad.astype(bf16)
+        mlow[rs, :] = lo
+        sums[3:4, :] += colsum(lo.astype(f32))
+
+    loop(4, 128, norm_one_back)
+
+    def mix_back(c):
+        cs = pl.ds(c, 256)
+        g = dot_nt(mlow[...], wm[cs, :])
+        grad, clip_sum = clip_back(g, ctx[:, cs], c1, i1)
+        sums[17:18, cs] += clip_sum
+        cgrad[:, cs] = grad.astype(bf16)
+
+    loop(3, 256, mix_back)
+
+    def attend_pair_back(u, carry):
+        g = lax.div(u, 6)
+        hp = lax.rem(u, 6)
+        rs = pl.ds(pl.multiple_of(g * 256, 256), 256)
+        q0 = pl.multiple_of(hp * 128, 128)
+        k0 = pl.multiple_of(D + q0, 128)
+        v0 = pl.multiple_of(2 * D + q0, 128)
+        q = qkv[rs, pl.ds(q0, 128)]
+        k = qkv[rs, pl.ds(k0, 128)]
+        v = qkv[rs, pl.ds(v0, 128)]
+        cg = cgrad[rs, pl.ds(q0, 128)]
+        ok = valid[g] > 0.5
+        pairs = pair[g] > 0.5
+        dq, dk, dv = [], [], []
+        for j in range(2):
+            s, p = softmax(q, k, ok, j)
+            ts = teach_scores[2 * hp + j, rs, :].astype(f32)
+            second = pltpu.roll(ts[128:192], 128, 1)
+            third = pltpu.roll(ts[192:256], 192, 1)
+            moved = jnp.concatenate([ts[0:128], second, third], axis=0)
+            ts = jnp.where(g > 0, moved, ts)
+            gap = jnp.where(pairs, s - ts, 0.0)
+            sums[16:17, 0:256] += colsum(gap * gap) * (0.5 / LONG_LEN)
+            pg = dot_nt(pick(cg, j), v)
+            sg = p * (pg - jnp.sum(pg * p, axis=1, keepdims=True)) + gap * (1.0 / LONG_LEN)
+            sg = sg.astype(bf16)
+            dv.append(dot_tn(p.astype(bf16), cg))
+            dq.append(dot_nn(sg, k))
+            dk.append(dot_tn(sg, q))
+        scale = HEAD_DIM**-0.5
+        dq = (jnp.where(first, dq[0], dq[1]) * scale).astype(bf16)
+        dk = (jnp.where(first, dk[0], dk[1]) * scale).astype(bf16)
+        dv = jnp.where(first, dv[0], dv[1]).astype(bf16)
+        for index, (grad, at) in enumerate(((dq, q0), (dk, k0), (dv, v0))):
+            qg[rs, pl.ds(at, 128)] = grad
+            sums[index : index + 1, pl.ds(q0, 128)] += colsum(grad.astype(f32))
+        return carry
+
+    lax.fori_loop(0, 12, attend_pair_back, 0)
+
+    def input_back(c):
+        cs = pl.ds(c, 256)
+        g = dot_nt(qg[...], wt[cs, :])
+        grad, clip_sum = clip_back(g, hid[:, cs].astype(f32), c0, i0)
+        sums[19:20, cs] += clip_sum
+        input_grad[:, cs] = grad + acc[:, cs]
+
+    loop(3, 256, input_back)
+    at = lax.broadcasted_iota(jnp.int32, (1, D), 1)
+    line = jnp.zeros((1, D), f32)
+    for spot, value in enumerate(
+        (sums[19:20, :], sums[17:18, :], sums[18:19, :], sums[14:15, :], sums[15:16, :] + sums[16:17, :])
+    ):
+        line = jnp.where(at == spot, jnp.sum(value), line)
+    sums[13:14, :] = line
+
+
+def layer(seq, live, level, words, small, hid, teach, teach_scores):
+    vm = pl.BlockSpec(memory_space=pltpu.VMEM)
+    sm = pl.BlockSpec(memory_space=pltpu.SMEM)
+    sds = jax.ShapeDtypeStruct
+    return pl.pallas_call(
+        layer_kernel,
+        out_shape=(
+            sds((ROWS, D), bf16),
+            sds((ROWS, D), f32),
+            sds((D, ROWS), bf16),
+            sds((D, ROWS), bf16),
+            sds((D, ROWS), bf16),
+            sds((D, ROWS), bf16),
+            sds((ROWS, FF), bf16),
+            sds((ROWS, FF), bf16),
+            sds((ROWS, D), bf16),
+            sds((ROWS, 3 * D), bf16),
+            sds((24, D), f32),
+        ),
+        in_specs=[sm] * 3 + [vm] * 5,
+        out_specs=(vm,) * 11,
+        scratch_shapes=[
+            pltpu.VMEM((D, 3 * D), bf16),
+            pltpu.VMEM((D, D), bf16),
+            pltpu.VMEM((D, FF), bf16),
+            pltpu.VMEM((FF, D), bf16),
+            pltpu.VMEM((16, D), f32),
+            pltpu.VMEM((8, 3 * D), f32),
+            pltpu.VMEM((8, FF), f32),
+            pltpu.VMEM((ROWS, 3 * D), bf16),
+            pltpu.VMEM((ROWS, D), bf16),
+            pltpu.VMEM((ROWS, D), f32),
+            pltpu.VMEM((ROWS, D), f32),
+            pltpu.VMEM((ROWS, 128), f32),
+            pltpu.VMEM((ROWS, FF), f32),
+            pltpu.VMEM((ROWS, D), f32),
+            pltpu.VMEM((ROWS, D), f32),
+            pltpu.VMEM((ROWS, D), f32),
+            pltpu.VMEM((ROWS, D), bf16),
+            pltpu.VMEM((2, 256, 256), f32),
+            pltpu.VMEM((2, 256, 256), f32),
+        ],
+        compiler_params=pltpu.CompilerParams(vmem_limit_bytes=VMEM_CAP),
+        name="layer",
+    )(seq, live, level, words, small, hid, teach, teach_scores)
+
+
+def reduce_kernel(
+    nlT, act, wlT, wg, clT, ml, xlT, qg, sums,
+    fin, small_out,
+    pt, rb, rx, ry, rz, sin,
+    s1, r1, s2, r2, s3, r3, s4, r4, s5, r5, s6, r6, sms, smr,
+):
+    dp = lax.axis_index("dp")
+    me = lax.axis_index("fsdp")
+    x = lax.rem(dp, 2)
+    y = lax.div(dp, 2)
+    z = lax.div(me, 2)
+    core = lax.rem(me, 2)
+    flip_x = dp + 1 - 2 * x
+    flip_y = dp + 2 - 4 * y
+
+    def turns(k):
+        odd = lax.rem(k, 2)
+        one = flip_x * (1 - odd) + flip_y * odd
+        two = flip_y * (1 - odd) + flip_x * odd
+        a = x * (1 - odd) + y * odd
+        b = y * (1 - odd) + x * odd
+        return one, two, a, b
+
+    def rows_at(start, count):
+        return pl.ds(pl.multiple_of(start, 8), count)
+
+    def core_copy(k):
+        slot = lax.rem(k, SLOTS)
+        return pltpu.make_async_remote_copy(
+            src_ref=pt.at[slot, :, 1 - core], dst_ref=rb.at[slot], send_sem=s1.at[slot],
+            recv_sem=r1.at[slot], device_id=(dp, z * 2 + 1 - core), device_id_type=MESH,
+        )
+
+    def one_copy(k):
+        slot = lax.rem(k, SLOTS)
+        one, two, a, b = turns(k)
+        return pltpu.make_async_remote_copy(
+            src_ref=pt.at[slot, :, core, rows_at((1 - a) * 48, 48)], dst_ref=rx.at[slot],
+            send_sem=s2.at[slot], recv_sem=r2.at[slot], device_id=(one, me), device_id_type=MESH,
+        )
+
+    def two_copy(k):
+        slot = lax.rem(k, SLOTS)
+        one, two, a, b = turns(k)
+        return pltpu.make_async_remote_copy(
+            src_ref=pt.at[slot, :, core, rows_at(a * 48 + (1 - b) * 24, 24)], dst_ref=ry.at[slot],
+            send_sem=s3.at[slot], recv_sem=r3.at[slot], device_id=(two, me), device_id_type=MESH,
+        )
+
+    def z_copy(k, hop):
+        slot = lax.rem(k, SLOTS)
+        one, two, a, b = turns(k)
+        to = lax.rem(z + hop, 4)
+        return pltpu.make_async_remote_copy(
+            src_ref=pt.at[slot, to, core, rows_at(a * 48 + b * 24, 24)],
+            dst_ref=rz.at[slot, hop - 1], send_sem=s4.at[slot, hop - 1],
+            recv_sem=r4.at[slot, hop - 1], device_id=(dp, to * 2 + core), device_id_type=MESH,
+        )
+
+    def fin_rows(k, start, count):
+        section = lax.div(k, 6)
+        return fin.at[
+            section, rows_at(start, count),
+            pl.ds(pl.multiple_of(lax.rem(k, 6) * CHUNK, CHUNK), CHUNK),
+        ]
+
+    def back_two(k):
+        slot = lax.rem(k, SLOTS)
+        one, two, a, b = turns(k)
+        ref = fin_rows(k, a * 48 + b * 24, 24)
+        return pltpu.make_async_remote_copy(
+            src_ref=ref, dst_ref=ref, send_sem=s5.at[slot], recv_sem=r5.at[slot],
+            device_id=(two, me), device_id_type=MESH,
+        )
+
+    def back_one(k):
+        slot = lax.rem(k, SLOTS)
+        one, two, a, b = turns(k)
+        ref = fin_rows(k, a * 48, 48)
+        return pltpu.make_async_remote_copy(
+            src_ref=ref, dst_ref=ref, send_sem=s6.at[slot], recv_sem=r6.at[slot],
+            device_id=(one, me), device_id_type=MESH,
+        )
+
+    def small_copy(step):
+        to = (
+            (dp, z * 2 + 1 - core), (flip_x, me), (flip_y, me),
+            (dp, lax.rem(z + 1, 4) * 2 + core), (dp, lax.rem(z + 2, 4) * 2 + core),
+            (dp, lax.rem(z + 3, 4) * 2 + core),
+        )[step]
+        return pltpu.make_async_remote_copy(
+            src_ref=small_out, dst_ref=sin.at[step], send_sem=sms.at[step],
+            recv_sem=smr.at[step], device_id=to, device_id_type=MESH,
+        )
+
+    small_out[...] = sums[0:16, :]
+
+    def tick(t, carry):
+        @pl.when(t >= 6)
+        def _():
+            back_one(t - 6).wait()
+
+        @pl.when((t >= 5) & (t < 5 + CHUNKS))
+        def _():
+            back_two(t - 5).wait()
+            back_one(t - 5).start()
+
+        @pl.when((t >= 4) & (t < 4 + CHUNKS))
+        def _():
+            k = t - 4
+            slot = lax.rem(k, SLOTS)
+            one, two, a, b = turns(k)
+            for hop in (1, 2, 3):
+                z_copy(k, hop).wait()
+            total = pt[slot, z, core, rows_at(a * 48 + b * 24, 24), :]
+            total = total + rz[slot, 0] + rz[slot, 1] + rz[slot, 2]
+            fin[
+                lax.div(k, 6), rows_at(a * 48 + b * 24, 24),
+                pl.ds(pl.multiple_of(lax.rem(k, 6) * CHUNK, CHUNK), CHUNK),
+            ] = total
+            back_two(k).start()
+
+        @pl.when((t >= 3) & (t < 3 + CHUNKS))
+        def _():
+            k = t - 3
+            slot = lax.rem(k, SLOTS)
+            one, two, a, b = turns(k)
+            two_copy(k).wait()
+            for q in range(4):
+                pt[slot, q, core, rows_at(a * 48 + b * 24, 24), :] += ry[slot, q]
+            for hop in (1, 2, 3):
+                z_copy(k, hop).start()
+
+        @pl.when((t >= 2) & (t < 2 + CHUNKS))
+        def _():
+            k = t - 2
+            slot = lax.rem(k, SLOTS)
+            one, two, a, b = turns(k)
+            one_copy(k).wait()
+            for q in range(4):
+                pt[slot, q, core, rows_at(a * 48, 48), :] += rx[slot, q]
+            two_copy(k).start()
+
+        @pl.when((t >= 1) & (t < 1 + CHUNKS))
+        def _():
+            k = t - 1
+            slot = lax.rem(k, SLOTS)
+            core_copy(k).wait()
+            for q in range(4):
+                pt[slot, q, core] += rb[slot, q]
+            one_copy(k).start()
+
+        slot = lax.rem(t, SLOTS)
+
+        @pl.when(t < 6)
+        def _():
+            j = lax.div(t, 2)
+            rows = pl.ds(pl.multiple_of(lax.rem(t, 2) * 384, 384), 384)
+            left = nlT[rows, :]
+            for owner in range(8):
+                cols = pl.ds(pl.multiple_of(owner * 384 + j * 128, 128), 128)
+                got = dot_nn(left, act[:, cols])
+                for part in range(4):
+                    pt[slot, owner // 2, owner % 2, :, part * 128 : (part + 1) * 128] = got[
+                        part * BLOCK : (part + 1) * BLOCK, :
+                    ]
+
+        def whole(left, right, half):
+            got = dot_nn(left, right)
+            for owner in range(8):
+                pt[slot, owner // 2, owner % 2, :, half * 256 : (half + 1) * 256] = got[
+                    owner * BLOCK : (owner + 1) * BLOCK, :
+                ]
+
+        @pl.when((t >= 6) & (t < 12))
+        def _():
+            for half in range(2):
+                cols = pl.ds(pl.multiple_of((t - 6) * CHUNK + half * 256, 256), 256)
+                whole(wlT[...], wg[:, cols], half)
+
+        for half in range(2):
+            part = (t - 12) * 2 + half
+
+            @pl.when((part >= 0) & (part < 3))
+            def _():
+                cols = pl.ds(pl.multiple_of(part * 256, 256), 256)
+                whole(clT[...], ml[:, cols], half)
+
+            @pl.when((part >= 3) & (part < 12))
+            def _():
+                cols = pl.ds(pl.multiple_of((part - 3) * 256, 256), 256)
+                whole(xlT[...], qg[:, cols], half)
+
+        @pl.when(t < CHUNKS)
+        def _():
+            core_copy(t).start()
+
+        @pl.when(t == 8)
+        def _():
+            small_copy(0).start()
+
+        @pl.when(t == 10)
+        def _():
+            small_copy(0).wait()
+            small_out[...] += sin[0]
+            small_copy(1).start()
+
+        @pl.when(t == 12)
+        def _():
+            small_copy(1).wait()
+            small_out[...] += sin[1]
+            small_copy(2).start()
+
+        @pl.when(t == 14)
+        def _():
+            small_copy(2).wait()
+            small_out[...] += sin[2]
+            for step in (3, 4, 5):
+                small_copy(step).start()
+
+        @pl.when(t == 16)
+        def _():
+            for step in (3, 4, 5):
+                small_copy(step).wait()
+            small_out[...] = small_out[...] + sin[3] + sin[4] + sin[5]
+
+        return carry
+
+    lax.fori_loop(0, CHUNKS + 6, tick, 0)
+
+
+def reduce_grads(nlT, act, wlT, wg, clT, ml, xlT, qg, sums):
+    vm = pl.BlockSpec(memory_space=pltpu.VMEM)
+    sds = jax.ShapeDtypeStruct
+    dma = pltpu.SemaphoreType.DMA
+    return pl.pallas_call(
+        reduce_kernel,
+        out_shape=(sds((3, BLOCK, FF), f32), sds((16, D), f32)),
+        in_specs=[vm] * 9,
+        out_specs=(vm, vm),
+        scratch_shapes=[
+            pltpu.VMEM((SLOTS, 4, 2, BLOCK, CHUNK), f32),
+            pltpu.VMEM((SLOTS, 4, BLOCK, CHUNK), f32),
+            pltpu.VMEM((SLOTS, 4, 48, CHUNK), f32),
+            pltpu.VMEM((SLOTS, 4, 24, CHUNK), f32),
+            pltpu.VMEM((SLOTS, 3, 24, CHUNK), f32),
+            pltpu.VMEM((6, 16, D), f32),
+        ]
+        + [dma((SLOTS,))] * 6
+        + [dma((SLOTS, 3))] * 2
+        + [dma((SLOTS,))] * 4
+        + [dma((6,))] * 2,
+        compiler_params=pltpu.CompilerParams(has_side_effects=True, vmem_limit_bytes=VMEM_CAP),
+        name="reduce_grads",
+    )(nlT, act, wlT, wg, clT, ml, xlT, qg, sums)
+
+
+def on_device_fast(
+    hidden_in, teacher_hidden, teacher_scores, seq_lengths, live_counts, triple_latent,
+    mixing_latent, widen_latent, narrow_latent, triple_bias, mixing_bias, widen_bias, narrow_bias,
+    norm_gain, norm_shift, clip_level,
+):
+    words, small = gather(
+        triple_latent, mixing_latent, widen_latent, narrow_latent, triple_bias,
+        mixing_bias[None], widen_bias[None], narrow_bias[None], norm_gain, norm_shift,
+    )
+    teach_scores = jnp.transpose(teacher_scores, (1, 0, 2))
+    out, input_grad, xlT, clT, wlT, nlT, act, wg, ml, qg, sums = layer(
+        seq_lengths, live_counts, clip_level, words, small, hidden_in, teacher_hidden, teach_scores
+    )
+    fin, small_sum = reduce_grads(nlT, act, wlT, wg, clT, ml, xlT, qg, sums)
+    narrow_sum = (
+        fin[0].reshape(BLOCK, 3, 2, 4, 128).transpose(1, 4, 2, 3, 0).reshape(4 * BLOCK, D)
+    )
+    totals = (fin[2][:, D:], fin[2][:, :D], fin[1], narrow_sum)
+    latents = (triple_latent, mixing_latent, widen_latent, narrow_latent)
+    latent_grads = tuple(
+        (
+            jnp.where(jnp.abs(latent) <= 1.0, (total / math.sqrt(fan_in))[None], 0.0)
+            for latent, total, fan_in in zip(latents, totals, (D, D, D, FF))
+        )
+    )
+    me = lax.axis_index("fsdp")
+    own = lax.dynamic_slice_in_dim(small_sum[0:9], me * BLOCK, BLOCK, 1)
+    wide = lax.dynamic_slice_in_dim(small_sum[9:13].reshape(FF), me * 4 * BLOCK, 4 * BLOCK, 0)
+    tokens = hidden_in.shape[0] * lax.axis_size("dp") * lax.axis_size("fsdp")
+    return (
+        out,
+        small_sum[13, 4] / (tokens * D),
+        input_grad,
+        latent_grads[0],
+        latent_grads[1],
+        latent_grads[2],
+        latent_grads[3],
+        own[0:3],
+        own[3],
+        wide,
+        own[4],
+        own[5:7],
+        own[7:9],
+        small_sum[13, 0:4],
+    )
+
+
 def solution(mesh):
     in_specs = (
         P(("dp", "fsdp"), None),
@@ -427,6 +1259,7 @@
         P(None, "fsdp"),
         P(),
     )
+    fits = mesh.shape["dp"] == 4 and mesh.shape["fsdp"] == 8
     return jax.shard_map(
-        on_device, mesh=mesh, in_specs=in_specs, out_specs=out_specs, check_vma=False
-    )
+        on_device_fast if fits else on_device, mesh=mesh, in_specs=in_specs, out_specs=out_specs, check_vma=False
+    )

time: 915 us -> 394 us (0.43); the launches traced: 904 us -> 394 us
  Pallas kernels: 0 us -> 364 us
  waiting for transfers between devices: 287 us -> 0 us
  blocking collectives: 209 us -> 0 us
  matrix products: 123 us -> 0 us
  local copies, waits for them, and re-layouts: 136 us -> 17.2 us
  other arithmetic: 116 us -> 10.6 us
  between operations: 32.8 us -> 2.48 us
    pallas_call x0 -> x3, Pallas kernels: none -> 364 us  [the longest x1 239 us: reduce_grads(): pl.pallas_call(reduce_kernel, out_shape=(sds((3, BLOCK, FF), f32), sds((1...]
    reduce_scatter x4 -> x0, waiting for transfers between devices: 257 us -> none  [the longest x1 100 us: on_device(): lax.psum_scatter(widen_weight_grad, 'fsdp', scatter_dimension=0, tiled=True)]
    all_gather x12 -> x0, blocking collectives: 155 us -> none  [the longest x1 17.2 us: on_device(): lax.all_gather(packed[0], 'fsdp', axis=1, tiled=True)]
    dot_general x30 -> x0, matrix products: 123 us -> none  [the longest x3 13.8 us: attend_back(): jnp.einsum('shqk,sqhd->skhd', score_low, queries, preferred_element_type=...]
    convert_element_type x8 -> x0, other arithmetic: 57.7 us -> none  [the longest x4 29.7 us: unpack_weight(): (scales[0][:, None] * sign_values[0] + scales[1][:, None] * sign_values[1...]
    slice x27 -> x4, local copies, waits for them, and re-layouts: 58.8 us -> 4.74 us  [the longest x1 1.41 us: on_device_fast(): own[7:9]]
    psum x1 -> x0, blocking collectives: 39.2 us -> none  [on_device(): lax.psum((bias_sums[0], bias_sums[1], bias_sums[2], bias_sums[3], jnp.sta...]
    unnamed x253 -> x10, local copies, waits for them, and re-layouts: 41.3 us -> 2.56 us
  transfers between devices with their start and end apart: 5 -> 0, of which waited for: 4 -> 0; matrix products, arithmetic and copies ran while one was open for 14% -> 0% of each run, Pallas kernels for 0% -> 0%
where the time goes in v1:
time: 394 us
  Pallas kernels  364 us (92%)
  local copies, waits for them, and re-layouts  17.2 us (4%)
  other arithmetic  10.6 us (3%)
    pallas_call x1, Pallas kernels, reduce_grads(): pl.pallas_call(reduce_kernel, out_shape=(sds((3, BLOCK, FF), f32), sds((1...  239 us
    pallas_call x1, Pallas kernels, layer(): pl.pallas_call(layer_kernel, out_shape=(sds((ROWS, D), bf16), sds((ROWS,...  82 us
    pallas_call x1, Pallas kernels, gather(): pl.pallas_call(gather_kernel, out_shape=(jax.ShapeDtypeStruct((8, 72, D),...  42.8 us

profile of v1, /device:TPU:0, one launch (start us, length us, event | category | flops | bytes accessed | tf_op | source)
XLA Modules:
  0.0 393.9 jit_solution(5244855934001664378)
XLA Ops:
  0.6 1.2 broadcast_in_dim.64.wb
  1.9 42.8 %gather_weights.1 = (s32[8,72,768]{2,1,0:T(8,128)}, f32[8,192,128]{2,1,0:T(8,128)}) custom-call(f32[2,96,2304]{2,1,0:T(8,128)} %triple.1, f32[2,96,768]{2,1,0:T(8,128)} %mixing.1, f32[2,96,3072]{2,1,0:T(8,128)} %widen.1, f32[2,384,768]{2,1,0:T(8,128)} %narrow.1, f32[3,96]{1,0:T(4,128)} %tb.1, f32[1,96]{1,0:T(1,128)} %bitcast.21, ...), custom_call_target="tpu_custom_call" | custom-call | tf_op jit(solution)/shard_map/gather_weights/pallas_call | solution.py:539
  44.7 82.0 %layer.1 = (bf16[512,768]{1,0:T(8,128)(2,1)}, f32[512,768]{1,0:T(8,128)}, bf16[768,512]{1,0:T(8,128)(2,1)}, bf16[768,512]{1,0:T(8,128)(2,1)}, bf16[768,512]{1,0:...) custom-call(s32[1,4]{1,0:T(1,128)} %seq.1, ...), custom_call_target="tpu_custom_call" | custom-call | tf_op jit(solution)/shard_map/layer/pallas_call | solution.py:880
  126.7 238.8 %reduce_grads.1 = (f32[3,96,3072]{2,1,0:T(8,128)}, f32[16,768]{1,0:T(8,128)}) custom-call(bf16[768,512]{1,0:T(8,128)(2,1)} %get-tuple-element.32.nlT, bf16[512,3072]{1,0:T(8,128)(2,1)} %get-tuple-element.33.act, bf16[768,512]{1,0:T(8,128)(2,1)} %get-tuple-element.34.wlT, bf16[512,3072]{1,0:T(8,128)(2,1)} %get-tuple-element.35.wg, ...), custom_call_target="tpu_custom_call" | custom-call | tf_op jit(solution)/shard_map/reduce_grads/pallas_call | solution.py:1158
  365.5 3.4 slice_multiply_fusion
  368.9 0.6 div.45
  369.4 1.7 copy.30
  371.1 0.0 copy-start
  371.1 3.3 div.47
  374.4 0.0 copy-done
  374.4 3.0 fusion.1
  377.4 0.0 copy-start.2
  377.4 0.1 slice_multiply_fusion.1
  377.5 1.4 copy-done.2
  378.9 0.0 copy-start.1
  378.9 0.0 copy-start.3
  378.9 1.5 fusion.2
  380.3 0.8 copy-done.1
  381.2 0.3 copy-done.3
  381.5 0.0 copy-start.4
  381.5 1.7 fusion
  383.2 0.0 copy-done.4
  383.3 0.9 fusion.3
  384.2 0.7 slice.52
  384.9 0.7 dynamic_slice.7
  385.6 1.4 fusion.4
  387.0 1.4 dynamic-slice_bitcast_fusion
  388.3 1.3 constant_dynamic-slice_fusion
  389.7 1.2 slice.43
  391.6 1.2 slice_bitcast_fusion.1
  (2 shorter events, 0.0 us)
Async XLA Ops:
  371.1 3.3 copy-start
  377.4 1.5 copy-start.2
  378.9 2.3 copy-start.1
  378.9 2.6 copy-start.3
  381.5 1.8 copy-start.4

commit v2 on v1

--- a/solution.py
+++ b/solution.py
@@ -398,6 +398,7 @@
 f32 = jnp.float32
 MESH = pl.DeviceIdType.MESH
 VMEM_CAP = 60 * 1024 * 1024
+LAYER_CAP = 63 * 1024 * 1024
 ROWS = LONG_SLOTS * LONG_LEN + MID_SLOTS * MID_LEN + SHORT_SLOTS * SHORT_LEN
 BLOCK = 96
 CHUNK = 512
@@ -618,9 +619,10 @@
 
 def layer_kernel(
     seq, live, level, words, small, hid, teach, teach_scores,
-    out, input_grad, xlT, clT, wlT, nlT, act, wg, mlow, qg, sums,
-    wt, wm, ww, wn, prm, bias, wbias, qkv, low, ctx, hat1, rstd1, widened, acc, gacc, sgrad,
-    cgrad, valid, pair,
+    out, acc, fin, small_out,
+    wt, wm, ww, wn, prm, bias, wbias, qkv, low, ctx, hat1, rstd1, widened, act, wg, sgrad,
+    cgrad, valid, pair, xlT, clT, wlT, nlT, sums, tbuf, pt, rb, rx, ry, rz, sin,
+    s1, r1, s2, r2, s3, r3, s4, r4, s5, r5, s6, r6, sms, smr, tsem,
 ):
     c0, c1, c2, c3 = level[0], level[1], level[2], level[3]
     i0, i1, i2, i3 = 1.0 / c0, 1.0 / c1, 1.0 / c2, 1.0 / c3
@@ -761,15 +763,15 @@
         sums[8:9, :] += colsum(gap)
         grad = norm_rows_back(gap, hat, rstd, prm[6:7, :])
         sgrad[rs, :] = grad
+        acc[rs, :] = jnp.zeros((128, D), f32)
         lo = grad.astype(bf16)
         low[rs, :] = lo
         nlT[:, rs] = lo.T
         sums[4:5, :] += colsum(lo.astype(f32))
 
     loop(4, 128, norm_two)
-    gacc[...] = sgrad[...] * 0.0
-
-    def feed_back(t, carry):
+
+    def feed_back(t):
         cs = pl.ds(pl.multiple_of(t * 512, 512), 512)
         g = dot_nt(low[...], wn[cs, :])
         w = widened[:, cs]
@@ -784,17 +786,13 @@
         lo = back.astype(bf16)
         wg[:, cs] = lo
         wbias[1:2, cs] = colsum(lo.astype(f32))
-        gacc[...] += dot_nt(lo, ww[:, cs])
-        return carry
-
-    lax.fori_loop(0, 6, feed_back, 0)
-    for part in range(4):
-        sums[9 + part : 10 + part, :] = wbias[1:2, part * D : (part + 1) * D]
+        acc[...] += dot_nt(lo, ww[:, cs])
+
     def norm_one_back(r):
         rs = pl.ds(r, 128)
         hat = hat1[rs, :]
         normed = hat * prm[5:6, :] + prm[7:8, :]
-        grad, clip_sum = clip_back(gacc[rs, :], normed, c2, i2)
+        grad, clip_sum = clip_back(acc[rs, :], normed, c2, i2)
         sums[18:19, :] += clip_sum
         grad = grad + sgrad[rs, :]
         sums[5:6, :] += colsum(grad * hat)
@@ -802,21 +800,25 @@
         grad = norm_rows_back(grad, hat, rstd1[rs, 0:1], prm[5:6, :])
         acc[rs, :] = grad
         lo = grad.astype(bf16)
-        mlow[rs, :] = lo
+        low[rs, :] = lo
         sums[3:4, :] += colsum(lo.astype(f32))
-
-    loop(4, 128, norm_one_back)
 
     def mix_back(c):
         cs = pl.ds(c, 256)
-        g = dot_nt(mlow[...], wm[cs, :])
+        g = dot_nt(low[...], wm[cs, :])
         grad, clip_sum = clip_back(g, ctx[:, cs], c1, i1)
         sums[17:18, cs] += clip_sum
         cgrad[:, cs] = grad.astype(bf16)
 
-    loop(3, 256, mix_back)
-
-    def attend_pair_back(u, carry):
+    def scores_copy(u, slot):
+        g = lax.div(u, 6)
+        hp = lax.rem(u, 6)
+        rs = pl.ds(pl.multiple_of(g * 256, 256), 256)
+        return pltpu.make_async_copy(
+            teach_scores.at[pl.ds(2 * hp, 2), rs], tbuf.at[slot], tsem.at[slot]
+        )
+
+    def attend_pair_back(u, slot):
         g = lax.div(u, 6)
         hp = lax.rem(u, 6)
         rs = pl.ds(pl.multiple_of(g * 256, 256), 256)
@@ -832,7 +834,7 @@
         dq, dk, dv = [], [], []
         for j in range(2):
             s, p = softmax(q, k, ok, j)
-            ts = teach_scores[2 * hp + j, rs, :].astype(f32)
+            ts = tbuf[slot, j].astype(f32)
             second = pltpu.roll(ts[128:192], 128, 1)
             third = pltpu.roll(ts[192:256], 192, 1)
             moved = jnp.concatenate([ts[0:128], second, third], axis=0)
@@ -850,50 +852,285 @@
         dk = (jnp.where(first, dk[0], dk[1]) * scale).astype(bf16)
         dv = jnp.where(first, dv[0], dv[1]).astype(bf16)
         for index, (grad, at) in enumerate(((dq, q0), (dk, k0), (dv, v0))):
-            qg[rs, pl.ds(at, 128)] = grad
+            qkv[rs, pl.ds(at, 128)] = grad
             sums[index : index + 1, pl.ds(q0, 128)] += colsum(grad.astype(f32))
-        return carry
-
-    lax.fori_loop(0, 12, attend_pair_back, 0)
 
     def input_back(c):
         cs = pl.ds(c, 256)
-        g = dot_nt(qg[...], wt[cs, :])
+        g = dot_nt(qkv[...], wt[cs, :])
         grad, clip_sum = clip_back(g, hid[:, cs].astype(f32), c0, i0)
         sums[19:20, cs] += clip_sum
-        input_grad[:, cs] = grad + acc[:, cs]
-
-    loop(3, 256, input_back)
-    at = lax.broadcasted_iota(jnp.int32, (1, D), 1)
-    line = jnp.zeros((1, D), f32)
-    for spot, value in enumerate(
-        (sums[19:20, :], sums[17:18, :], sums[18:19, :], sums[14:15, :], sums[15:16, :] + sums[16:17, :])
-    ):
-        line = jnp.where(at == spot, jnp.sum(value), line)
-    sums[13:14, :] = line
+        acc[:, cs] += grad
+
+    def close_sums():
+        for part in range(4):
+            sums[9 + part : 10 + part, :] = wbias[1:2, part * D : (part + 1) * D]
+        at = lax.broadcasted_iota(jnp.int32, (1, D), 1)
+        line = jnp.zeros((1, D), f32)
+        for spot, value in enumerate(
+            (
+                sums[19:20, :], sums[17:18, :], sums[18:19, :], sums[14:15, :],
+                sums[15:16, :] + sums[16:17, :],
+            )
+        ):
+            line = jnp.where(at == spot, jnp.sum(value), line)
+        sums[13:14, :] = line
+        small_out[...] = sums[0:16, :]
+
+    dp = lax.axis_index("dp")
+    me = lax.axis_index("fsdp")
+    x = lax.rem(dp, 2)
+    y = lax.div(dp, 2)
+    z = lax.div(me, 2)
+    core = lax.rem(me, 2)
+    over_x = (dp + 1 - 2 * x, me)
+    over_y = (dp + 2 - 4 * y, me)
+    over_core = (dp, z * 2 + 1 - core)
+    firsts = (over_x, over_y)
+    seconds = (over_y, over_x)
+
+    def cols_of(p):
+        return pl.ds(p * 256, 256)
+
+    def remote(src, dst, send, recv, to):
+        return pltpu.make_async_remote_copy(
+            src_ref=src, dst_ref=dst, send_sem=send, recv_sem=recv, device_id=to,
+            device_id_type=MESH,
+        )
+
+    def core_copy(k):
+        slot = lax.rem(k, SLOTS)
+        return remote(pt.at[slot, :, 1 - core], rb.at[lax.rem(k, 2)], s1.at[slot], r1.at[slot], over_core)
+
+    def one_copy(k, p):
+        slot = lax.rem(k, SLOTS)
+        if p == 0:
+            src = pt.at[slot, :, core, 1 - x, :, :, cols_of(p)]
+        else:
+            src = pt.at[slot, :, core, :, 1 - y, :, cols_of(p)]
+        return remote(src, rx.at[lax.rem(k, 2), p], s2.at[slot, p], r2.at[slot, p], firsts[p])
+
+    def two_copy(k, p):
+        slot = lax.rem(k, SLOTS)
+        if p == 0:
+            src = pt.at[slot, :, core, x, 1 - y, :, cols_of(p)]
+        else:
+            src = pt.at[slot, :, core, 1 - x, y, :, cols_of(p)]
+        return remote(src, ry.at[lax.rem(k, 2), p], s3.at[slot, p], r3.at[slot, p], seconds[p])
+
+    def z_copy(k, hop):
+        slot = lax.rem(k, SLOTS)
+        to = lax.rem(z + hop, 4)
+        return remote(
+            pt.at[slot, to, core, x, y], rz.at[lax.rem(k, 2), hop - 1], s4.at[slot, hop - 1],
+            r4.at[slot, hop - 1], (dp, to * 2 + core),
+        )
+
+    def fin_cols(k, start, count):
+        return pl.ds(pl.multiple_of(lax.rem(k, 6) * CHUNK + start, count), count)
+
+    def back_two(k, p):
+        slot = lax.rem(k, SLOTS)
+        ref = fin.at[lax.div(k, 6), x, y, :, fin_cols(k, p * 256, 256)]
+        return remote(ref, ref, s5.at[slot, p], r5.at[slot, p], seconds[p])
+
+    def back_one(k, p):
+        slot = lax.rem(k, SLOTS)
+        if p == 0:
+            ref = fin.at[lax.div(k, 6), x, :, :, fin_cols(k, p * 256, 256)]
+        else:
+            ref = fin.at[lax.div(k, 6), :, y, :, fin_cols(k, p * 256, 256)]
+        return remote(ref, ref, s6.at[slot, p], r6.at[slot, p], firsts[p])
+
+    def small_copy(step):
+        to = (
+            over_core, over_x, over_y, (dp, lax.rem(z + 1, 4) * 2 + core),
+            (dp, lax.rem(z + 2, 4) * 2 + core), (dp, lax.rem(z + 3, 4) * 2 + core),
+        )[step]
+        return remote(small_out, sin.at[step], sms.at[step], smr.at[step], to)
+
+    def tick(t, carry):
+        @pl.when(t >= 6)
+        def _():
+            for p in range(2):
+                back_one(t - 6, p).wait()
+
+        @pl.when((t >= 5) & (t < 5 + CHUNKS))
+        def _():
+            for p in range(2):
+                back_two(t - 5, p).wait()
+                back_one(t - 5, p).start()
+
+        @pl.when((t >= 4) & (t < 4 + CHUNKS))
+        def _():
+            k = t - 4
+            slot = lax.rem(k, SLOTS)
+            for hop in (1, 2, 3):
+                z_copy(k, hop).wait()
+            duo = lax.rem(k, 2)
+            total = pt[slot, z, core, x, y] + rz[duo, 0] + rz[duo, 1] + rz[duo, 2]
+            fin[lax.div(k, 6), x, y, :, fin_cols(k, 0, CHUNK)] = total
+            for p in range(2):
+                back_two(k, p).start()
+
+        @pl.when((t >= 3) & (t < 3 + CHUNKS))
+        def _():
+            k = t - 3
+            slot = lax.rem(k, SLOTS)
+            for p in range(2):
+                two_copy(k, p).wait()
+                for q in range(4):
+                    pt[slot, q, core, x, y, :, cols_of(p)] += ry[lax.rem(k, 2), p, q]
+            for hop in (1, 2, 3):
+                z_copy(k, hop).start()
+
+        @pl.when((t >= 2) & (t < 2 + CHUNKS))
+        def _():
+            k = t - 2
+            slot = lax.rem(k, SLOTS)
+            for p in range(2):
+                one_copy(k, p).wait()
+                for q in range(4):
+                    for i in range(2):
+                        if p == 0:
+                            pt[slot, q, core, x, i, :, cols_of(p)] += rx[lax.rem(k, 2), p, q, i]
+                        else:
+                            pt[slot, q, core, i, y, :, cols_of(p)] += rx[lax.rem(k, 2), p, q, i]
+                two_copy(k, p).start()
+
+        @pl.when((t >= 1) & (t < 1 + CHUNKS))
+        def _():
+            k = t - 1
+            slot = lax.rem(k, SLOTS)
+            core_copy(k).wait()
+            for q in range(4):
+                pt[slot, q, core] += rb[lax.rem(k, 2), q]
+            for p in range(2):
+                one_copy(k, p).start()
+
+        slot = lax.rem(t, SLOTS)
+
+        def put(owner, cols, block):
+            for i in range(2):
+                for j in range(2):
+                    at = (i * 2 + j) * 24
+                    pt[slot, owner // 2, owner % 2, i, j, :, cols] = block[at : at + 24, :]
+
+        @pl.when(t < 6)
+        def _():
+            j = lax.div(t, 2)
+            rows = pl.ds(pl.multiple_of(lax.rem(t, 2) * 384, 384), 384)
+            left = nlT[rows, :]
+            for owner in range(8):
+                cols = pl.ds(pl.multiple_of(owner * 384 + j * 128, 128), 128)
+                got = dot_nn(left, act[:, cols])
+                for part in range(4):
+                    put(owner, pl.ds(part * 128, 128), got[part * BLOCK : (part + 1) * BLOCK, :])
+
+        def whole(left, right, half):
+            got = dot_nn(left, right)
+            for owner in range(8):
+                put(owner, pl.ds(half * 256, 256), got[owner * BLOCK : (owner + 1) * BLOCK, :])
+
+        @pl.when((t >= 6) & (t < 12))
+        def _():
+            for half in range(2):
+                cols = pl.ds(pl.multiple_of((t - 6) * CHUNK + half * 256, 256), 256)
+                whole(wlT[...], wg[:, cols], half)
+
+        for half in range(2):
+            part = (t - 12) * 2 + half
+
+            @pl.when((part >= 0) & (part < 3))
+            def _():
+                cols = pl.ds(pl.multiple_of(part * 256, 256), 256)
+                whole(clT[...], low[:, cols], half)
+
+            @pl.when((part >= 3) & (part < 12))
+            def _():
+                cols = pl.ds(pl.multiple_of((part - 3) * 256, 256), 256)
+                whole(xlT[...], qkv[:, cols], half)
+
+        @pl.when(t < CHUNKS)
+        def _():
+            core_copy(t).start()
+
+        @pl.when(t < 6)
+        def _():
+            feed_back(t)
+
+        @pl.when(t == 6)
+        def _():
+            for slot in range(2):
+                scores_copy(slot, slot).start()
+            loop(4, 128, norm_one_back)
+            loop(3, 256, mix_back)
+
+        @pl.when((t >= 7) & (t < 13))
+        def _():
+            for slot in range(2):
+                u = (t - 7) * 2 + slot
+                scores_copy(u, slot).wait()
+                attend_pair_back(u, slot)
+
+                @pl.when(t < 12)
+                def _():
+                    scores_copy(u + 2, slot).start()
+
+        @pl.when((t >= 13) & (t < 16))
+        def _():
+            input_back(pl.multiple_of((t - 13) * 256, 256))
+
+        @pl.when(t == 16)
+        def _():
+            close_sums()
+            small_copy(0).start()
+
+        @pl.when(t == 17)
+        def _():
+            small_copy(0).wait()
+            small_out[...] += sin[0]
+            small_copy(1).start()
+
+        @pl.when(t == 18)
+        def _():
+            small_copy(1).wait()
+            small_out[...] += sin[1]
+            small_copy(2).start()
+
+        @pl.when(t == 19)
+        def _():
+            small_copy(2).wait()
+            small_out[...] += sin[2]
+            for step in (3, 4, 5):
+                small_copy(step).start()
+
+        @pl.when(t == 20)
+        def _():
+            for step in (3, 4, 5):
+                small_copy(step).wait()
+            small_out[...] = small_out[...] + sin[3] + sin[4] + sin[5]
+
+        return carry
+
+    lax.fori_loop(0, CHUNKS + 6, tick, 0)
 
 
 def layer(seq, live, level, words, small, hid, teach, teach_scores):
     vm = pl.BlockSpec(memory_space=pltpu.VMEM)
     sm = pl.BlockSpec(memory_space=pltpu.SMEM)
     sds = jax.ShapeDtypeStruct
+    dma = pltpu.SemaphoreType.DMA
     return pl.pallas_call(
         layer_kernel,
         out_shape=(
             sds((ROWS, D), bf16),
             sds((ROWS, D), f32),
-            sds((D, ROWS), bf16),
-            sds((D, ROWS), bf16),
-            sds((D, ROWS), bf16),
-            sds((D, ROWS), bf16),
-            sds((ROWS, FF), bf16),
-            sds((ROWS, FF), bf16),
-            sds((ROWS, D), bf16),
-            sds((ROWS, 3 * D), bf16),
-            sds((24, D), f32),
+            sds((3, 2, 2, 24, FF), f32),
+            sds((16, D), f32),
         ),
-        in_specs=[sm] * 3 + [vm] * 5,
-        out_specs=(vm,) * 11,
+        in_specs=[sm] * 3 + [vm] * 4 + [pl.BlockSpec(memory_space=pl.ANY)],
+        out_specs=(vm,) * 4,
         scratch_shapes=[
             pltpu.VMEM((D, 3 * D), bf16),
             pltpu.VMEM((D, D), bf16),
@@ -908,273 +1145,34 @@
             pltpu.VMEM((ROWS, D), f32),
             pltpu.VMEM((ROWS, 128), f32),
             pltpu.VMEM((ROWS, FF), f32),
-            pltpu.VMEM((ROWS, D), f32),
-            pltpu.VMEM((ROWS, D), f32),
+            pltpu.VMEM((ROWS, FF), bf16),
+            pltpu.VMEM((ROWS, FF), bf16),
             pltpu.VMEM((ROWS, D), f32),
             pltpu.VMEM((ROWS, D), bf16),
             pltpu.VMEM((2, 256, 256), f32),
             pltpu.VMEM((2, 256, 256), f32),
-        ],
-        compiler_params=pltpu.CompilerParams(vmem_limit_bytes=VMEM_CAP),
+            pltpu.VMEM((D, ROWS), bf16),
+            pltpu.VMEM((D, ROWS), bf16),
+            pltpu.VMEM((D, ROWS), bf16),
+            pltpu.VMEM((D, ROWS), bf16),
+            pltpu.VMEM((24, D), f32),
+            pltpu.VMEM((2, 2, 256, 256), bf16),
+            pltpu.VMEM((SLOTS, 4, 2, 2, 2, 24, CHUNK), f32),
+            pltpu.VMEM((2, 4, 2, 2, 24, CHUNK), f32),
+            pltpu.VMEM((2, 2, 4, 2, 24, 256), f32),
+            pltpu.VMEM((2, 2, 4, 24, 256), f32),
+            pltpu.VMEM((2, 3, 24, CHUNK), f32),
+            pltpu.VMEM((6, 16, D), f32),
+        ]
+        + [dma((SLOTS,))] * 2
+        + [dma((SLOTS, 2))] * 4
+        + [dma((SLOTS, 3))] * 2
+        + [dma((SLOTS, 2))] * 4
+        + [dma((6,))] * 2
+        + [dma((2,))],
+        compiler_params=pltpu.CompilerParams(has_side_effects=True, vmem_limit_bytes=LAYER_CAP),
         name="layer",
     )(seq, live, level, words, small, hid, teach, teach_scores)
-
-
-def reduce_kernel(
-    nlT, act, wlT, wg, clT, ml, xlT, qg, sums,
-    fin, small_out,
-    pt, rb, rx, ry, rz, sin,
-    s1, r1, s2, r2, s3, r3, s4, r4, s5, r5, s6, r6, sms, smr,
-):
-    dp = lax.axis_index("dp")
-    me = lax.axis_index("fsdp")
-    x = lax.rem(dp, 2)
-    y = lax.div(dp, 2)
-    z = lax.div(me, 2)
-    core = lax.rem(me, 2)
-    flip_x = dp + 1 - 2 * x
-    flip_y = dp + 2 - 4 * y
-
-    def turns(k):
-        odd = lax.rem(k, 2)
-        one = flip_x * (1 - odd) + flip_y * odd
-        two = flip_y * (1 - odd) + flip_x * odd
-        a = x * (1 - odd) + y * odd
-        b = y * (1 - odd) + x * odd
-        return one, two, a, b
-
-    def rows_at(start, count):
-        return pl.ds(pl.multiple_of(start, 8), count)
-
-    def core_copy(k):
-        slot = lax.rem(k, SLOTS)
-        return pltpu.make_async_remote_copy(
-            src_ref=pt.at[slot, :, 1 - core], dst_ref=rb.at[slot], send_sem=s1.at[slot],
-            recv_sem=r1.at[slot], device_id=(dp, z * 2 + 1 - core), device_id_type=MESH,
-        )
-
-    def one_copy(k):
-        slot = lax.rem(k, SLOTS)
-        one, two, a, b = turns(k)
-        return pltpu.make_async_remote_copy(
-            src_ref=pt.at[slot, :, core, rows_at((1 - a) * 48, 48)], dst_ref=rx.at[slot],
-            send_sem=s2.at[slot], recv_sem=r2.at[slot], device_id=(one, me), device_id_type=MESH,
-        )
-
-    def two_copy(k):
-        slot = lax.rem(k, SLOTS)
-        one, two, a, b = turns(k)
-        return pltpu.make_async_remote_copy(
-            src_ref=pt.at[slot, :, core, rows_at(a * 48 + (1 - b) * 24, 24)], dst_ref=ry.at[slot],
-            send_sem=s3.at[slot], recv_sem=r3.at[slot], device_id=(two, me), device_id_type=MESH,
-        )
-
-    def z_copy(k, hop):
-        slot = lax.rem(k, SLOTS)
-        one, two, a, b = turns(k)
-        to = lax.rem(z + hop, 4)
-        return pltpu.make_async_remote_copy(
-            src_ref=pt.at[slot, to, core, rows_at(a * 48 + b * 24, 24)],
-            dst_ref=rz.at[slot, hop - 1], send_sem=s4.at[slot, hop - 1],
-            recv_sem=r4.at[slot, hop - 1], device_id=(dp, to * 2 + core), device_id_type=MESH,
-        )
-
-    def fin_rows(k, start, count):
-        section = lax.div(k, 6)
-        return fin.at[
-            section, rows_at(start, count),
-            pl.ds(pl.multiple_of(lax.rem(k, 6) * CHUNK, CHUNK), CHUNK),
-        ]
-
-    def back_two(k):
-        slot = lax.rem(k, SLOTS)
-        one, two, a, b = turns(k)
-        ref = fin_rows(k, a * 48 + b * 24, 24)
-        return pltpu.make_async_remote_copy(
-            src_ref=ref, dst_ref=ref, send_sem=s5.at[slot], recv_sem=r5.at[slot],
-            device_id=(two, me), device_id_type=MESH,
-        )
-
-    def back_one(k):
-        slot = lax.rem(k, SLOTS)
-        one, two, a, b = turns(k)
-        ref = fin_rows(k, a * 48, 48)
-        return pltpu.make_async_remote_copy(
-            src_ref=ref, dst_ref=ref, send_sem=s6.at[slot], recv_sem=r6.at[slot],
-            device_id=(one, me), device_id_type=MESH,
-        )
-
-    def small_copy(step):
-        to = (
-            (dp, z * 2 + 1 - core), (flip_x, me), (flip_y, me),
-            (dp, lax.rem(z + 1, 4) * 2 + core), (dp, lax.rem(z + 2, 4) * 2 + core),
-            (dp, lax.rem(z + 3, 4) * 2 + core),
-        )[step]
-        return pltpu.make_async_remote_copy(
-            src_ref=small_out, dst_ref=sin.at[step], send_sem=sms.at[step],
-            recv_sem=smr.at[step], device_id=to, device_id_type=MESH,
-        )
-
-    small_out[...] = sums[0:16, :]
-
-    def tick(t, carry):
-        @pl.when(t >= 6)
-        def _():
-            back_one(t - 6).wait()
-
-        @pl.when((t >= 5) & (t < 5 + CHUNKS))
-        def _():
-            back_two(t - 5).wait()
-            back_one(t - 5).start()
-
-        @pl.when((t >= 4) & (t < 4 + CHUNKS))
-        def _():
-            k = t - 4
-            slot = lax.rem(k, SLOTS)
-            one, two, a, b = turns(k)
-            for hop in (1, 2, 3):
-                z_copy(k, hop).wait()
-            total = pt[slot, z, core, rows_at(a * 48 + b * 24, 24), :]
-            total = total + rz[slot, 0] + rz[slot, 1] + rz[slot, 2]
-            fin[
-                lax.div(k, 6), rows_at(a * 48 + b * 24, 24),
-                pl.ds(pl.multiple_of(lax.rem(k, 6) * CHUNK, CHUNK), CHUNK),
-            ] = total
-            back_two(k).start()
-
-        @pl.when((t >= 3) & (t < 3 + CHUNKS))
-        def _():
-            k = t - 3
-            slot = lax.rem(k, SLOTS)
-            one, two, a, b = turns(k)
-            two_copy(k).wait()
-            for q in range(4):
-                pt[slot, q, core, rows_at(a * 48 + b * 24, 24), :] += ry[slot, q]
-            for hop in (1, 2, 3):
-                z_copy(k, hop).start()
-
-        @pl.when((t >= 2) & (t < 2 + CHUNKS))
-        def _():
-            k = t - 2
-            slot = lax.rem(k, SLOTS)
-            one, two, a, b = turns(k)
-            one_copy(k).wait()
-            for q in range(4):
-                pt[slot, q, core, rows_at(a * 48, 48), :] += rx[slot, q]
-            two_copy(k).start()
-
-        @pl.when((t >= 1) & (t < 1 + CHUNKS))
-        def _():
-            k = t - 1
-            slot = lax.rem(k, SLOTS)
-            core_copy(k).wait()
-            for q in range(4):
-                pt[slot, q, core] += rb[slot, q]
-            one_copy(k).start()
-
-        slot = lax.rem(t, SLOTS)
-
-        @pl.when(t < 6)
-        def _():
-            j = lax.div(t, 2)
-            rows = pl.ds(pl.multiple_of(lax.rem(t, 2) * 384, 384), 384)
-            left = nlT[rows, :]
-            for owner in range(8):
-                cols = pl.ds(pl.multiple_of(owner * 384 + j * 128, 128), 128)
-                got = dot_nn(left, act[:, cols])
-                for part in range(4):
-                    pt[slot, owner // 2, owner % 2, :, part * 128 : (part + 1) * 128] = got[
-                        part * BLOCK : (part + 1) * BLOCK, :
-                    ]
-
-        def whole(left, right, half):
-            got = dot_nn(left, right)
-            for owner in range(8):
-                pt[slot, owner // 2, owner % 2, :, half * 256 : (half + 1) * 256] = got[
-                    owner * BLOCK : (owner + 1) * BLOCK, :
-                ]
-
-        @pl.when((t >= 6) & (t < 12))
-        def _():
-            for half in range(2):
-                cols = pl.ds(pl.multiple_of((t - 6) * CHUNK + half * 256, 256), 256)
-                whole(wlT[...], wg[:, cols], half)
-
-        for half in range(2):
-            part = (t - 12) * 2 + half
-
-            @pl.when((part >= 0) & (part < 3))
-            def _():
-                cols = pl.ds(pl.multiple_of(part * 256, 256), 256)
-                whole(clT[...], ml[:, cols], half)
-
-            @pl.when((part >= 3) & (part < 12))
-            def _():
-                cols = pl.ds(pl.multiple_of((part - 3) * 256, 256), 256)
-                whole(xlT[...], qg[:, cols], half)
-
-        @pl.when(t < CHUNKS)
-        def _():
-            core_copy(t).start()
-
-        @pl.when(t == 8)
-        def _():
-            small_copy(0).start()
-
-        @pl.when(t == 10)
-        def _():
-            small_copy(0).wait()
-            small_out[...] += sin[0]
-            small_copy(1).start()
-
-        @pl.when(t == 12)
-        def _():
-            small_copy(1).wait()
-            small_out[...] += sin[1]
-            small_copy(2).start()
-
-        @pl.when(t == 14)
-        def _():
-            small_copy(2).wait()
-            small_out[...] += sin[2]
-            for step in (3, 4, 5):
-                small_copy(step).start()
-
-        @pl.when(t == 16)
-        def _():
-            for step in (3, 4, 5):
-                small_copy(step).wait()
-            small_out[...] = small_out[...] + sin[3] + sin[4] + sin[5]
-
-        return carry
-
-    lax.fori_loop(0, CHUNKS + 6, tick, 0)
-
-
-def reduce_grads(nlT, act, wlT, wg, clT, ml, xlT, qg, sums):
-    vm = pl.BlockSpec(memory_space=pltpu.VMEM)
-    sds = jax.ShapeDtypeStruct
-    dma = pltpu.SemaphoreType.DMA
-    return pl.pallas_call(
-        reduce_kernel,
-        out_shape=(sds((3, BLOCK, FF), f32), sds((16, D), f32)),
-        in_specs=[vm] * 9,
-        out_specs=(vm, vm),
-        scratch_shapes=[
-            pltpu.VMEM((SLOTS, 4, 2, BLOCK, CHUNK), f32),
-            pltpu.VMEM((SLOTS, 4, BLOCK, CHUNK), f32),
-            pltpu.VMEM((SLOTS, 4, 48, CHUNK), f32),
-            pltpu.VMEM((SLOTS, 4, 24, CHUNK), f32),
-            pltpu.VMEM((SLOTS, 3, 24, CHUNK), f32),
-            pltpu.VMEM((6, 16, D), f32),
-        ]
-        + [dma((SLOTS,))] * 6
-        + [dma((SLOTS, 3))] * 2
-        + [dma((SLOTS,))] * 4
-        + [dma((6,))] * 2,
-        compiler_params=pltpu.CompilerParams(has_side_effects=True, vmem_limit_bytes=VMEM_CAP),
-        name="reduce_grads",
-    )(nlT, act, wlT, wg, clT, ml, xlT, qg, sums)
 
 
 def on_device_fast(
@@ -1187,10 +1185,10 @@
         mixing_bias[None], widen_bias[None], narrow_bias[None], norm_gain, norm_shift,
     )
     teach_scores = jnp.transpose(teacher_scores, (1, 0, 2))
-    out, input_grad, xlT, clT, wlT, nlT, act, wg, ml, qg, sums = layer(
+    out, input_grad, fin, small_sum = layer(
         seq_lengths, live_counts, clip_level, words, small, hidden_in, teacher_hidden, teach_scores
     )
-    fin, small_sum = reduce_grads(nlT, act, wlT, wg, clT, ml, xlT, qg, sums)
+    fin = fin.reshape(3, BLOCK, FF)
     narrow_sum = (
         fin[0].reshape(BLOCK, 3, 2, 4, 128).transpose(1, 4, 2, 3, 0).reshape(4 * BLOCK, D)
     )

time: 394 us -> 295 us (0.75)
  Pallas kernels: 364 us -> 262 us
    pallas_call x1 -> x0, Pallas kernels: 239 us -> none  [reduce_grads(): pl.pallas_call(reduce_kernel, out_shape=(sds((3, BLOCK, FF), f32), sds((1...]
    pallas_call x1, Pallas kernels: 82 us -> 219 us  [layer(): pl.pallas_call(layer_kernel, out_shape=(sds((ROWS, D), bf16), sds((ROWS,...]
where the time goes in v2:
time: 295 us
  Pallas kernels  262 us (89%)
  local copies, waits for them, and re-layouts  18.5 us (6%)
  other arithmetic  11.5 us (4%)
    pallas_call x1, Pallas kernels, layer(): pl.pallas_call(layer_kernel, out_shape=(sds((ROWS, D), bf16), sds((ROWS,...  219 us
    pallas_call x1, Pallas kernels, gather(): pl.pallas_call(gather_kernel, out_shape=(jax.ShapeDtypeStruct((8, 72, D),...  42.8 us
    select_n x4, other arithmetic, on_device_fast(): jnp.where(jnp.abs(latent) <= 1.0, (total / math.sqrt(fan_in))[None], 0.0)  7.15 us

profile of v2, /device:TPU:0, one launch (start us, length us, event | category | flops | bytes accessed | tf_op | source)
XLA Modules:
  0.0 294.6 jit_solution(8018599668952124397)
XLA Ops:
  0.6 1.2 broadcast_in_dim.62.wb
  1.9 42.8 %gather_weights.1 = (s32[8,72,768]{2,1,0:T(8,128)}, f32[8,192,128]{2,1,0:T(8,128)}) custom-call(f32[2,96,2304]{2,1,0:T(8,128)} %triple.1, f32[2,96,768]{2,1,0:T(8,128)} %mixing.1, f32[2,96,3072]{2,1,0:T(8,128)} %widen.1, f32[2,384,768]{2,1,0:T(8,128)} %narrow.1, f32[3,96]{1,0:T(4,128)} %tb.1, f32[1,96]{1,0:T(1,128)} %bitcast.24, ...), custom_call_target="tpu_custom_call" | custom-call | tf_op jit(solution)/shard_map/gather_weights/pallas_call | solution.py:540
  44.7 219.3 %layer.1 = (bf16[512,768]{1,0:T(8,128)(2,1)}, f32[512,768]{1,0:T(8,128)}, f32[3,2,2,24,3072]{4,3,2,1,0:T(8,128)}, f32[16,768]{1,0:T(8,128)}) custom-call(s32[1,4]{1,0:T(1,128)} %seq.1, s32[1,3]{1,0:T(1,128)} %live.1, f32[4]{0:T(128)} %level.1, s32[8,72,768]{2,1,0:T(8,128)} %get-tuple-element.20.words, f32[8,192,128]{2,1,0:T(8,128)} %get-tuple-element.21.small, ...), custom_call_target="tpu_custom_call" | custom-call | tf_op jit(solution)/shard_map/layer/pallas_call | solution.py:1124
  264.0 1.3 slice.46
  265.9 1.4 dynamic-slice_bitcast_fusion
  267.2 1.2 slice_bitcast_fusion
  268.4 1.4 fusion.4
  269.8 1.3 constant_dynamic-slice_fusion
  271.2 0.7 slice.55
  271.9 0.7 dynamic_slice.7
  272.6 3.4 %slice_multiply_fusion = (f32[1,2,2,24,3072]{4,3,2,1,0:T(8,128)S(1)}, f32[1,2,2,24,3072]{4,3,2,1,0:T(8,128)}, f32[1,2,2,24,3072]{4,3,2,1,0:T(8,128)S(1)}) fusion(f32[3,2,2,24,3072]{4,3,2,1,0:T(8,128)} %get-tuple-element.25), kind=kLoop, calls=%fused_computation.6 | loop fusion | flops 589824 | bytes 7077888 | tf_op jit(solution)/shard_map/div | solution.py:1199
  275.9 1.5 div.48
  277.5 0.0 copy-start.6
  277.5 1.0 slice_multiply_fusion.2
  278.5 0.2 copy-done.6
  278.7 0.0 copy-start.4
  278.7 0.9 fusion.3
  279.6 0.6 copy-done.4
  280.2 0.9 copy.30
  281.1 0.0 copy-start.2
  281.1 2.1 div.50
  283.2 0.0 copy-done.2
  283.2 0.0 copy-start
  283.2 0.0 copy-start.5
  283.2 2.8 fusion.2
  286.0 0.0 copy-done
  286.0 0.0 copy-done.5
  286.0 0.0 copy-start.1
  286.0 0.0 copy-start.3
  286.0 1.7 fusion.1
  287.8 0.8 copy-done.1
  288.5 0.3 copy-done.3
  288.9 0.0 copy-start.8
  288.9 1.7 fusion
  290.6 0.0 copy-done.8
  290.6 0.0 copy-start.7
  290.6 0.9 copy.33
  291.5 0.8 copy-done.7
  292.3 1.1 copy.34
  (2 shorter events, 0.0 us)
Async XLA Ops:
  277.5 1.2 copy-start.6
  278.7 1.5 copy-start.4
  281.1 2.2 copy-start.2
  283.2 2.8 copy-start
  283.2 2.8 copy-start.5
  286.0 2.5 copy-start.1
  286.0 2.8 copy-start.3
  288.9 1.7 copy-start.8
  290.6 1.7 copy-start.7

commit v3 on v2

--- a/solution.py
+++ b/solution.py
@@ -402,7 +402,9 @@
 ROWS = LONG_SLOTS * LONG_LEN + MID_SLOTS * MID_LEN + SHORT_SLOTS * SHORT_LEN
 BLOCK = 96
 CHUNK = 512
-CHUNKS = 18
+HALF = CHUNK // 2
+SECTION = FF // CHUNK
+CHUNKS = 3 * SECTION
 SLOTS = 4
 
 
@@ -426,134 +428,13 @@
     lax.fori_loop(0, count, run, 0)
 
 
-def latent_piece(refs, block, half, group):
-    triple, mixing, widen, narrow = refs
-    rows = pl.ds(group * 8, 8)
-    if block < 3:
-        return triple[half, rows, block * D : (block + 1) * D]
-    if block == 3:
-        return mixing[half, rows, :]
-    if block < 8:
-        return widen[half, rows, (block - 4) * D : (block - 3) * D]
-    return narrow[half, pl.ds((block - 8) * BLOCK + group * 8, 8), :]
-
-
 def plane_of(block, half, group):
     place = block * 24 + half * 12 + group
     bit = place % 32
     return place // 32, (1 << bit) if bit < 31 else -(1 << 31)
 
 
-def gather_kernel(
-    triple, mixing, widen, narrow, tb, mb, wb, nb, gain, shift,
-    words, small, spread, wsend, wrecv, ssend, srecv, cwsend, cwrecv, cssend, csrecv,
-):
-    dp = lax.axis_index("dp")
-    me = lax.axis_index("fsdp")
-    z = lax.div(me, 2)
-    core = lax.rem(me, 2)
-    refs = (triple, mixing, widen, narrow)
-    masks = [[] for _ in range(9)]
-    for block in range(12):
-        for half in range(2):
-            for group in range(12):
-                word, bit = plane_of(block, half, group)
-                masks[word].append((block, half, group, bit))
-    for word in range(9):
-        total = jnp.zeros((8, D), jnp.int32)
-        for block, half, group, bit in masks[word]:
-            piece = latent_piece(refs, block, half, group)
-            total = total | jnp.where(piece > 0, jnp.int32(bit), jnp.int32(0))
-        words[me, word * 8 : (word + 1) * 8, :] = total
-    lane = lax.broadcasted_iota(jnp.int32, (8, 128), 1)
-
-    def scale_rows(group, carry):
-        tile = jnp.zeros((8, 128), f32)
-        rows = pl.ds(pl.multiple_of(group * 8, 8), 8)
-        for half in range(2):
-            for index in range(7):
-                if index == 0:
-                    part = triple[half, rows, :]
-                elif index == 1:
-                    part = mixing[half, rows, :]
-                elif index == 2:
-                    part = widen[half, rows, :]
-                else:
-                    part = narrow[
-                        half, pl.ds(pl.multiple_of((index - 3) * BLOCK + group * 8, 8), 8), :
-                    ]
-                fan = FF if index >= 3 else D
-                mean = jnp.sum(jnp.abs(part), axis=1, keepdims=True) * (1.0 / part.shape[1])
-                tile = jnp.where(lane == index * 2 + half, mean / math.sqrt(fan), tile)
-        small[me, rows, :] = tile
-        return carry
-
-    lax.fori_loop(0, 12, scale_rows, 0)
-    spread[...] = jnp.zeros_like(spread)
-    spread[0:3, 0:BLOCK] = tb[...]
-    spread[3:4, 0:BLOCK] = mb[...]
-    spread[4:5, 0:BLOCK] = nb[...]
-    spread[5:7, 0:BLOCK] = gain[...]
-    spread[7:9, 0:BLOCK] = shift[...]
-    spread[16:17, 0 : 4 * BLOCK] = wb[...]
-    placed = pltpu.roll(spread[0:16, :], me * BLOCK, 1)
-    wide = pltpu.roll(spread[16:24, :], core * (4 * BLOCK), 1)
-    row = lax.broadcasted_iota(jnp.int32, (16, D), 0)
-    wide_rows = jnp.broadcast_to(wide[0:1, :], (16, D))
-    placed = placed + jnp.where(row == 9 + z, wide_rows, 0.0)
-    for part in range(6):
-        small[me, 96 + part * 16 : 112 + part * 16, :] = placed[:, part * 128 : (part + 1) * 128]
-
-    def over_z(hop, ref, send, recv):
-        peer = lax.rem(z + hop, 4) * 2 + core
-        return pltpu.make_async_remote_copy(
-            src_ref=ref.at[me], dst_ref=ref.at[me], send_sem=send.at[hop - 1],
-            recv_sem=recv.at[hop - 1], device_id=(dp, peer), device_id_type=MESH,
-        )
-
-    def over_core(hop, ref, send, recv):
-        owner = lax.rem(z + 4 - hop, 4) * 2 + core
-        return pltpu.make_async_remote_copy(
-            src_ref=ref.at[owner], dst_ref=ref.at[owner], send_sem=send.at[hop],
-            recv_sem=recv.at[hop], device_id=(dp, z * 2 + 1 - core), device_id_type=MESH,
-        )
-
-    for hop in (1, 2, 3):
-        over_z(hop, small, ssend, srecv).start()
-    for hop in (1, 2, 3):
-        over_z(hop, words, wsend, wrecv).start()
-    over_core(0, small, cssend, csrecv).start()
-    over_core(0, words, cwsend, cwrecv).start()
-    for hop in (1, 2, 3):
-        over_z(hop, small, ssend, srecv).wait()
-        over_core(hop, small, cssend, csrecv).start()
-    for hop in (1, 2, 3):
-        over_z(hop, words, wsend, wrecv).wait()
-        over_core(hop, words, cwsend, cwrecv).start()
-    for hop in range(4):
-        over_core(hop, small, cssend, csrecv).wait()
-        over_core(hop, words, cwsend, cwrecv).wait()
-
-
-def gather(triple, mixing, widen, narrow, tb, mb, wb, nb, gain, shift):
-    vm = pl.BlockSpec(memory_space=pltpu.VMEM)
-    return pl.pallas_call(
-        gather_kernel,
-        out_shape=(
-            jax.ShapeDtypeStruct((8, 72, D), jnp.int32),
-            jax.ShapeDtypeStruct((8, 192, 128), f32),
-        ),
-        in_specs=[vm] * 10,
-        out_specs=(vm, vm),
-        scratch_shapes=[pltpu.VMEM((24, D), f32)]
-        + [pltpu.SemaphoreType.DMA((3,))] * 4
-        + [pltpu.SemaphoreType.DMA((4,))] * 4,
-        compiler_params=pltpu.CompilerParams(has_side_effects=True, vmem_limit_bytes=VMEM_CAP),
-        name="gather_weights",
-    )(triple, mixing, widen, narrow, tb, mb, wb, nb, gain, shift)
-
-
-def unpack_block(words, small, block, dst):
+def unpack_block(words, scl, block, dst):
     index = 0 if block < 3 else 1 if block == 3 else 2 if block < 8 else block - 5
 
     def one(owner, carry):
@@ -566,7 +447,7 @@
                     bits = words[owner, word * 8 : (word + 1) * 8, :] & jnp.int32(bit)
                     column = index * 2 + half
                     scale = jnp.broadcast_to(
-                        small[owner, group * 8 : (group + 1) * 8, column : column + 1], (8, D)
+                        scl[owner, group * 8 : (group + 1) * 8, column : column + 1], (8, D)
                     )
                     value = jnp.where(bits != 0, scale, -scale)
                     total = value if total is None else total + value
@@ -618,23 +499,152 @@
 
 
 def layer_kernel(
-    seq, live, level, words, small, hid, teach, teach_scores,
+    seq, live, level, tb, mb, wb, nb, gain, shift, hid, teach, teach_scores, tl, ml, wl, nl,
     out, acc, fin, small_out,
+    words, small, scl, spread,
     wt, wm, ww, wn, prm, bias, wbias, qkv, low, ctx, hat1, rstd1, widened, act, wg, sgrad,
-    cgrad, valid, pair, xlT, clT, wlT, nlT, sums, tbuf, pt, rb, rx, ry, rz, sin,
-    s1, r1, s2, r2, s3, r3, s4, r4, s5, r5, s6, r6, sms, smr, tsem,
+    cgrad, valid, pair, xlT, clT, wlT, nlT, sums, tbuf, pt, rb, rx, rz, rf, held, ry, sin,
+    s1, r1, s2, r2, s3, r3, s4, r4, s5, r5, s6, r6, s7, r7, sms, smr, tsem, lsem, zs, zr, cs_, cr_,
 ):
+    dp = lax.axis_index("dp")
+    me = lax.axis_index("fsdp")
+    x = lax.rem(dp, 2)
+    y = lax.div(dp, 2)
+    z = lax.div(me, 2)
+    core = lax.rem(me, 2)
+    over_x = (dp + 1 - 2 * x, me)
+    over_y = (dp + 2 - 4 * y, me)
+    over_core = (dp, z * 2 + 1 - core)
+
+    def remote(src, dst, send, recv, to):
+        return pltpu.make_async_remote_copy(
+            src_ref=src, dst_ref=dst, send_sem=send, recv_sem=recv, device_id=to,
+            device_id_type=MESH,
+        )
+
+    greet = pltpu.get_barrier_semaphore()
+    for to in (over_core, over_x, over_y) + tuple(
+        (dp, lax.rem(z + hop, 4) * 2 + core) for hop in (1, 2, 3)
+    ):
+        pl.semaphore_signal(greet, inc=1, device_id=to, device_id_type=MESH)
+
+    loads = []
+    for half in range(2):
+        band = slice(192 + half * BLOCK, 192 + (half + 1) * BLOCK)
+        loads.append([
+            pltpu.make_async_copy(tl.at[half], widened.at[band, 0 : 3 * D], lsem.at[half, 0]),
+            pltpu.make_async_copy(ml.at[half], widened.at[band, 3 * D : FF], lsem.at[half, 1]),
+            pltpu.make_async_copy(
+                wl.at[half], widened.at[half * BLOCK : (half + 1) * BLOCK, :], lsem.at[half, 2]
+            ),
+            pltpu.make_async_copy(
+                nl.at[half], (ctx if half == 0 else sgrad).at[0 : 4 * BLOCK, :], lsem.at[half, 3]
+            ),
+        ])
+    for index in range(4):
+        for half in range(2):
+            loads[half][index].start()
+
+    def latent_piece(block, half, group):
+        if block < 4:
+            rows = pl.ds(192 + half * BLOCK + group * 8, 8)
+            return widened[rows, block * D : (block + 1) * D]
+        if block < 8:
+            return widened[pl.ds(half * BLOCK + group * 8, 8), (block - 4) * D : (block - 3) * D]
+        rows = pl.ds((block - 8) * BLOCK + group * 8, 8)
+        return (ctx if half == 0 else sgrad)[rows, :]
+
+    planes = [[] for _ in range(9)]
+    for block in range(12):
+        for half in range(2):
+            for group in range(12):
+                word, bit = plane_of(block, half, group)
+                planes[word].append((block, half, group, bit))
+
+    def pack(word):
+        total = jnp.zeros((8, D), jnp.int32)
+        for block, half, group, bit in planes[word]:
+            piece = latent_piece(block, half, group)
+            total = total | jnp.where(piece > 0, jnp.int32(bit), jnp.int32(0))
+        words[me, word * 8 : (word + 1) * 8, :] = total
+
+    def part_of(owner, index):
+        return small.at[owner] if index == 3 else words.at[owner, index * 24 : (index + 1) * 24]
+
+    def z_send(index, hop):
+        ref = part_of(me, index)
+        peer = lax.rem(z + hop, 4) * 2 + core
+        return remote(ref, ref, zs.at[index, hop - 1], zr.at[index, hop - 1], (dp, peer))
+
+    def core_send(index, hop):
+        ref = part_of(lax.rem(z + 4 - hop, 4) * 2 + core, index)
+        return remote(ref, ref, cs_.at[index, hop], cr_.at[index, hop], over_core)
+
+    def send_out(index):
+        for hop in (2, 1, 3):
+            z_send(index, hop).start()
+        core_send(index, 0).start()
+
+    def pass_on(index):
+        for hop in (1, 3, 2):
+            z_send(index, hop).wait()
+            core_send(index, hop).start()
+
+    def all_here(index):
+        for hop in range(4):
+            core_send(index, hop).wait()
+
+    for half in range(2):
+        loads[half][0].wait()
+        loads[half][1].wait()
+    for word in range(3):
+        pack(word)
+    pl.semaphore_wait(greet, 6)
+    send_out(0)
+    for half in range(2):
+        loads[half][2].wait()
+        loads[half][3].wait()
+    slot_lane = lax.broadcasted_iota(jnp.int32, (8, 128), 1)
+
+    def scale_rows(group):
+        tile = jnp.zeros((8, 128), f32)
+        for half in range(2):
+            rows = pl.ds(pl.multiple_of(192 + half * BLOCK + group, 8), 8)
+            for index in range(7):
+                if index == 0:
+                    part = widened[rows, 0 : 3 * D]
+                elif index == 1:
+                    part = widened[rows, 3 * D : FF]
+                elif index == 2:
+                    part = widened[pl.ds(pl.multiple_of(half * BLOCK + group, 8), 8), :]
+                else:
+                    at = pl.ds(pl.multiple_of((index - 3) * BLOCK + group, 8), 8)
+                    part = (ctx if half == 0 else sgrad)[at, :]
+                fan = FF if index >= 3 else D
+                mean = jnp.sum(jnp.abs(part), axis=1, keepdims=True) * (1.0 / part.shape[1])
+                tile = jnp.where(slot_lane == index * 2 + half, mean / math.sqrt(fan), tile)
+        spread[pl.ds(group, 8), :] = tile
+
+    loop(12, 8, scale_rows)
+    spread[BLOCK:128, :] = jnp.zeros((128 - BLOCK, 128), f32)
+    small[me, 0:16, :] = spread[...].T[0:16, :]
+    small[me, 16:32, :] = jnp.zeros((16, 128), f32)
+    small[me, 16:19, 0:BLOCK] = tb[...]
+    small[me, 19:20, 0:BLOCK] = mb[...]
+    small[me, 20:21, 0:BLOCK] = nb[...]
+    small[me, 21:23, 0:BLOCK] = gain[...]
+    small[me, 23:25, 0:BLOCK] = shift[...]
+    for part in range(3):
+        small[me, 25 + part : 26 + part, :] = wb[:, part * 128 : (part + 1) * 128]
+    send_out(3)
+    for word in range(3, 6):
+        pack(word)
+    send_out(1)
+    for word in range(6, 9):
+        pack(word)
+    send_out(2)
     c0, c1, c2, c3 = level[0], level[1], level[2], level[3]
     i0, i1, i2, i3 = 1.0 / c0, 1.0 / c1, 1.0 / c2, 1.0 / c3
-    for part in range(6):
-        total = small[0, 96 + part * 16 : 112 + part * 16, :]
-        for owner in range(1, 8):
-            total = total + small[owner, 96 + part * 16 : 112 + part * 16, :]
-        prm[:, part * 128 : (part + 1) * 128] = total
-    for part in range(3):
-        bias[0:1, part * D : (part + 1) * D] = prm[part : part + 1, :]
-    for part in range(4):
-        wbias[0:1, part * D : (part + 1) * D] = prm[9 + part : 10 + part, :]
     sums[...] = jnp.zeros_like(sums)
     row = lax.broadcasted_iota(jnp.int32, (256, 256), 0)
     col = lax.broadcasted_iota(jnp.int32, (256, 256), 1)
@@ -660,11 +670,6 @@
     pair[1] = jnp.where(key_ok & query_ok, 1.0, 0.0)
     ones = jnp.where(query_ok, 1.0, 0.0)
 
-    for block in range(12):
-        unpack_block(
-            words, small, block, wt if block < 3 else wm if block == 3 else ww if block < 8 else wn
-        )
-
     def clip_in(r):
         x = hid[pl.ds(r, 128), :].astype(f32)
         lo = (c0 * jnp.tanh(x * i0)).astype(bf16)
@@ -672,12 +677,33 @@
         xlT[:, pl.ds(r, 128)] = lo.T
 
     loop(4, 128, clip_in)
+    pass_on(0)
+    pass_on(3)
+    all_here(3)
+    total = jnp.zeros((16, D), f32)
+    param_lane = lax.broadcasted_iota(jnp.int32, (16, 128), 1)
+    for owner in range(8):
+        turned = jnp.concatenate([small[owner, 0:16, :], jnp.zeros((112, 128), f32)], axis=0).T
+        scl[owner] = turned[0:BLOCK, :]
+        piece = jnp.where(param_lane < BLOCK, small[owner, 16:32, :], 0.0)
+        wide = jnp.concatenate([piece, jnp.zeros((16, D - 128), f32)], axis=1)
+        total = total + (pltpu.roll(wide, owner * BLOCK, 1) if owner else wide)
+        for part in range(3):
+            at = owner * 4 * BLOCK + part * 128
+            wbias[0:1, at : at + 128] = small[owner, 25 + part : 26 + part, :]
+    prm[...] = total
+    for part in range(3):
+        bias[0:1, part * D : (part + 1) * D] = prm[part : part + 1, :]
+    all_here(0)
+    for block in range(3):
+        unpack_block(words, scl, block, wt)
 
     def qkv_cols(c):
         cs = pl.ds(c, 256)
         qkv[:, cs] = (dot_nn(low[...], wt[:, cs]) + bias[0:1, cs]).astype(bf16)
 
     loop(9, 256, qkv_cols)
+    pass_on(1)
     lane = lax.broadcasted_iota(jnp.int32, (256, 128), 1)
     first = lane < 64
 
@@ -707,6 +733,8 @@
         return carry
 
     lax.fori_loop(0, 12, attend_pair, 0)
+    pass_on(2)
+    unpack_block(words, scl, 3, wm)
 
     def clip_ctx(r):
         lo = (c1 * jnp.tanh(ctx[pl.ds(r, 128), :] * i1)).astype(bf16)
@@ -733,15 +761,26 @@
         acc[rs, :] = normed + prm[4:5, :]
 
     loop(4, 128, norm_one)
+    all_here(1)
+    for block in range(4, 8):
+        unpack_block(words, scl, block, ww)
+    all_here(2)
+    for block in range(8, 12):
+        unpack_block(words, scl, block, wn)
 
     def feed(c):
         cs = pl.ds(c, 512)
-        w = dot_nn(low[...], ww[:, cs]) + wbias[0:1, cs]
-        widened[:, cs] = w
-        a = 0.5 * w * (1.0 + lax.erf(w * HALF_ROOT))
-        lo = (c3 * jnp.tanh(a * i3)).astype(bf16)
-        act[:, cs] = lo
-        acc[...] += dot_nn(lo, wn[cs, :])
+
+        def feed_rows(r):
+            rs = pl.ds(r, 256)
+            w = dot_nn(low[rs, :], ww[:, cs]) + wbias[0:1, cs]
+            widened[rs, cs] = w
+            a = 0.5 * w * (1.0 + lax.erf(w * HALF_ROOT))
+            lo = (c3 * jnp.tanh(a * i3)).astype(bf16)
+            act[rs, cs] = lo
+            acc[rs, :] += dot_nn(lo, wn[cs, :])
+
+        loop(2, 256, feed_rows)
 
     loop(6, 512, feed)
 
@@ -772,21 +811,26 @@
     loop(4, 128, norm_two)
 
     def feed_back(t):
-        cs = pl.ds(pl.multiple_of(t * 512, 512), 512)
-        g = dot_nt(low[...], wn[cs, :])
-        w = widened[:, cs]
-        e = 0.5 * (1.0 + lax.erf(w * HALF_ROOT))
-        a = w * e
-        u = a * i3
-        th = jnp.tanh(u)
-        slope = 1.0 - th * th
-        clip_sum = colsum(g * (th - u * slope))
-        sums[14:15, 0:512] += clip_sum
-        back = g * slope * (e + w * (DENSITY * jnp.exp(-0.5 * w * w)))
-        lo = back.astype(bf16)
-        wg[:, cs] = lo
-        wbias[1:2, cs] = colsum(lo.astype(f32))
-        acc[...] += dot_nt(lo, ww[:, cs])
+        cs = pl.ds(pl.multiple_of(t * CHUNK, CHUNK), CHUNK)
+        wbias[1:2, cs] = jnp.zeros((1, CHUNK), f32)
+
+        def feed_back_rows(r):
+            rs = pl.ds(r, 256)
+            g = dot_nt(low[rs, :], wn[cs, :])
+            w = widened[rs, cs]
+            e = 0.5 * (1.0 + lax.erf(w * HALF_ROOT))
+            a = w * e
+            u = a * i3
+            th = jnp.tanh(u)
+            slope = 1.0 - th * th
+            sums[14:15, 0:CHUNK] += colsum(g * (th - u * slope))
+            back = g * slope * (e + w * (DENSITY * jnp.exp(-0.5 * w * w)))
+            lo = back.astype(bf16)
+            wg[rs, cs] = lo
+            wbias[1:2, cs] += colsum(lo.astype(f32))
+            acc[rs, :] += dot_nt(lo, ww[:, cs])
+
+        loop(2, 256, feed_back_rows)
 
     def norm_one_back(r):
         rs = pl.ds(r, 128)
@@ -877,154 +921,203 @@
         sums[13:14, :] = line
         small_out[...] = sums[0:16, :]
 
-    dp = lax.axis_index("dp")
-    me = lax.axis_index("fsdp")
-    x = lax.rem(dp, 2)
-    y = lax.div(dp, 2)
-    z = lax.div(me, 2)
-    core = lax.rem(me, 2)
-    over_x = (dp + 1 - 2 * x, me)
-    over_y = (dp + 2 - 4 * y, me)
-    over_core = (dp, z * 2 + 1 - core)
     firsts = (over_x, over_y)
     seconds = (over_y, over_x)
-
-    def cols_of(p):
-        return pl.ds(p * 256, 256)
-
-    def remote(src, dst, send, recv, to):
-        return pltpu.make_async_remote_copy(
-            src_ref=src, dst_ref=dst, send_sem=send, recv_sem=recv, device_id=to,
-            device_id_type=MESH,
+    cols = (pl.ds(0, HALF), pl.ds(HALF, HALF))
+    outer = (z == 0) | (z == 3)
+    inner = (z == 1) | (z == 2)
+    near = z + 1 - 2 * lax.rem(z, 2)
+    beyond = 1 - lax.div(z, 2)
+
+    def on_z(to):
+        return (dp, to * 2 + core)
+
+    def core_copy(k):
+        slot, duo = lax.rem(k, SLOTS), lax.rem(k, 2)
+        return remote(pt.at[slot, :, 1 - core], rb.at[duo], s1.at[slot], r1.at[slot], over_core)
+
+    def first_copy(k, p):
+        slot, duo = lax.rem(k, SLOTS), lax.rem(k, 2)
+        if p == 0:
+            src = pt.at[slot, :, core, 1 - x, :, :, cols[p]]
+        else:
+            src = pt.at[slot, :, core, :, 1 - y, :, cols[p]]
+        return remote(src, rx.at[duo, p], s2.at[slot, p], r2.at[slot, p], firsts[p])
+
+    def own_rows(slot, blocks, p):
+        if p == 0:
+            return pt.at[slot, blocks, core, x, :, :, cols[p]]
+        return pt.at[slot, blocks, core, :, y, :, cols[p]]
+
+    def in_copy(k, p):
+        slot, duo = lax.rem(k, SLOTS), lax.rem(k, 2)
+        src = own_rows(slot, pl.ds(beyond, 3), p)
+        return remote(src, rz.at[duo, p], s3.at[slot, p], r3.at[slot, p], on_z(near))
+
+    def out_copy(k, p, kind):
+        slot = lax.rem(k, SLOTS)
+        to = (near, 3 - z, lax.rem(z + 2, 4))[kind]
+        return remote(
+            own_rows(slot, to, p), rf.at[slot, min(kind, 1), p], s4.at[slot, kind, p],
+            r4.at[slot, min(kind, 1), p], on_z(to),
         )
 
-    def core_copy(k):
+    def second_copy(k, p):
+        slot, duo = lax.rem(k, SLOTS), lax.rem(k, 2)
+        src = held.at[duo, p, 1 - y if p == 0 else 1 - x]
+        return remote(src, ry.at[duo, p], s5.at[slot, p], r5.at[slot, p], seconds[p])
+
+    def fin_cols(k, start, count):
+        return pl.ds(pl.multiple_of(lax.rem(k, SECTION) * CHUNK + start, 128), count)
+
+    def back_second(k, p):
         slot = lax.rem(k, SLOTS)
-        return remote(pt.at[slot, :, 1 - core], rb.at[lax.rem(k, 2)], s1.at[slot], r1.at[slot], over_core)
-
-    def one_copy(k, p):
+        ref = fin.at[lax.div(k, SECTION), x, y, :, fin_cols(k, p * HALF, HALF)]
+        return remote(ref, ref, s6.at[slot, p], r6.at[slot, p], seconds[p])
+
+    def back_first(k, p):
         slot = lax.rem(k, SLOTS)
         if p == 0:
-            src = pt.at[slot, :, core, 1 - x, :, :, cols_of(p)]
+            ref = fin.at[lax.div(k, SECTION), x, :, :, fin_cols(k, p * HALF, HALF)]
         else:
-            src = pt.at[slot, :, core, :, 1 - y, :, cols_of(p)]
-        return remote(src, rx.at[lax.rem(k, 2), p], s2.at[slot, p], r2.at[slot, p], firsts[p])
-
-    def two_copy(k, p):
-        slot = lax.rem(k, SLOTS)
-        if p == 0:
-            src = pt.at[slot, :, core, x, 1 - y, :, cols_of(p)]
-        else:
-            src = pt.at[slot, :, core, 1 - x, y, :, cols_of(p)]
-        return remote(src, ry.at[lax.rem(k, 2), p], s3.at[slot, p], r3.at[slot, p], seconds[p])
-
-    def z_copy(k, hop):
-        slot = lax.rem(k, SLOTS)
-        to = lax.rem(z + hop, 4)
-        return remote(
-            pt.at[slot, to, core, x, y], rz.at[lax.rem(k, 2), hop - 1], s4.at[slot, hop - 1],
-            r4.at[slot, hop - 1], (dp, to * 2 + core),
-        )
-
-    def fin_cols(k, start, count):
-        return pl.ds(pl.multiple_of(lax.rem(k, 6) * CHUNK + start, count), count)
-
-    def back_two(k, p):
-        slot = lax.rem(k, SLOTS)
-        ref = fin.at[lax.div(k, 6), x, y, :, fin_cols(k, p * 256, 256)]
-        return remote(ref, ref, s5.at[slot, p], r5.at[slot, p], seconds[p])
-
-    def back_one(k, p):
-        slot = lax.rem(k, SLOTS)
-        if p == 0:
-            ref = fin.at[lax.div(k, 6), x, :, :, fin_cols(k, p * 256, 256)]
-        else:
-            ref = fin.at[lax.div(k, 6), :, y, :, fin_cols(k, p * 256, 256)]
-        return remote(ref, ref, s6.at[slot, p], r6.at[slot, p], firsts[p])
+            ref = fin.at[lax.div(k, SECTION), :, y, :, fin_cols(k, p * HALF, HALF)]
+        return remote(ref, ref, s7.at[slot, p], r7.at[slot, p], firsts[p])
 
     def small_copy(step):
         to = (
-            over_core, over_x, over_y, (dp, lax.rem(z + 1, 4) * 2 + core),
-            (dp, lax.rem(z + 2, 4) * 2 + core), (dp, lax.rem(z + 3, 4) * 2 + core),
+            over_core, over_x, over_y, on_z(lax.rem(z + 1, 4)), on_z(lax.rem(z + 2, 4)),
+            on_z(lax.rem(z + 3, 4)),
         )[step]
         return remote(small_out, sin.at[step], sms.at[step], smr.at[step], to)
 
     def tick(t, carry):
-        @pl.when(t >= 6)
+        def stage(lag):
+            return (t >= lag) & (t < lag + CHUNKS)
+
+        @pl.when(stage(7))
         def _():
             for p in range(2):
-                back_one(t - 6, p).wait()
-
-        @pl.when((t >= 5) & (t < 5 + CHUNKS))
+                back_first(t - 7, p).wait()
+
+        @pl.when(stage(6))
         def _():
             for p in range(2):
-                back_two(t - 5, p).wait()
-                back_one(t - 5, p).start()
-
-        @pl.when((t >= 4) & (t < 4 + CHUNKS))
+                back_second(t - 6, p).wait()
+                back_first(t - 6, p).start()
+
+        @pl.when(stage(5))
+        def _():
+            k = t - 5
+            duo = lax.rem(k, 2)
+            for p in range(2):
+                second_copy(k, p).wait()
+                total = held[duo, p, y if p == 0 else x] + ry[duo, p]
+                fin[lax.div(k, SECTION), x, y, :, fin_cols(k, p * HALF, HALF)] = total
+                back_second(k, p).start()
+
+        @pl.when(stage(4) & outer)
         def _():
             k = t - 4
-            slot = lax.rem(k, SLOTS)
-            for hop in (1, 2, 3):
-                z_copy(k, hop).wait()
-            duo = lax.rem(k, 2)
-            total = pt[slot, z, core, x, y] + rz[duo, 0] + rz[duo, 1] + rz[duo, 2]
-            fin[lax.div(k, 6), x, y, :, fin_cols(k, 0, CHUNK)] = total
+            slot, duo = lax.rem(k, SLOTS), lax.rem(k, 2)
             for p in range(2):
-                back_two(k, p).start()
-
-        @pl.when((t >= 3) & (t < 3 + CHUNKS))
+                out_copy(k, p, 0).wait_recv()
+                out_copy(k, p, 2).wait_recv()
+                for i in range(2):
+                    own = (
+                        pt[slot, z, core, x, i, :, cols[p]]
+                        if p == 0
+                        else pt[slot, z, core, i, y, :, cols[p]]
+                    )
+                    held[duo, p, i] = own + rf[slot, 0, p, i] + rf[slot, 1, p, i]
+
+        @pl.when(stage(4) & inner)
+        def _():
+            k = t - 4
+            slot, duo = lax.rem(k, SLOTS), lax.rem(k, 2)
+            for p in range(2):
+                out_copy(k, p, 1).wait()
+                out_copy(k, p, 0).wait_send()
+                out_copy(k, p, 2).wait_send()
+                for i in range(2):
+                    own = (
+                        pt[slot, z, core, x, i, :, cols[p]]
+                        if p == 0
+                        else pt[slot, z, core, i, y, :, cols[p]]
+                    )
+                    held[duo, p, i] = own + rf[slot, 1, p, i]
+
+        @pl.when(stage(4))
+        def _():
+            for p in range(2):
+                second_copy(t - 4, p).start()
+
+        @pl.when(stage(3) & outer)
+        def _():
+            for p in range(2):
+                in_copy(t - 3, p).wait_send()
+
+        @pl.when(stage(3) & inner)
         def _():
             k = t - 3
-            slot = lax.rem(k, SLOTS)
+            slot, duo = lax.rem(k, SLOTS), lax.rem(k, 2)
             for p in range(2):
-                two_copy(k, p).wait()
-                for q in range(4):
-                    pt[slot, q, core, x, y, :, cols_of(p)] += ry[lax.rem(k, 2), p, q]
-            for hop in (1, 2, 3):
-                z_copy(k, hop).start()
-
-        @pl.when((t >= 2) & (t < 2 + CHUNKS))
+                in_copy(k, p).wait_recv()
+                for q in range(3):
+                    for i in range(2):
+                        if p == 0:
+                            pt[slot, beyond + q, core, x, i, :, cols[p]] += rz[duo, p, q, i]
+                        else:
+                            pt[slot, beyond + q, core, i, y, :, cols[p]] += rz[duo, p, q, i]
+                for kind in (2, 1, 0):
+                    out_copy(k, p, kind).start()
+
+        @pl.when(stage(2))
         def _():
             k = t - 2
-            slot = lax.rem(k, SLOTS)
+            slot, duo = lax.rem(k, SLOTS), lax.rem(k, 2)
             for p in range(2):
-                one_copy(k, p).wait()
+                first_copy(k, p).wait()
                 for q in range(4):
                     for i in range(2):
                         if p == 0:
-                            pt[slot, q, core, x, i, :, cols_of(p)] += rx[lax.rem(k, 2), p, q, i]
+                            pt[slot, q, core, x, i, :, cols[p]] += rx[duo, p, q, i]
                         else:
-                            pt[slot, q, core, i, y, :, cols_of(p)] += rx[lax.rem(k, 2), p, q, i]
-                two_copy(k, p).start()
-
-        @pl.when((t >= 1) & (t < 1 + CHUNKS))
+                            pt[slot, q, core, i, y, :, cols[p]] += rx[duo, p, q, i]
+
+                @pl.when(outer)
+                def _():
+                    in_copy(k, p).start()
+
+        @pl.when(stage(1))
         def _():
             k = t - 1
-            slot = lax.rem(k, SLOTS)
+            slot, duo = lax.rem(k, SLOTS), lax.rem(k, 2)
             core_copy(k).wait()
             for q in range(4):
-                pt[slot, q, core] += rb[lax.rem(k, 2), q]
+                pt[slot, q, core] += rb[duo, q]
             for p in range(2):
-                one_copy(k, p).start()
+                first_copy(k, p).start()
 
         slot = lax.rem(t, SLOTS)
 
-        def put(owner, cols, block):
+        def put(owner, cs, block):
             for i in range(2):
                 for j in range(2):
                     at = (i * 2 + j) * 24
-                    pt[slot, owner // 2, owner % 2, i, j, :, cols] = block[at : at + 24, :]
-
-        @pl.when(t < 6)
-        def _():
-            j = lax.div(t, 2)
-            rows = pl.ds(pl.multiple_of(lax.rem(t, 2) * 384, 384), 384)
-            left = nlT[rows, :]
+                    pt[slot, owner // 2, owner % 2, i, j, :, cs] = block[at : at + 24, :]
+
+        pieces = CHUNK // 128
+        turns = 8 // pieces
+
+        @pl.when(t < SECTION)
+        def _():
+            j = lax.div(t, turns)
+            count = pieces * BLOCK
+            left = nlT[pl.ds(pl.multiple_of(lax.rem(t, turns) * count, count), count), :]
             for owner in range(8):
-                cols = pl.ds(pl.multiple_of(owner * 384 + j * 128, 128), 128)
-                got = dot_nn(left, act[:, cols])
-                for part in range(4):
+                cs = pl.ds(pl.multiple_of(owner * 384 + j * 128, 128), 128)
+                got = dot_nn(left, act[:, cs])
+                for part in range(pieces):
                     put(owner, pl.ds(part * 128, 128), got[part * BLOCK : (part + 1) * BLOCK, :])
 
         def whole(left, right, half):
@@ -1032,80 +1125,84 @@
             for owner in range(8):
                 put(owner, pl.ds(half * 256, 256), got[owner * BLOCK : (owner + 1) * BLOCK, :])
 
-        @pl.when((t >= 6) & (t < 12))
-        def _():
-            for half in range(2):
-                cols = pl.ds(pl.multiple_of((t - 6) * CHUNK + half * 256, 256), 256)
-                whole(wlT[...], wg[:, cols], half)
-
-        for half in range(2):
-            part = (t - 12) * 2 + half
+        for half in range(CHUNK // 256):
+
+            @pl.when((t >= SECTION) & (t < 2 * SECTION))
+            def _():
+                cs = pl.ds(pl.multiple_of((t - SECTION) * CHUNK + half * 256, 256), 256)
+                whole(wlT[...], wg[:, cs], half)
+
+            part = (t - 2 * SECTION) * (CHUNK // 256) + half
 
             @pl.when((part >= 0) & (part < 3))
             def _():
-                cols = pl.ds(pl.multiple_of(part * 256, 256), 256)
-                whole(clT[...], low[:, cols], half)
+                whole(clT[...], low[:, pl.ds(pl.multiple_of(part * 256, 256), 256)], half)
 
             @pl.when((part >= 3) & (part < 12))
             def _():
-                cols = pl.ds(pl.multiple_of((part - 3) * 256, 256), 256)
-                whole(xlT[...], qkv[:, cols], half)
+                whole(xlT[...], qkv[:, pl.ds(pl.multiple_of((part - 3) * 256, 256), 256)], half)
 
         @pl.when(t < CHUNKS)
         def _():
             core_copy(t).start()
 
-        @pl.when(t < 6)
+        units = 12 // SECTION
+        begin = SECTION + 1
+
+        @pl.when(t < SECTION)
         def _():
             feed_back(t)
 
-        @pl.when(t == 6)
+        @pl.when(t == SECTION)
         def _():
             for slot in range(2):
                 scores_copy(slot, slot).start()
             loop(4, 128, norm_one_back)
             loop(3, 256, mix_back)
 
-        @pl.when((t >= 7) & (t < 13))
-        def _():
-            for slot in range(2):
-                u = (t - 7) * 2 + slot
-                scores_copy(u, slot).wait()
-                attend_pair_back(u, slot)
-
-                @pl.when(t < 12)
+        @pl.when((t >= begin) & (t < begin + SECTION))
+        def _():
+            for index in range(units):
+                u = (t - begin) * units + index
+                at = lax.rem(u, 2)
+                scores_copy(u, at).wait()
+                attend_pair_back(u, at)
+
+                @pl.when(u < 10)
                 def _():
-                    scores_copy(u + 2, slot).start()
-
-        @pl.when((t >= 13) & (t < 16))
-        def _():
-            input_back(pl.multiple_of((t - 13) * 256, 256))
-
-        @pl.when(t == 16)
+                    scores_copy(u + 2, at).start()
+
+        done = begin + SECTION
+
+        @pl.when((t >= done) & (t < done + 3))
+        def _():
+            input_back(pl.multiple_of((t - done) * 256, 256))
+
+        @pl.when(t == done + 3)
         def _():
             close_sums()
             small_copy(0).start()
 
-        @pl.when(t == 17)
+        @pl.when(t == done + 4)
         def _():
             small_copy(0).wait()
             small_out[...] += sin[0]
             small_copy(1).start()
 
-        @pl.when(t == 18)
+        @pl.when(t == done + 5)
         def _():
             small_copy(1).wait()
             small_out[...] += sin[1]
             small_copy(2).start()
 
-        @pl.when(t == 19)
+        @pl.when(t == done + 6)
         def _():
             small_copy(2).wait()
             small_out[...] += sin[2]
             for step in (3, 4, 5):
                 small_copy(step).start()
 
-        @pl.when(t == 20)
+        @pl.when(t == done + 7)
         def _():
             for step in (3, 4, 5):
                 small_copy(step).wait()
@@ -1113,10 +1210,10 @@
 
         return carry
 
-    lax.fori_loop(0, CHUNKS + 6, tick, 0)
-
-
-def layer(seq, live, level, words, small, hid, teach, teach_scores):
+    lax.fori_loop(0, CHUNKS + 7, tick, 0)
+
+
+def layer(*args):
     vm = pl.BlockSpec(memory_space=pltpu.VMEM)
     sm = pl.BlockSpec(memory_space=pltpu.SMEM)
     sds = jax.ShapeDtypeStruct
@@ -1129,9 +1226,13 @@
             sds((3, 2, 2, 24, FF), f32),
             sds((16, D), f32),
         ),
-        in_specs=[sm] * 3 + [vm] * 4 + [pl.BlockSpec(memory_space=pl.ANY)],
+        in_specs=[sm] * 3 + [vm] * 8 + [pl.BlockSpec(memory_space=pl.ANY)] * 5,
         out_specs=(vm,) * 4,
         scratch_shapes=[
+            pltpu.VMEM((8, 72, D), jnp.int32),
+            pltpu.VMEM((8, 32, 128), f32),
+            pltpu.VMEM((8, BLOCK, 128), f32),
+            pltpu.VMEM((128, 128), f32),
             pltpu.VMEM((D, 3 * D), bf16),
             pltpu.VMEM((D, D), bf16),
             pltpu.VMEM((D, FF), bf16),
@@ -1159,20 +1260,127 @@
             pltpu.VMEM((2, 2, 256, 256), bf16),
             pltpu.VMEM((SLOTS, 4, 2, 2, 2, 24, CHUNK), f32),
             pltpu.VMEM((2, 4, 2, 2, 24, CHUNK), f32),
-            pltpu.VMEM((2, 2, 4, 2, 24, 256), f32),
-            pltpu.VMEM((2, 2, 4, 24, 256), f32),
-            pltpu.VMEM((2, 3, 24, CHUNK), f32),
+            pltpu.VMEM((2, 2, 4, 2, 24, HALF), f32),
+            pltpu.VMEM((2, 2, 3, 2, 24, HALF), f32),
+            pltpu.VMEM((SLOTS, 2, 2, 2, 24, HALF), f32),
+            pltpu.VMEM((2, 2, 2, 24, HALF), f32),
+            pltpu.VMEM((2, 2, 24, HALF), f32),
             pltpu.VMEM((6, 16, D), f32),
         ]
         + [dma((SLOTS,))] * 2
         + [dma((SLOTS, 2))] * 4
-        + [dma((SLOTS, 3))] * 2
-        + [dma((SLOTS, 2))] * 4
+        + [dma((SLOTS, 3, 2)), dma((SLOTS, 2, 2))]
+        + [dma((SLOTS, 2))] * 6
         + [dma((6,))] * 2
-        + [dma((2,))],
-        compiler_params=pltpu.CompilerParams(has_side_effects=True, vmem_limit_bytes=LAYER_CAP),
+        + [dma((2,)), dma((2, 4)), dma((4, 3)), dma((4, 3)), dma((4, 4)), dma((4, 4))],
+        compiler_params=pltpu.CompilerParams(collective_id=0, has_side_effects=True, vmem_limit_bytes=LAYER_CAP),
         name="layer",
-    )(seq, live, level, words, small, hid, teach, teach_scores)
+    )(*args)
+
+
+def finish_kernel(
+    count, fin, small, tl, ml, wl, nl,
+    tg, mg, wg, ng, tb, mb, wb, nb, gain, shift, clips, loss,
+    fbuf, tin, min_, win, nin, tout, mout, wout, nout, fsem, isem, osem,
+):
+    fcopies = [pltpu.make_async_copy(fin.at[i], fbuf.at[i], fsem.at[i]) for i in range(3)]
+    icopies, ocopies = [], []
+    for half in range(2):
+        for index, (src, dst) in enumerate(((nl, nin), (wl, win), (ml, min_), (tl, tin))):
+            at = index * 2 + half
+            icopies.append(pltpu.make_async_copy(src.at[half], dst.at[half], isem.at[at]))
+    for half in range(2):
+        for index, (src, dst) in enumerate(((nout, ng), (wout, wg), (mout, mg), (tout, tg))):
+            at = index * 2 + half
+            ocopies.append(pltpu.make_async_copy(src.at[half], dst.at[half], osem.at[at]))
+    for index in range(4):
+        if index < 3:
+            fcopies[index].start()
+        icopies[index].start()
+        icopies[index + 4].start()
+    me = lax.axis_index("fsdp")
+    z = lax.div(me, 2)
+    core = lax.rem(me, 2)
+    own = pltpu.roll(small[...], lax.rem(8 - me, 8) * BLOCK, 1)
+    tb[...] = own[0:3, 0:BLOCK]
+    mb[...] = own[3:4, 0:BLOCK]
+    nb[...] = own[4:5, 0:BLOCK]
+    gain[...] = own[5:7, 0:BLOCK]
+    shift[...] = own[7:9, 0:BLOCK]
+    wide = pltpu.roll(small[...], core * (4 * BLOCK), 1)
+    row = lax.broadcasted_iota(jnp.int32, (16, D), 0)
+    picked = jnp.sum(jnp.where(row == 9 + z, wide, 0.0), axis=0, keepdims=True)
+    wb[...] = picked[:, 0 : 4 * BLOCK]
+    line = small[13:14, :]
+    lane = lax.broadcasted_iota(jnp.int32, (1, D), 1)
+    for spot in range(4):
+        clips[spot] = jnp.sum(jnp.where(lane == spot, line, 0.0))
+    loss[0, 0] = jnp.sum(jnp.where(lane == 4, line, 0.0)) * count[0]
+
+    def keep(latent, total, fan):
+        return jnp.where(jnp.abs(latent) <= 1.0, total * (1.0 / math.sqrt(fan)), 0.0)
+
+    def arrived(index):
+        icopies[index].wait()
+        icopies[index + 4].wait()
+
+    def leave(index):
+        ocopies[index].start()
+        ocopies[index + 4].start()
+
+    fcopies[0].wait()
+    arrived(0)
+    for j in range(3):
+        for i in range(2):
+            tiles = range((j * 2 + i) * 4, (j * 2 + i) * 4 + 4)
+            parts = [fbuf[0, :, tile * 128 : (tile + 1) * 128] for tile in tiles]
+            total = jnp.concatenate(parts, axis=0).T
+            rows = slice(j * 128, (j + 1) * 128)
+            cols = slice(i * 384, (i + 1) * 384)
+            for half in range(2):
+                nout[half, rows, cols] = keep(nin[half, rows, cols], total, FF)
+    leave(0)
+    fcopies[1].wait()
+    arrived(1)
+    for half in range(2):
+        wout[half] = keep(win[half], fbuf[1], D)
+    leave(1)
+    fcopies[2].wait()
+    arrived(2)
+    for half in range(2):
+        mout[half] = keep(min_[half], fbuf[2, :, 0:D], D)
+    leave(2)
+    arrived(3)
+    for half in range(2):
+        tout[half] = keep(tin[half], fbuf[2, :, D:], D)
+    leave(3)
+    for copy in ocopies:
+        copy.wait()
+
+
+def finish(count, fin, small, tl, ml, wl, nl):
+    vm = pl.BlockSpec(memory_space=pltpu.VMEM)
+    sm = pl.BlockSpec(memory_space=pltpu.SMEM)
+    hbm = pl.BlockSpec(memory_space=pl.ANY)
+    sds = jax.ShapeDtypeStruct
+    shapes = [v.shape for v in (tl, ml, wl, nl)]
+    dma = pltpu.SemaphoreType.DMA
+    return pl.pallas_call(
+        finish_kernel,
+        out_shape=[sds(v, f32) for v in shapes]
+        + [
+            sds((3, BLOCK), f32), sds((1, BLOCK), f32), sds((1, 4 * BLOCK), f32),
+            sds((1, BLOCK), f32), sds((2, BLOCK), f32), sds((2, BLOCK), f32),
+            sds((4,), f32), sds((1, 1), f32),
+        ],
+        in_specs=[sm, hbm, vm] + [hbm] * 4,
+        out_specs=[hbm] * 4 + [vm] * 6 + [sm] * 2,
+        scratch_shapes=[pltpu.VMEM((3, BLOCK, FF), f32)]
+        + [pltpu.VMEM(v, f32) for v in shapes] * 2
+        + [dma((3,)), dma((8,)), dma((8,))],
+        compiler_params=pltpu.CompilerParams(vmem_limit_bytes=VMEM_CAP),
+        name="finish",
+    )(count, fin, small, tl, ml, wl, nl)
 
 
 def on_device_fast(
@@ -1180,45 +1388,21 @@
     mixing_latent, widen_latent, narrow_latent, triple_bias, mixing_bias, widen_bias, narrow_bias,
     norm_gain, norm_shift, clip_level,
 ):
-    words, small = gather(
-        triple_latent, mixing_latent, widen_latent, narrow_latent, triple_bias,
-        mixing_bias[None], widen_bias[None], narrow_bias[None], norm_gain, norm_shift,
-    )
-    teach_scores = jnp.transpose(teacher_scores, (1, 0, 2))
     out, input_grad, fin, small_sum = layer(
-        seq_lengths, live_counts, clip_level, words, small, hidden_in, teacher_hidden, teach_scores
+        seq_lengths, live_counts, clip_level, triple_bias, mixing_bias[None], widen_bias[None],
+        narrow_bias[None], norm_gain, norm_shift, hidden_in, teacher_hidden,
+        jnp.transpose(teacher_scores, (1, 0, 2)), triple_latent, mixing_latent, widen_latent,
+        narrow_latent,
     )
     fin = fin.reshape(3, BLOCK, FF)
-    narrow_sum = (
-        fin[0].reshape(BLOCK, 3, 2, 4, 128).transpose(1, 4, 2, 3, 0).reshape(4 * BLOCK, D)
-    )
-    totals = (fin[2][:, D:], fin[2][:, :D], fin[1], narrow_sum)
-    latents = (triple_latent, mixing_latent, widen_latent, narrow_latent)
-    latent_grads = tuple(
-        (
-            jnp.where(jnp.abs(latent) <= 1.0, (total / math.sqrt(fan_in))[None], 0.0)
-            for latent, total, fan_in in zip(latents, totals, (D, D, D, FF))
-        )
-    )
-    me = lax.axis_index("fsdp")
-    own = lax.dynamic_slice_in_dim(small_sum[0:9], me * BLOCK, BLOCK, 1)
-    wide = lax.dynamic_slice_in_dim(small_sum[9:13].reshape(FF), me * 4 * BLOCK, 4 * BLOCK, 0)
     tokens = hidden_in.shape[0] * lax.axis_size("dp") * lax.axis_size("fsdp")
+    count = jnp.full((1,), 1.0 / (tokens * D), f32)
+    tg, mg, wg, ng, tb, mb, wb, nb, gain, shift, clips, loss = finish(
+        count, fin, small_sum, triple_latent, mixing_latent, widen_latent, narrow_latent
+    )
     return (
-        out,
-        small_sum[13, 4] / (tokens * D),
-        input_grad,
-        latent_grads[0],
-        latent_grads[1],
-        latent_grads[2],
-        latent_grads[3],
-        own[0:3],
-        own[3],
-        wide,
-        own[4],
-        own[5:7],
-        own[7:9],
-        small_sum[13, 0:4],
+        out, loss.reshape(()), input_grad, tg, mg, wg, ng, tb, mb.reshape(BLOCK),
+        wb.reshape(4 * BLOCK), nb.reshape(BLOCK), gain, shift, clips,
     )
 
 

time: 295 us -> 230 us (0.78)
  Pallas kernels: 262 us -> 224 us
  local copies, waits for them, and re-layouts: 18.5 us -> 3.28 us
  other arithmetic: 11.5 us -> 1.39 us
    pallas_call x1, Pallas kernels: 42.8 us -> 7.99 us  [finish(): pl.pallas_call(finish_kernel, out_shape=[sds(v, f32) for v in shapes] + [...]
    select_n x4 -> x0, other arithmetic: 7.15 us -> none  [on_device_fast(): jnp.where(jnp.abs(latent) <= 1.0, (total / math.sqrt(fan_in))[None], 0.0)]
    slice x4 -> x0, local copies, waits for them, and re-layouts: 4.75 us -> none  [the longest x1 1.41 us: on_device_fast(): own[7:9]]
    div x3 -> x0, local copies, waits for them, and re-layouts: 4.61 us -> none  [on_device_fast(): total / math.sqrt(fan_in)]
    div x3 -> x0, other arithmetic: 4.37 us -> none  [on_device_fast(): total / math.sqrt(fan_in)]
where the time goes in v3:
time: 230 us
  Pallas kernels  224 us (97%)
  local copies, waits for them, and re-layouts  3.28 us (1%)
    pallas_call x1, Pallas kernels, layer(): pl.pallas_call(layer_kernel, out_shape=(sds((ROWS, D), bf16), sds((ROWS,...  216 us
    pallas_call x1, Pallas kernels, finish(): pl.pallas_call(finish_kernel, out_shape=[sds(v, f32) for v in shapes] + [...  7.99 us

profile of v3, /device:TPU:0, one launch (start us, length us, event | category | flops | bytes accessed | tf_op | source)
XLA Modules:
  0.0 229.8 jit_solution(11860846742390879511)
XLA Ops:
  0.6 1.2 broadcast_in_dim.10.wb
  1.9 216.4 %layer.1 = (bf16[512,768]{1,0:T(8,128)(2,1)}, f32[512,768]{1,0:T(8,128)}, f32[3,2,2,24,3072]{4,3,2,1,0:T(8,128)}, f32[16,768]{1,0:T(8,128)}) custom-call(s32[1,4]{1,0:T(1,128)} %seq.1, s32[1,3]{1,0:T(1,128)} %live.1, f32[4]{0:T(128)} %level.1, f32[3,96]{1,0:T(4,128)} %tb.1, f32[1,96]{1,0:T(1,128)} %bitcast.9, f32[1,384]{1,0:T(1,128)} %broadcast_in_dim.10.wb, ...), custom_call_target="tpu_custom_call" | custom-call | tf_op jit(solution)/shard_map/layer/pallas_call | solution.py:1221
  218.3 0.0 copy-start.1
  218.3 8.0 %finish.1 = (f32[2,96,2304]{2,1,0:T(8,128)}, f32[2,96,768]{2,1,0:T(8,128)}, f32[2,96,3072]{2,1,0:T(8,128)}, f32[2,384,768]{2,1,0:T(8,128)}, f32[3,96]{1,0:T(4,12...) custom-call(f32[1]{0:T(128)} %constant.0.clone.1.count, ...), custom_call_target="tpu_custom_call" | custom-call | tf_op jit(solution)/shard_map/finish/pallas_call | solution.py:1368
  226.3 0.0 copy-start
  226.3 1.4 reduce
  227.7 0.0 copy-done.1
  227.7 0.9 copy.32
  228.6 0.0 copy-done
  228.6 1.1 copy.33
Async XLA Ops:
  218.3 9.4 %copy-start.1 = (bf16[512,768]{1,0:T(8,128)(2,1)S(1)}, bf16[512,768]{1,0:T(8,128)(2,1)}, u32[]{:S(2)}) copy-start(bf16[512,768]{1,0:T(8,128)(2,1)} %get-tuple-element.60) | copy-start | bytes 2359300
  226.3 2.3 copy-start

commit v4 on v3

--- a/solution.py
+++ b/solution.py
@@ -404,7 +404,8 @@
 CHUNK = 512
 HALF = CHUNK // 2
 SECTION = FF // CHUNK
-CHUNKS = 3 * SECTION
+WIDE = 3 * SECTION - 1
+CHUNKS = WIDE + 2
 SLOTS = 4
 
 
@@ -435,38 +436,42 @@
 
 
 def unpack_block(words, scl, block, dst):
+    def one(owner, carry):
+        unpack_owner(words, scl, block, dst, owner)
+        return carry
+
+    lax.fori_loop(0, 8, one, 0)
+
+
+def unpack_owner(words, scl, block, dst, owner):
     index = 0 if block < 3 else 1 if block == 3 else 2 if block < 8 else block - 5
 
-    def one(owner, carry):
-        for pair in range(6):
-            parts = []
-            for group in (2 * pair, 2 * pair + 1):
-                total = None
-                for half in range(2):
-                    word, bit = plane_of(block, half, group)
-                    bits = words[owner, word * 8 : (word + 1) * 8, :] & jnp.int32(bit)
-                    column = index * 2 + half
-                    scale = jnp.broadcast_to(
-                        scl[owner, group * 8 : (group + 1) * 8, column : column + 1], (8, D)
-                    )
-                    value = jnp.where(bits != 0, scale, -scale)
-                    total = value if total is None else total + value
-                parts.append(total)
-            tile = jnp.concatenate(parts, axis=0).astype(bf16)
-            if block < 8:
-                start = owner * BLOCK + pair * 16
-            else:
-                start = owner * (4 * BLOCK) + (block - 8) * BLOCK + pair * 16
-            rows = pl.ds(pl.multiple_of(start, 16), 16)
-            if block < 3:
-                dst[rows, block * D : (block + 1) * D] = tile
-            elif block < 8 and block > 3:
-                dst[rows, (block - 4) * D : (block - 3) * D] = tile
-            else:
-                dst[rows, :] = tile
-        return carry
-
-    lax.fori_loop(0, 8, one, 0)
+    for pair in range(6):
+        parts = []
+        for group in (2 * pair, 2 * pair + 1):
+            total = None
+            for half in range(2):
+                word, bit = plane_of(block, half, group)
+                bits = words[owner, word * 8 : (word + 1) * 8, :] & jnp.int32(bit)
+                column = index * 2 + half
+                scale = jnp.broadcast_to(
+                    scl[owner, group * 8 : (group + 1) * 8, column : column + 1], (8, D)
+                )
+                value = jnp.where(bits != 0, scale, -scale)
+                total = value if total is None else total + value
+            parts.append(total)
+        tile = jnp.concatenate(parts, axis=0).astype(bf16)
+        if block < 8:
+            start = owner * BLOCK + pair * 16
+        else:
+            start = owner * (4 * BLOCK) + (block - 8) * BLOCK + pair * 16
+        rows = pl.ds(pl.multiple_of(start, 16), 16)
+        if block < 3:
+            dst[rows, block * D : (block + 1) * D] = tile
+        elif block < 8 and block > 3:
+            dst[rows, (block - 4) * D : (block - 3) * D] = tile
+        else:
+            dst[rows, :] = tile
 
 
 def clip_back(grad, value, level, inverse):
@@ -504,7 +509,7 @@
     words, small, scl, spread,
     wt, wm, ww, wn, prm, bias, wbias, qkv, low, ctx, hat1, rstd1, widened, act, wg, sgrad,
     cgrad, valid, pair, xlT, clT, wlT, nlT, sums, tbuf, pt, rb, rx, rz, rf, held, ry, sin,
-    s1, r1, s2, r2, s3, r3, s4, r4, s5, r5, s6, r6, s7, r7, sms, smr, tsem, lsem, zs, zr, cs_, cr_,
+    s1, r1, s2, r2, s3, r3, s4, r4, s5, r5, s6, r6, sms, smr, tsem, lsem, zs, zr, cs_, cr_, hsem,
 ):
     dp = lax.axis_index("dp")
     me = lax.axis_index("fsdp")
@@ -527,6 +532,8 @@
         (dp, lax.rem(z + hop, 4) * 2 + core) for hop in (1, 2, 3)
     ):
         pl.semaphore_signal(greet, inc=1, device_id=to, device_id_type=MESH)
+
+    teach_load = pltpu.make_async_copy(teach, cgrad, hsem.at[0])
 
     loads = []
     for half in range(2):
@@ -544,6 +551,7 @@
     for index in range(4):
         for half in range(2):
             loads[half][index].start()
+    teach_load.start()
 
     def latent_piece(block, half, group):
         if block < 4:
@@ -637,12 +645,8 @@
     for part in range(3):
         small[me, 25 + part : 26 + part, :] = wb[:, part * 128 : (part + 1) * 128]
     send_out(3)
-    for word in range(3, 6):
+    for word in range(3, 9):
         pack(word)
-    send_out(1)
-    for word in range(6, 9):
-        pack(word)
-    send_out(2)
     c0, c1, c2, c3 = level[0], level[1], level[2], level[3]
     i0, i1, i2, i3 = 1.0 / c0, 1.0 / c1, 1.0 / c2, 1.0 / c3
     sums[...] = jnp.zeros_like(sums)
@@ -674,10 +678,8 @@
         x = hid[pl.ds(r, 128), :].astype(f32)
         lo = (c0 * jnp.tanh(x * i0)).astype(bf16)
         low[pl.ds(r, 128), :] = lo
-        xlT[:, pl.ds(r, 128)] = lo.T
 
     loop(4, 128, clip_in)
-    pass_on(0)
     pass_on(3)
     all_here(3)
     total = jnp.zeros((16, D), f32)
@@ -694,16 +696,30 @@
     prm[...] = total
     for part in range(3):
         bias[0:1, part * D : (part + 1) * D] = prm[part : part + 1, :]
-    all_here(0)
-    for block in range(3):
-        unpack_block(words, scl, block, wt)
-
-    def qkv_cols(c):
-        cs = pl.ds(c, 256)
+    def same_core(hop, carry):
+        @pl.when(hop > 0)
+        def _():
+            z_send(0, hop).wait()
+            core_send(0, hop).start()
+
+        for block in range(3):
+            unpack_owner(words, scl, block, wt, lax.rem(z + 4 - hop, 4) * 2 + core)
+        return carry
+
+    def other_core(hop, carry):
+        core_send(0, hop).wait()
+        for block in range(3):
+            unpack_owner(words, scl, block, wt, lax.rem(z + 4 - hop, 4) * 2 + 1 - core)
+        return carry
+
+    lax.fori_loop(0, 4, same_core, 0)
+    send_out(1)
+    lax.fori_loop(0, 4, other_core, 0)
+
+    for part in range(9):
+        cs = slice(part * 256, (part + 1) * 256)
         qkv[:, cs] = (dot_nn(low[...], wt[:, cs]) + bias[0:1, cs]).astype(bf16)
-
-    loop(9, 256, qkv_cols)
-    pass_on(1)
+    send_out(2)
     lane = lax.broadcasted_iota(jnp.int32, (256, 128), 1)
     first = lane < 64
 
@@ -716,38 +732,28 @@
         e = jnp.exp(masked - jnp.max(masked, axis=1, keepdims=True))
         return s, e / jnp.sum(e, axis=1, keepdims=True)
 
-    def attend_pair(u, carry):
-        g = lax.div(u, 6)
-        hp = lax.rem(u, 6)
-        rs = pl.ds(pl.multiple_of(g * 256, 256), 256)
-        qs = pl.multiple_of(hp * 128, 128)
-        q = qkv[rs, pl.ds(qs, 128)]
-        k = qkv[rs, pl.ds(pl.multiple_of(D + qs, 128), 128)]
-        v = qkv[rs, pl.ds(pl.multiple_of(2 * D + qs, 128), 128)]
-        ok = valid[g] > 0.5
-        parts = []
-        for j in range(2):
-            s, p = softmax(q, k, ok, j)
-            parts.append(dot_nn(p.astype(bf16), v))
-        ctx[rs, pl.ds(qs, 128)] = jnp.where(first, parts[0], parts[1])
-        return carry
-
-    lax.fori_loop(0, 12, attend_pair, 0)
-    pass_on(2)
+    for g in range(2):
+        for c in range(0, D, 128):
+            rs = slice(g * 256, (g + 1) * 256)
+            q, k, v = (qkv[rs, at + c : at + c + 128] for at in (0, D, 2 * D))
+            ok = valid[g] > 0.5
+            parts = []
+            for j in range(2):
+                s, p = softmax(q, k, ok, j)
+                parts.append(dot_nn(p.astype(bf16), v))
+            ctx[rs, c : c + 128] = jnp.where(first, parts[0], parts[1])
+    pass_on(1)
     unpack_block(words, scl, 3, wm)
 
     def clip_ctx(r):
         lo = (c1 * jnp.tanh(ctx[pl.ds(r, 128), :] * i1)).astype(bf16)
         low[pl.ds(r, 128), :] = lo
-        clT[:, pl.ds(r, 128)] = lo.T
 
     loop(4, 128, clip_ctx)
 
-    def mix_cols(c):
-        cs = pl.ds(c, 256)
+    for part in range(3):
+        cs = slice(part * 256, (part + 1) * 256)
         acc[:, cs] = dot_nn(low[...], wm[:, cs]) + prm[3:4, cs] + hid[:, cs].astype(f32)
-
-    loop(3, 256, mix_cols)
 
     def norm_one(r):
         rs = pl.ds(r, 128)
@@ -757,32 +763,32 @@
         normed = hat * prm[5:6, :] + prm[7:8, :]
         lo = (c2 * jnp.tanh(normed * i2)).astype(bf16)
         low[rs, :] = lo
-        wlT[:, rs] = lo.T
         acc[rs, :] = normed + prm[4:5, :]
 
     loop(4, 128, norm_one)
     all_here(1)
+    pass_on(2)
     for block in range(4, 8):
         unpack_block(words, scl, block, ww)
     all_here(2)
     for block in range(8, 12):
         unpack_block(words, scl, block, wn)
 
-    def feed(c):
-        cs = pl.ds(c, 512)
-
-        def feed_rows(r):
-            rs = pl.ds(r, 256)
-            w = dot_nn(low[rs, :], ww[:, cs]) + wbias[0:1, cs]
-            widened[rs, cs] = w
-            a = 0.5 * w * (1.0 + lax.erf(w * HALF_ROOT))
-            lo = (c3 * jnp.tanh(a * i3)).astype(bf16)
-            act[rs, cs] = lo
-            acc[rs, :] += dot_nn(lo, wn[cs, :])
-
-        loop(2, 256, feed_rows)
-
-    loop(6, 512, feed)
+    for t in range(8):
+        if t < 6:
+            cs = slice(t * 512, (t + 1) * 512)
+            widened[:, cs] = dot_nn(low[...], ww[:, cs]) + wbias[0:1, cs]
+        if 1 <= t <= 6:
+            cs = slice((t - 1) * 512, t * 512)
+            for r in range(0, ROWS, 64):
+                w = widened[r : r + 64, cs]
+                a = 0.5 * w * (1.0 + lax.erf(w * HALF_ROOT))
+                act[r : r + 64, cs] = (c3 * jnp.tanh(a * i3)).astype(bf16)
+        if t >= 2:
+            cs = slice((t - 2) * 512, (t - 1) * 512)
+            acc[...] += dot_nn(act[:, cs], wn[cs, :])
+
+    teach_load.wait()
 
     def norm_two(r):
         rs = pl.ds(r, 128)
@@ -796,7 +802,7 @@
         l3 = jnp.where(live[0, 2] > 1, l3, 0)
         ok = (at < l0) | ((at >= 256) & (at < 256 + l1)) | ((at >= 384) & (at < 384 + l2))
         ok = ok | ((at >= 448) & (at < 448 + l3))
-        gap = jnp.where(ok, full - teach[rs, :].astype(f32), 0.0)
+        gap = jnp.where(ok, full - cgrad[rs, :].astype(f32), 0.0)
         sums[15:16, :] += colsum(gap * gap) * 0.5
         sums[6:7, :] += colsum(gap * hat)
         sums[8:9, :] += colsum(gap)
@@ -831,6 +837,18 @@
             acc[rs, :] += dot_nt(lo, ww[:, cs])
 
         loop(2, 256, feed_back_rows)
+
+    def turn_widen(r):
+        rs = pl.ds(r, 128)
+        normed = hat1[rs, :] * prm[5:6, :] + prm[7:8, :]
+        wlT[:, rs] = (c2 * jnp.tanh(normed * i2)).astype(bf16).T
+
+    def turn_context(r):
+        clT[:, pl.ds(r, 128)] = (c1 * jnp.tanh(ctx[pl.ds(r, 128), :] * i1)).astype(bf16).T
+
+    def turn_inputs(r):
+        v = hid[pl.ds(r, 128), :].astype(f32)
+        xlT[:, pl.ds(r, 128)] = (c0 * jnp.tanh(v * i0)).astype(bf16).T
 
     def norm_one_back(r):
         rs = pl.ds(r, 128)
@@ -923,7 +941,6 @@
 
     firsts = (over_x, over_y)
     seconds = (over_y, over_x)
-    cols = (pl.ds(0, HALF), pl.ds(HALF, HALF))
     outer = (z == 0) | (z == 3)
     inner = (z == 1) | (z == 2)
     near = z + 1 - 2 * lax.rem(z, 2)
@@ -932,56 +949,63 @@
     def on_z(to):
         return (dp, to * 2 + core)
 
-    def core_copy(k):
+    def lanes(p, w):
+        return pl.ds(p * (w // 2), w // 2)
+
+    def core_copy(k, w):
         slot, duo = lax.rem(k, SLOTS), lax.rem(k, 2)
-        return remote(pt.at[slot, :, 1 - core], rb.at[duo], s1.at[slot], r1.at[slot], over_core)
-
-    def first_copy(k, p):
+        cs = pl.ds(0, w)
+        return remote(
+            pt.at[slot, :, 1 - core, :, :, :, cs], rb.at[duo, :, :, :, :, cs], s1.at[slot],
+            r1.at[slot], over_core,
+        )
+
+    def own_rows(slot, blocks, p, w, mine):
+        i = (x if p == 0 else y) if mine else (1 - x if p == 0 else 1 - y)
+        if p == 0:
+            return pt.at[slot, blocks, core, i, :, :, lanes(p, w)]
+        return pt.at[slot, blocks, core, :, i, :, lanes(p, w)]
+
+    def first_copy(k, w, p):
         slot, duo = lax.rem(k, SLOTS), lax.rem(k, 2)
-        if p == 0:
-            src = pt.at[slot, :, core, 1 - x, :, :, cols[p]]
-        else:
-            src = pt.at[slot, :, core, :, 1 - y, :, cols[p]]
-        return remote(src, rx.at[duo, p], s2.at[slot, p], r2.at[slot, p], firsts[p])
-
-    def own_rows(slot, blocks, p):
-        if p == 0:
-            return pt.at[slot, blocks, core, x, :, :, cols[p]]
-        return pt.at[slot, blocks, core, :, y, :, cols[p]]
-
-    def in_copy(k, p):
+        src = own_rows(slot, pl.ds(0, 4), p, w, False)
+        dst = rx.at[duo, p, :, :, :, lanes(0, w)]
+        return remote(src, dst, s2.at[slot, p], r2.at[slot, p], firsts[p])
+
+    def in_copy(k, w, p):
         slot, duo = lax.rem(k, SLOTS), lax.rem(k, 2)
-        src = own_rows(slot, pl.ds(beyond, 3), p)
-        return remote(src, rz.at[duo, p], s3.at[slot, p], r3.at[slot, p], on_z(near))
-
-    def out_copy(k, p, kind):
+        src = own_rows(slot, pl.ds(beyond, 3), p, w, True)
+        dst = rz.at[duo, p, :, :, :, lanes(0, w)]
+        return remote(src, dst, s3.at[slot, p], r3.at[slot, p], on_z(near))
+
+    def out_copy(k, w, p, kind):
         slot = lax.rem(k, SLOTS)
         to = (near, 3 - z, lax.rem(z + 2, 4))[kind]
         return remote(
-            own_rows(slot, to, p), rf.at[slot, min(kind, 1), p], s4.at[slot, kind, p],
-            r4.at[slot, min(kind, 1), p], on_z(to),
+            own_rows(slot, to, p, w, True), rf.at[slot, min(kind, 1), p, :, :, lanes(0, w)],
+            s4.at[slot, kind, p], r4.at[slot, min(kind, 1), p], on_z(to),
         )
 
-    def second_copy(k, p):
+    def second_copy(k, w, p):
         slot, duo = lax.rem(k, SLOTS), lax.rem(k, 2)
-        src = held.at[duo, p, 1 - y if p == 0 else 1 - x]
-        return remote(src, ry.at[duo, p], s5.at[slot, p], r5.at[slot, p], seconds[p])
-
-    def fin_cols(k, start, count):
-        return pl.ds(pl.multiple_of(lax.rem(k, SECTION) * CHUNK + start, 128), count)
-
-    def back_second(k, p):
+        cs = lanes(0, w)
+        return remote(
+            held.at[duo, p, :, :, cs], ry.at[duo, p, :, :, cs], s5.at[slot, p], r5.at[slot, p],
+            seconds[p],
+        )
+
+    def fin_at(k, w, p, rows):
+        if w == CHUNK:
+            flat = k * CHUNK
+        else:
+            flat = WIDE * CHUNK + (k - WIDE) * w
+        cs = pl.ds(pl.multiple_of(lax.rem(flat, FF) + p * (w // 2), 128), w // 2)
+        return (lax.div(flat, FF), *((x, rows) if p == 0 else (rows, y)), slice(None), cs)
+
+    def back_first(k, w, p):
         slot = lax.rem(k, SLOTS)
-        ref = fin.at[lax.div(k, SECTION), x, y, :, fin_cols(k, p * HALF, HALF)]
-        return remote(ref, ref, s6.at[slot, p], r6.at[slot, p], seconds[p])
-
-    def back_first(k, p):
-        slot = lax.rem(k, SLOTS)
-        if p == 0:
-            ref = fin.at[lax.div(k, SECTION), x, :, :, fin_cols(k, p * HALF, HALF)]
-        else:
-            ref = fin.at[lax.div(k, SECTION), :, y, :, fin_cols(k, p * HALF, HALF)]
-        return remote(ref, ref, s7.at[slot, p], r7.at[slot, p], firsts[p])
+        ref = fin.at[fin_at(k, w, p, slice(None))]
+        return remote(ref, ref, s6.at[slot, p], r6.at[slot, p], firsts[p])
 
     def small_copy(step):
         to = (
@@ -990,113 +1014,107 @@
         )[step]
         return remote(small_out, sin.at[step], sms.at[step], smr.at[step], to)
 
-    def tick(t, carry):
-        def stage(lag):
-            return (t >= lag) & (t < lag + CHUNKS)
-
-        @pl.when(stage(7))
+    def finish_first(k, w):
+        for p in range(2):
+            back_first(k, w, p).wait()
+
+    def finish_second(k, w):
+        duo = lax.rem(k, 2)
+        for p in range(2):
+            second_copy(k, w, p).wait()
+            for i in range(2):
+                cs = lanes(0, w)
+                fin[fin_at(k, w, p, i)] = held[duo, p, i, :, cs] + ry[duo, p, i, :, cs]
+            back_first(k, w, p).start()
+
+    def finish_out(k, w):
+        slot, duo = lax.rem(k, SLOTS), lax.rem(k, 2)
+        cs = lanes(0, w)
+
+        @pl.when(outer)
         def _():
             for p in range(2):
-                back_first(t - 7, p).wait()
-
-        @pl.when(stage(6))
+                out_copy(k, w, p, 0).wait_recv()
+                out_copy(k, w, p, 2).wait_recv()
+                for i in range(2):
+                    at = (x, i) if p == 0 else (i, y)
+                    own = pt[(slot, z, core, *at, slice(None), lanes(p, w))]
+                    held[duo, p, i, :, cs] = (
+                        own + rf[slot, 0, p, i, :, cs] + rf[slot, 1, p, i, :, cs]
+                    )
+
+        @pl.when(inner)
         def _():
             for p in range(2):
-                back_second(t - 6, p).wait()
-                back_first(t - 6, p).start()
-
-        @pl.when(stage(5))
-        def _():
-            k = t - 5
-            duo = lax.rem(k, 2)
+                out_copy(k, w, p, 1).wait()
+                out_copy(k, w, p, 0).wait_send()
+                out_copy(k, w, p, 2).wait_send()
+                for i in range(2):
+                    at = (x, i) if p == 0 else (i, y)
+                    own = pt[(slot, z, core, *at, slice(None), lanes(p, w))]
+                    held[duo, p, i, :, cs] = own + rf[slot, 1, p, i, :, cs]
+
+        for p in range(2):
+            second_copy(k, w, p).start()
+
+    def finish_in(k, w):
+        slot, duo = lax.rem(k, SLOTS), lax.rem(k, 2)
+
+        @pl.when(outer)
+        def _():
             for p in range(2):
-                second_copy(k, p).wait()
-                total = held[duo, p, y if p == 0 else x] + ry[duo, p]
-                fin[lax.div(k, SECTION), x, y, :, fin_cols(k, p * HALF, HALF)] = total
-                back_second(k, p).start()
-
-        @pl.when(stage(4) & outer)
-        def _():
-            k = t - 4
-            slot, duo = lax.rem(k, SLOTS), lax.rem(k, 2)
+                in_copy(k, w, p).wait_send()
+
+        @pl.when(inner)
+        def _():
             for p in range(2):
-                out_copy(k, p, 0).wait_recv()
-                out_copy(k, p, 2).wait_recv()
-                for i in range(2):
-                    own = (
-                        pt[slot, z, core, x, i, :, cols[p]]
-                        if p == 0
-                        else pt[slot, z, core, i, y, :, cols[p]]
-                    )
-                    held[duo, p, i] = own + rf[slot, 0, p, i] + rf[slot, 1, p, i]
-
-        @pl.when(stage(4) & inner)
-        def _():
-            k = t - 4
-            slot, duo = lax.rem(k, SLOTS), lax.rem(k, 2)
-            for p in range(2):
-                out_copy(k, p, 1).wait()
-                out_copy(k, p, 0).wait_send()
-                out_copy(k, p, 2).wait_send()
-                for i in range(2):
-                    own = (
-                        pt[slot, z, core, x, i, :, cols[p]]
-                        if p == 0
-                        else pt[slot, z, core, i, y, :, cols[p]]
-                    )
-                    held[duo, p, i] = own + rf[slot, 1, p, i]
-
-        @pl.when(stage(4))
-        def _():
-            for p in range(2):
-                second_copy(t - 4, p).start()
-
-        @pl.when(stage(3) & outer)
-        def _():
-            for p in range(2):
-                in_copy(t - 3, p).wait_send()
-
-        @pl.when(stage(3) & inner)
-        def _():
-            k = t - 3
-            slot, duo = lax.rem(k, SLOTS), lax.rem(k, 2)
-            for p in range(2):
-                in_copy(k, p).wait_recv()
+                in_copy(k, w, p).wait_recv()
                 for q in range(3):
                     for i in range(2):
-                        if p == 0:
-                            pt[slot, beyond + q, core, x, i, :, cols[p]] += rz[duo, p, q, i]
-                        else:
-                            pt[slot, beyond + q, core, i, y, :, cols[p]] += rz[duo, p, q, i]
+                        at = (x, i) if p == 0 else (i, y)
+                        at = (slot, beyond + q, core, *at, slice(None), lanes(p, w))
+                        pt[at] += rz[duo, p, q, i, :, lanes(0, w)]
                 for kind in (2, 1, 0):
-                    out_copy(k, p, kind).start()
-
-        @pl.when(stage(2))
-        def _():
-            k = t - 2
-            slot, duo = lax.rem(k, SLOTS), lax.rem(k, 2)
-            for p in range(2):
-                first_copy(k, p).wait()
-                for q in range(4):
-                    for i in range(2):
-                        if p == 0:
-                            pt[slot, q, core, x, i, :, cols[p]] += rx[duo, p, q, i]
-                        else:
-                            pt[slot, q, core, i, y, :, cols[p]] += rx[duo, p, q, i]
-
-                @pl.when(outer)
-                def _():
-                    in_copy(k, p).start()
-
-        @pl.when(stage(1))
-        def _():
-            k = t - 1
-            slot, duo = lax.rem(k, SLOTS), lax.rem(k, 2)
-            core_copy(k).wait()
+                    out_copy(k, w, p, kind).start()
+
+    def finish_one(k, w):
+        slot, duo = lax.rem(k, SLOTS), lax.rem(k, 2)
+        for p in range(2):
+            first_copy(k, w, p).wait()
             for q in range(4):
-                pt[slot, q, core] += rb[duo, q]
-            for p in range(2):
-                first_copy(k, p).start()
+                for i in range(2):
+                    at = (x, i) if p == 0 else (i, y)
+                    at = (slot, q, core, *at, slice(None), lanes(p, w))
+                    pt[at] += rx[duo, p, q, i, :, lanes(0, w)]
+
+            @pl.when(outer)
+            def _():
+                in_copy(k, w, p).start()
+
+    def finish_core(k, w):
+        slot, duo = lax.rem(k, SLOTS), lax.rem(k, 2)
+        core_copy(k, w).wait()
+        cs = pl.ds(0, w)
+        for q in range(4):
+            pt[slot, q, core, :, :, :, cs] += rb[duo, q, :, :, :, cs]
+        for p in range(2):
+            first_copy(k, w, p).start()
+
+    stages = (
+        (6, finish_first), (5, finish_second), (4, finish_out), (3, finish_in), (2, finish_one),
+        (1, finish_core),
+    )
+
+    def tick(t, carry):
+        for lag, step in stages:
+
+            @pl.when((t >= lag) & (t < lag + WIDE))
+            def _():
+                step(t - lag, CHUNK)
+
+            @pl.when((t >= lag + WIDE) & (t < lag + CHUNKS))
+            def _():
+                step(t - lag, HALF)
 
         slot = lax.rem(t, SLOTS)
 
@@ -1125,26 +1143,38 @@
             for owner in range(8):
                 put(owner, pl.ds(half * 256, 256), got[owner * BLOCK : (owner + 1) * BLOCK, :])
 
-        for half in range(CHUNK // 256):
+        for half in range(2):
 
             @pl.when((t >= SECTION) & (t < 2 * SECTION))
             def _():
                 cs = pl.ds(pl.multiple_of((t - SECTION) * CHUNK + half * 256, 256), 256)
                 whole(wlT[...], wg[:, cs], half)
 
-            part = (t - 2 * SECTION) * (CHUNK // 256) + half
+            part = (t - 2 * SECTION) * 2 + half
 
             @pl.when((part >= 0) & (part < 3))
             def _():
                 whole(clT[...], low[:, pl.ds(pl.multiple_of(part * 256, 256), 256)], half)
 
-            @pl.when((part >= 3) & (part < 12))
+            @pl.when((part >= 3) & (part < 10))
             def _():
                 whole(xlT[...], qkv[:, pl.ds(pl.multiple_of((part - 3) * 256, 256), 256)], half)
 
-        @pl.when(t < CHUNKS)
-        def _():
-            core_copy(t).start()
+        @pl.when(t < WIDE)
+        def _():
+            core_copy(t, CHUNK).start()
+
+        @pl.when((t >= WIDE) & (t < CHUNKS))
+        def _():
+            cs = pl.ds(pl.multiple_of((t - WIDE + 7) * 256, 256), 256)
+            whole(xlT[...], qkv[:, cs], 0)
+            core_copy(t, HALF).start()
+
+        for when, turn in ((3, turn_inputs), (4, turn_context), (5, turn_widen)):
+
+            @pl.when(t == when)
+            def _():
+                loop(4, 128, turn)
 
         units = 12 // SECTION
         begin = SECTION + 1
@@ -1210,7 +1240,7 @@
 
         return carry
 
-    lax.fori_loop(0, CHUNKS + 7, tick, 0)
+    lax.fori_loop(0, CHUNKS + 6, tick, 0)
 
 
 def layer(*args):
@@ -1226,7 +1256,7 @@
             sds((3, 2, 2, 24, FF), f32),
             sds((16, D), f32),
         ),
-        in_specs=[sm] * 3 + [vm] * 8 + [pl.BlockSpec(memory_space=pl.ANY)] * 5,
+        in_specs=[sm] * 3 + [vm] * 7 + [pl.BlockSpec(memory_space=pl.ANY)] * 6,
         out_specs=(vm,) * 4,
         scratch_shapes=[
             pltpu.VMEM((8, 72, D), jnp.int32),
@@ -1264,15 +1294,15 @@
             pltpu.VMEM((2, 2, 3, 2, 24, HALF), f32),
             pltpu.VMEM((SLOTS, 2, 2, 2, 24, HALF), f32),
             pltpu.VMEM((2, 2, 2, 24, HALF), f32),
-            pltpu.VMEM((2, 2, 24, HALF), f32),
+            pltpu.VMEM((2, 2, 2, 24, HALF), f32),
             pltpu.VMEM((6, 16, D), f32),
         ]
         + [dma((SLOTS,))] * 2
         + [dma((SLOTS, 2))] * 4
         + [dma((SLOTS, 3, 2)), dma((SLOTS, 2, 2))]
-        + [dma((SLOTS, 2))] * 6
+        + [dma((SLOTS, 2))] * 4
         + [dma((6,))] * 2
-        + [dma((2,)), dma((2, 4)), dma((4, 3)), dma((4, 3)), dma((4, 4)), dma((4, 4))],
+        + [dma((2,)), dma((2, 4)), dma((4, 3)), dma((4, 3)), dma((4, 4)), dma((4, 4)), dma((1,))],
         compiler_params=pltpu.CompilerParams(collective_id=0, has_side_effects=True, vmem_limit_bytes=LAYER_CAP),
         name="layer",
     )(*args)

time: 230 us -> 215 us (0.935)
  Pallas kernels: 224 us -> 209 us
    pallas_call x1, Pallas kernels: 216 us -> 201 us  [layer(): pl.pallas_call(layer_kernel, out_shape=(sds((ROWS, D), bf16), sds((ROWS,...]
where the time goes in v4:
time: 215 us; the launch traced here: 214 us
  Pallas kernels  209 us (97%)
  local copies, waits for them, and re-layouts  3.28 us (2%)
    pallas_call x1, Pallas kernels, layer(): pl.pallas_call(layer_kernel, out_shape=(sds((ROWS, D), bf16), sds((ROWS,...  201 us
    pallas_call x1, Pallas kernels, finish(): pl.pallas_call(finish_kernel, out_shape=[sds(v, f32) for v in shapes] + [...  7.99 us

profile of v4, /device:TPU:0, one launch (start us, length us, event | category | flops | bytes accessed | tf_op | source)
XLA Modules:
  0.0 214.5 jit_solution(8748975682550624468)
XLA Ops:
  0.6 1.2 broadcast_in_dim.10.wb
  1.9 201.2 %layer.1 = (bf16[512,768]{1,0:T(8,128)(2,1)}, f32[512,768]{1,0:T(8,128)}, f32[3,2,2,24,3072]{4,3,2,1,0:T(8,128)}, f32[16,768]{1,0:T(8,128)}) custom-call(s32[1,4]{1,0:T(1,128)} %seq.1, s32[1,3]{1,0:T(1,128)} %live.1, f32[4]{0:T(128)} %level.1, f32[3,96]{1,0:T(4,128)} %tb.1, f32[1,96]{1,0:T(1,128)} %bitcast.9, f32[1,384]{1,0:T(1,128)} %broadcast_in_dim.10.wb, ...), custom_call_target="tpu_custom_call" | custom-call | tf_op jit(solution)/shard_map/layer/pallas_call | solution.py:1251
  203.1 0.0 copy-start.1
  203.1 8.0 %finish.1 = (f32[2,96,2304]{2,1,0:T(8,128)}, f32[2,96,768]{2,1,0:T(8,128)}, f32[2,96,3072]{2,1,0:T(8,128)}, f32[2,384,768]{2,1,0:T(8,128)}, f32[3,96]{1,0:T(4,12...) custom-call(f32[1]{0:T(128)} %constant.0.clone.1.count, ...), custom_call_target="tpu_custom_call" | custom-call | tf_op jit(solution)/shard_map/finish/pallas_call | solution.py:1398
  211.1 0.0 copy-start
  211.1 1.4 reduce
  212.5 0.0 copy-done.1
  212.5 0.9 copy.32
  213.3 0.0 copy-done
  213.3 1.1 copy.33
Async XLA Ops:
  203.1 9.4 %copy-start.1 = (bf16[512,768]{1,0:T(8,128)(2,1)S(1)}, bf16[512,768]{1,0:T(8,128)(2,1)}, u32[]{:S(2)}) copy-start(bf16[512,768]{1,0:T(8,128)(2,1)} %get-tuple-element.60) | copy-start | bytes 2359300
  211.1 2.3 %copy-start = (f32[512,768]{1,0:T(8,128)S(1)}, f32[512,768]{1,0:T(8,128)}, u32[]{:S(2)}) copy-start(f32[512,768]{1,0:T(8,128)} %get-tuple-element.62) | copy-start | bytes 4718596

commit v5 on v4

--- a/solution.py
+++ b/solution.py
@@ -504,12 +504,12 @@
 
 
 def layer_kernel(
-    seq, live, level, tb, mb, wb, nb, gain, shift, hid, teach, teach_scores, tl, ml, wl, nl,
-    out, acc, fin, small_out,
-    words, small, scl, spread,
+    seq, live, level, tb, mb, wb, nb, gain, shift, hid_in, teach, teach_scores, tl, ml, wl, nl,
+    out_to, acc_to, fin_to, kept_to, small_out,
+    out, acc, fin, kept, hid, words, small, scl, spread,
     wt, wm, ww, wn, prm, bias, wbias, qkv, low, ctx, hat1, rstd1, widened, act, wg, sgrad,
-    cgrad, valid, pair, xlT, clT, wlT, nlT, sums, tbuf, pt, rb, rx, rz, rf, held, ry, sin,
-    s1, r1, s2, r2, s3, r3, s4, r4, s5, r5, s6, r6, sms, smr, tsem, lsem, zs, zr, cs_, cr_, hsem,
+    cgrad, valid, pair, xlT, clT, wlT, nlT, sums, tbuf, pt, rb, rx, rz, rf, held, ry, rd, sin,
+    s1, r1, s2, r2, s3, r3, s4, r4, s5, r5, s6, r6, sms, smr, tsem, lsem, zs, zr, cs_, cr_, hsem, fsem, s7, r7,
 ):
     dp = lax.axis_index("dp")
     me = lax.axis_index("fsdp")
@@ -534,6 +534,10 @@
         pl.semaphore_signal(greet, inc=1, device_id=to, device_id_type=MESH)
 
     teach_load = pltpu.make_async_copy(teach, cgrad, hsem.at[0])
+    hid_load = pltpu.make_async_copy(hid_in, hid, hsem.at[1])
+    out_save = pltpu.make_async_copy(out, out_to, hsem.at[2])
+    acc_save = pltpu.make_async_copy(acc, acc_to, hsem.at[3])
+    kept_save = pltpu.make_async_copy(kept, kept_to, hsem.at[4])
 
     loads = []
     for half in range(2):
@@ -551,6 +555,7 @@
     for index in range(4):
         for half in range(2):
             loads[half][index].start()
+    hid_load.start()
     teach_load.start()
 
     def latent_piece(block, half, group):
@@ -575,6 +580,13 @@
             piece = latent_piece(block, half, group)
             total = total | jnp.where(piece > 0, jnp.int32(bit), jnp.int32(0))
         words[me, word * 8 : (word + 1) * 8, :] = total
+
+    def pack_kept(word):
+        total = jnp.zeros((8, D), jnp.int32)
+        for block, half, group, bit in planes[word]:
+            piece = jnp.abs(latent_piece(block, half, group))
+            total = total | jnp.where(piece <= 1.0, jnp.int32(bit), jnp.int32(0))
+        kept[word * 8 : (word + 1) * 8, :] = total
 
     def part_of(owner, index):
         return small.at[owner] if index == 3 else words.at[owner, index * 24 : (index + 1) * 24]
@@ -643,10 +655,13 @@
     small[me, 21:23, 0:BLOCK] = gain[...]
     small[me, 23:25, 0:BLOCK] = shift[...]
     for part in range(3):
-        small[me, 25 + part : 26 + part, :] = wb[:, part * 128 : (part + 1) * 128]
+        small[me, 25 + part : 26 + part, :] = wb[part * 128 : (part + 1) * 128].reshape(1, 128)
     send_out(3)
     for word in range(3, 9):
         pack(word)
+    for word in range(9):
+        pack_kept(word)
+    kept_save.start()
     c0, c1, c2, c3 = level[0], level[1], level[2], level[3]
     i0, i1, i2, i3 = 1.0 / c0, 1.0 / c1, 1.0 / c2, 1.0 / c3
     sums[...] = jnp.zeros_like(sums)
@@ -679,6 +694,7 @@
         lo = (c0 * jnp.tanh(x * i0)).astype(bf16)
         low[pl.ds(r, 128), :] = lo
 
+    hid_load.wait()
     loop(4, 128, clip_in)
     pass_on(3)
     all_here(3)
@@ -815,6 +831,7 @@
         sums[4:5, :] += colsum(lo.astype(f32))
 
     loop(4, 128, norm_two)
+    out_save.start()
 
     def feed_back(t):
         cs = pl.ds(pl.multiple_of(t * CHUNK, CHUNK), CHUNK)
@@ -986,8 +1003,18 @@
             s4.at[slot, kind, p], r4.at[slot, min(kind, 1), p], on_z(to),
         )
 
+    def direct_copy(p, hop):
+        to = lax.rem(z + hop, 4)
+        return remote(
+            own_rows((CHUNKS - 1) % SLOTS, to, p, HALF, True), rd.at[hop - 1, p],
+            s7.at[hop - 1, p], r7.at[hop - 1, p], on_z(to),
+        )
+
+    def room_of(k):
+        return 2 if isinstance(k, int) else lax.rem(k, 2)
+
     def second_copy(k, w, p):
-        slot, duo = lax.rem(k, SLOTS), lax.rem(k, 2)
+        slot, duo = lax.rem(k, SLOTS), room_of(k)
         cs = lanes(0, w)
         return remote(
             held.at[duo, p, :, :, cs], ry.at[duo, p, :, :, cs], s5.at[slot, p], r5.at[slot, p],
@@ -1017,9 +1044,22 @@
     def finish_first(k, w):
         for p in range(2):
             back_first(k, w, p).wait()
+        fin_save(k, w).start()
+
+    def fin_save(k, w):
+        if w == CHUNK:
+            flat = k * CHUNK
+        else:
+            flat = WIDE * CHUNK + (k - WIDE) * w
+        cs = pl.ds(pl.multiple_of(lax.rem(flat, FF), 128), w)
+        at = (lax.div(flat, FF), slice(None), slice(None), slice(None), cs)
+        return pltpu.make_async_copy(fin.at[at], fin_to.at[at], fsem.at[lax.rem(k, SLOTS)])
+
+    def finish_save(k, w):
+        fin_save(k, w).wait()
 
     def finish_second(k, w):
-        duo = lax.rem(k, 2)
+        duo = room_of(k)
         for p in range(2):
             second_copy(k, w, p).wait()
             for i in range(2):
@@ -1077,19 +1117,39 @@
                 for kind in (2, 1, 0):
                     out_copy(k, w, p, kind).start()
 
+    def add_first(k, w, p):
+        slot, duo = lax.rem(k, SLOTS), lax.rem(k, 2)
+        first_copy(k, w, p).wait()
+        for q in range(4):
+            for i in range(2):
+                at = (x, i) if p == 0 else (i, y)
+                at = (slot, q, core, *at, slice(None), lanes(p, w))
+                pt[at] += rx[duo, p, q, i, :, lanes(0, w)]
+
     def finish_one(k, w):
-        slot, duo = lax.rem(k, SLOTS), lax.rem(k, 2)
         for p in range(2):
-            first_copy(k, w, p).wait()
-            for q in range(4):
-                for i in range(2):
-                    at = (x, i) if p == 0 else (i, y)
-                    at = (slot, q, core, *at, slice(None), lanes(p, w))
-                    pt[at] += rx[duo, p, q, i, :, lanes(0, w)]
+            add_first(k, w, p)
 
             @pl.when(outer)
             def _():
                 in_copy(k, w, p).start()
+
+    def last_one():
+        for p in range(2):
+            add_first(CHUNKS - 1, HALF, p)
+            for hop in (2, 1, 3):
+                direct_copy(p, hop).start()
+
+    def last_direct():
+        slot = (CHUNKS - 1) % SLOTS
+        for p in range(2):
+            for hop in (1, 3, 2):
+                direct_copy(p, hop).wait()
+            for i in range(2):
+                at = (x, i) if p == 0 else (i, y)
+                own = pt[(slot, z, core, *at, slice(None), lanes(p, HALF))]
+                held[2, p, i, :, lanes(0, HALF)] = own + rd[0, p, i] + rd[1, p, i] + rd[2, p, i]
+            second_copy(CHUNKS - 1, HALF, p).start()
 
     def finish_core(k, w):
         slot, duo = lax.rem(k, SLOTS), lax.rem(k, 2)
@@ -1101,9 +1161,14 @@
             first_copy(k, w, p).start()
 
     stages = (
-        (6, finish_first), (5, finish_second), (4, finish_out), (3, finish_in), (2, finish_one),
-        (1, finish_core),
-    )
+        (7, finish_save), (6, finish_first), (5, finish_second), (4, finish_out), (3, finish_in),
+        (2, finish_one), (1, finish_core),
+    )
+    last = CHUNKS - 1
+    last_stages = {
+        5: lambda: finish_second(last, HALF), 4: last_direct, 2: last_one,
+        6: lambda: finish_first(last, HALF), 1: lambda: finish_core(last, HALF),
+    }
 
     def tick(t, carry):
         for lag, step in stages:
@@ -1112,9 +1177,15 @@
             def _():
                 step(t - lag, CHUNK)
 
-            @pl.when((t >= lag + WIDE) & (t < lag + CHUNKS))
+            @pl.when(t == lag + WIDE)
             def _():
                 step(t - lag, HALF)
+
+            if lag in last_stages:
+
+                @pl.when(t == last + lag - (1 if lag > 2 else 0))
+                def _():
+                    last_stages[lag]()
 
         slot = lax.rem(t, SLOTS)
 
@@ -1170,7 +1241,7 @@
             whole(xlT[...], qkv[:, cs], 0)
             core_copy(t, HALF).start()
 
-        for when, turn in ((3, turn_inputs), (4, turn_context), (5, turn_widen)):
+        for when, turn in ((2, turn_inputs), (3, turn_context), (4, turn_widen)):
 
             @pl.when(t == when)
             def _():
@@ -1179,7 +1250,11 @@
         units = 12 // SECTION
         begin = SECTION + 1
 
-        @pl.when(t < SECTION)
+        @pl.when((t >= 1) & (t < SECTION))
+        def _():
+            feed_back(t - 1)
+
+        @pl.when(t == SECTION - 1)
         def _():
             feed_back(t)
 
@@ -1210,6 +1285,7 @@
 
         @pl.when(t == done + 3)
         def _():
+            acc_save.start()
             close_sums()
             small_copy(0).start()
 
@@ -1240,7 +1316,11 @@
 
         return carry
 
-    lax.fori_loop(0, CHUNKS + 6, tick, 0)
+    lax.fori_loop(0, CHUNKS + 5, tick, 0)
+    fin_save(WIDE, HALF).wait()
+    fin_save(last, HALF).wait()
+    for copy in (out_save, acc_save, kept_save):
+        copy.wait()
 
 
 def layer(*args):
@@ -1254,11 +1334,17 @@
             sds((ROWS, D), bf16),
             sds((ROWS, D), f32),
             sds((3, 2, 2, 24, FF), f32),
+            sds((72, D), jnp.int32),
             sds((16, D), f32),
         ),
-        in_specs=[sm] * 3 + [vm] * 7 + [pl.BlockSpec(memory_space=pl.ANY)] * 6,
-        out_specs=(vm,) * 4,
+        in_specs=[sm] * 3 + [vm] * 6 + [pl.BlockSpec(memory_space=pl.ANY)] * 7,
+        out_specs=(pl.BlockSpec(memory_space=pl.ANY),) * 4 + (vm,),
         scratch_shapes=[
+            pltpu.VMEM((ROWS, D), bf16),
+            pltpu.VMEM((ROWS, D), f32),
+            pltpu.VMEM((3, 2, 2, 24, FF), f32),
+            pltpu.VMEM((72, D), jnp.int32),
+            pltpu.VMEM((ROWS, D), bf16),
             pltpu.VMEM((8, 72, D), jnp.int32),
             pltpu.VMEM((8, 32, 128), f32),
             pltpu.VMEM((8, BLOCK, 128), f32),
@@ -1293,8 +1379,9 @@
             pltpu.VMEM((2, 2, 4, 2, 24, HALF), f32),
             pltpu.VMEM((2, 2, 3, 2, 24, HALF), f32),
             pltpu.VMEM((SLOTS, 2, 2, 2, 24, HALF), f32),
-            pltpu.VMEM((2, 2, 2, 24, HALF), f32),
-            pltpu.VMEM((2, 2, 2, 24, HALF), f32),
+            pltpu.VMEM((3, 2, 2, 24, HALF), f32),
+            pltpu.VMEM((3, 2, 2, 24, HALF), f32),
+            pltpu.VMEM((3, 2, 2, 24, HALF // 2), f32),
             pltpu.VMEM((6, 16, D), f32),
         ]
         + [dma((SLOTS,))] * 2
@@ -1302,32 +1389,24 @@
         + [dma((SLOTS, 3, 2)), dma((SLOTS, 2, 2))]
         + [dma((SLOTS, 2))] * 4
         + [dma((6,))] * 2
-        + [dma((2,)), dma((2, 4)), dma((4, 3)), dma((4, 3)), dma((4, 4)), dma((4, 4)), dma((1,))],
+        + [dma((2,)), dma((2, 4)), dma((4, 3)), dma((4, 3)), dma((4, 4)), dma((4, 4)), dma((5,)), dma((SLOTS,)), dma((3, 2)), dma((3, 2))],
         compiler_params=pltpu.CompilerParams(collective_id=0, has_side_effects=True, vmem_limit_bytes=LAYER_CAP),
         name="layer",
     )(*args)
 
 
 def finish_kernel(
-    count, fin, small, tl, ml, wl, nl,
-    tg, mg, wg, ng, tb, mb, wb, nb, gain, shift, clips, loss,
-    fbuf, tin, min_, win, nin, tout, mout, wout, nout, fsem, isem, osem,
+    count, small, kept, fin, tg, mg, wg, ng, tb, mb, wb, nb, gain, shift, clips, loss,
+    fbuf, turned, tout, mout, wout, nout, fsem, osem,
 ):
     fcopies = [pltpu.make_async_copy(fin.at[i], fbuf.at[i], fsem.at[i]) for i in range(3)]
-    icopies, ocopies = [], []
-    for half in range(2):
-        for index, (src, dst) in enumerate(((nl, nin), (wl, win), (ml, min_), (tl, tin))):
-            at = index * 2 + half
-            icopies.append(pltpu.make_async_copy(src.at[half], dst.at[half], isem.at[at]))
+    ocopies = []
     for half in range(2):
         for index, (src, dst) in enumerate(((nout, ng), (wout, wg), (mout, mg), (tout, tg))):
             at = index * 2 + half
             ocopies.append(pltpu.make_async_copy(src.at[half], dst.at[half], osem.at[at]))
-    for index in range(4):
-        if index < 3:
-            fcopies[index].start()
-        icopies[index].start()
-        icopies[index + 4].start()
+    for index in (1, 2, 0):
+        fcopies[index].start()
     me = lax.axis_index("fsdp")
     z = lax.div(me, 2)
     core = lax.rem(me, 2)
@@ -1345,55 +1424,58 @@
     lane = lax.broadcasted_iota(jnp.int32, (1, D), 1)
     for spot in range(4):
         clips[spot] = jnp.sum(jnp.where(lane == spot, line, 0.0))
-    loss[0, 0] = jnp.sum(jnp.where(lane == 4, line, 0.0)) * count[0]
-
-    def keep(latent, total, fan):
-        return jnp.where(jnp.abs(latent) <= 1.0, total * (1.0 / math.sqrt(fan)), 0.0)
-
-    def arrived(index):
-        icopies[index].wait()
-        icopies[index + 4].wait()
-
-    def leave(index):
-        ocopies[index].start()
-        ocopies[index + 4].start()
-
+    loss[0] = jnp.sum(jnp.where(lane == 4, line, 0.0)) * count[0]
+
+    def keep(block, half, group, total, fan):
+        word, bit = plane_of(block, half, group)
+        bits = kept[word * 8 : (word + 1) * 8, :] & jnp.int32(bit)
+        return jnp.where(bits != 0, total * (1.0 / math.sqrt(fan)), 0.0)
+
+    def spread_out(blocks, half, dst, src, at):
+        for index, block in enumerate(blocks):
+            cols = slice(index * D, (index + 1) * D)
+            for group in range(12):
+                rows = slice(group * 8, (group + 1) * 8)
+                total = src[rows, at + index * D : at + (index + 1) * D]
+                dst[half, rows, cols] = keep(block, half, group, total, D)
+
+    def leave(index, half):
+        ocopies[index + 4 * half].start()
+
+    fcopies[1].wait()
+    for half in range(2):
+        spread_out(range(4, 8), half, wout, fbuf.at[1], 0)
+        leave(1, half)
+    fcopies[2].wait()
+    for half in range(2):
+        spread_out(range(3), half, tout, fbuf.at[2], D)
+        leave(3, half)
+    for half in range(2):
+        spread_out(range(3, 4), half, mout, fbuf.at[2], 0)
+        leave(2, half)
     fcopies[0].wait()
-    arrived(0)
     for j in range(3):
         for i in range(2):
             tiles = range((j * 2 + i) * 4, (j * 2 + i) * 4 + 4)
             parts = [fbuf[0, :, tile * 128 : (tile + 1) * 128] for tile in tiles]
             total = jnp.concatenate(parts, axis=0).T
-            rows = slice(j * 128, (j + 1) * 128)
-            cols = slice(i * 384, (i + 1) * 384)
-            for half in range(2):
-                nout[half, rows, cols] = keep(nin[half, rows, cols], total, FF)
-    leave(0)
-    fcopies[1].wait()
-    arrived(1)
+            turned[j * 128 : (j + 1) * 128, i * 384 : (i + 1) * 384] = total
     for half in range(2):
-        wout[half] = keep(win[half], fbuf[1], D)
-    leave(1)
-    fcopies[2].wait()
-    arrived(2)
-    for half in range(2):
-        mout[half] = keep(min_[half], fbuf[2, :, 0:D], D)
-    leave(2)
-    arrived(3)
-    for half in range(2):
-        tout[half] = keep(tin[half], fbuf[2, :, D:], D)
-    leave(3)
+        for block in range(8, 12):
+            for group in range(12):
+                rows = slice((block - 8) * BLOCK + group * 8, (block - 8) * BLOCK + group * 8 + 8)
+                nout[half, rows, :] = keep(block, half, group, turned[rows, :], FF)
+        leave(0, half)
     for copy in ocopies:
         copy.wait()
 
 
-def finish(count, fin, small, tl, ml, wl, nl):
+def finish(count, small, kept, fin):
     vm = pl.BlockSpec(memory_space=pltpu.VMEM)
     sm = pl.BlockSpec(memory_space=pltpu.SMEM)
     hbm = pl.BlockSpec(memory_space=pl.ANY)
     sds = jax.ShapeDtypeStruct
-    shapes = [v.shape for v in (tl, ml, wl, nl)]
+    shapes = [(2, BLOCK, 3 * D), (2, BLOCK, D), (2, BLOCK, FF), (2, 4 * BLOCK, D)]
     dma = pltpu.SemaphoreType.DMA
     return pl.pallas_call(
         finish_kernel,
@@ -1401,16 +1483,16 @@
         + [
             sds((3, BLOCK), f32), sds((1, BLOCK), f32), sds((1, 4 * BLOCK), f32),
             sds((1, BLOCK), f32), sds((2, BLOCK), f32), sds((2, BLOCK), f32),
-            sds((4,), f32), sds((1, 1), f32),
+            sds((4,), f32), sds((1,), f32),
         ],
-        in_specs=[sm, hbm, vm] + [hbm] * 4,
+        in_specs=[sm, vm, vm, hbm],
         out_specs=[hbm] * 4 + [vm] * 6 + [sm] * 2,
-        scratch_shapes=[pltpu.VMEM((3, BLOCK, FF), f32)]
-        + [pltpu.VMEM(v, f32) for v in shapes] * 2
-        + [dma((3,)), dma((8,)), dma((8,))],
+        scratch_shapes=[pltpu.VMEM((3, BLOCK, FF), f32), pltpu.VMEM((4 * BLOCK, D), f32)]
+        + [pltpu.VMEM(v, f32) for v in shapes]
+        + [dma((3,)), dma((8,))],
         compiler_params=pltpu.CompilerParams(vmem_limit_bytes=VMEM_CAP),
         name="finish",
-    )(count, fin, small, tl, ml, wl, nl)
+    )(count, small, kept, fin)
 
 
 def on_device_fast(
@@ -1418,8 +1500,8 @@
     mixing_latent, widen_latent, narrow_latent, triple_bias, mixing_bias, widen_bias, narrow_bias,
     norm_gain, norm_shift, clip_level,
 ):
-    out, input_grad, fin, small_sum = layer(
-        seq_lengths, live_counts, clip_level, triple_bias, mixing_bias[None], widen_bias[None],
+    out, input_grad, fin, kept, small_sum = layer(
+        seq_lengths, live_counts, clip_level, triple_bias, mixing_bias[None], widen_bias,
         narrow_bias[None], norm_gain, norm_shift, hidden_in, teacher_hidden,
         jnp.transpose(teacher_scores, (1, 0, 2)), triple_latent, mixing_latent, widen_latent,
         narrow_latent,
@@ -1428,10 +1510,10 @@
     tokens = hidden_in.shape[0] * lax.axis_size("dp") * lax.axis_size("fsdp")
     count = jnp.full((1,), 1.0 / (tokens * D), f32)
     tg, mg, wg, ng, tb, mb, wb, nb, gain, shift, clips, loss = finish(
-        count, fin, small_sum, triple_latent, mixing_latent, widen_latent, narrow_latent
+        count, small_sum, kept, fin
     )
     return (
-        out, loss.reshape(()), input_grad, tg, mg, wg, ng, tb, mb.reshape(BLOCK),
+        out, loss[0], input_grad, tg, mg, wg, ng, tb, mb.reshape(BLOCK),
         wb.reshape(4 * BLOCK), nb.reshape(BLOCK), gain, shift, clips,
     )
 

time: 215 us -> 209 us (0.972)
  Pallas kernels: 209 us -> 205 us
    pallas_call x1, Pallas kernels: 201 us -> 199 us  [layer(): pl.pallas_call(layer_kernel, out_shape=(sds((ROWS, D), bf16), sds((ROWS,...]
where the time goes in v5:
time: 209 us
  Pallas kernels  205 us (98%)
    pallas_call x1, Pallas kernels, layer(): pl.pallas_call(layer_kernel, out_shape=(sds((ROWS, D), bf16), sds((ROWS,...  199 us
    pallas_call x1, Pallas kernels, finish(): pl.pallas_call(finish_kernel, out_shape=[sds(v, f32) for v in shapes] + [...  6.19 us

profile of v5, /device:TPU:0, one launch (start us, length us, event | category | flops | bytes accessed | tf_op | source)
XLA Modules:
  0.0 208.8 jit_solution(41372137951116346)
XLA Ops:
  0.7 198.7 %layer.1 = (bf16[512,768]{1,0:T(8,128)(2,1)}, f32[512,768]{1,0:T(8,128)}, f32[3,2,2,24,3072]{4,3,2,1,0:T(8,128)}, s32[72,768]{1,0:T(8,128)}, f32[16,768]{1,0:T(8,128)}) custom-call(s32[1,4]{1,0:T(1,128)} %seq.1, s32[1,3]{1,0:T(1,128)} %live.1, f32[4]{0:T(128)} %level.1, f32[3,96]{1,0:T(4,128)} %tb.1, f32[1,96]{1,0:T(1,128)} %bitcast.9, f32[384]{0:T(512)} %wb.1, ...), custom_call_target="tpu_custom_call" | custom-call | tf_op jit(solution)/shard_map/layer/pallas_call | solution.py:1331
  199.3 0.0 copy-start.1
  199.3 0.0 copy-start
  199.3 6.2 %finish.1 = (f32[2,96,2304]{2,1,0:T(8,128)}, f32[2,96,768]{2,1,0:T(8,128)}, f32[2,96,3072]{2,1,0:T(8,128)}, f32[2,384,768]{2,1,0:T(8,128)}, f32[3,96]{1,0:T(4,12...) custom-call(f32[1]{0:T(128)} %constant.0.clone.1.count, ...), custom_call_target="tpu_custom_call" | custom-call | tf_op jit(solution)/shard_map/finish/pallas_call | solution.py:1480
  205.5 1.3 reduce
  206.8 0.0 copy-done.1
  206.8 0.9 copy.32
  207.7 0.0 copy-done
  207.7 1.1 copy.33
Async XLA Ops:
  199.3 7.5 %copy-start.1 = (bf16[512,768]{1,0:T(8,128)(2,1)S(1)}, bf16[512,768]{1,0:T(8,128)(2,1)}, u32[]{:S(2)}) copy-start(bf16[512,768]{1,0:T(8,128)(2,1)} %get-tuple-element.62) | copy-start | bytes 2359300
  199.3 8.4 %copy-start = (f32[512,768]{1,0:T(8,128)S(1)}, f32[512,768]{1,0:T(8,128)}, u32[]{:S(2)}) copy-start(f32[512,768]{1,0:T(8,128)} %get-tuple-element.64) | copy-start | bytes 4718596

commit v6 on v5

--- a/solution.py
+++ b/solution.py
@@ -435,9 +435,10 @@
     return place // 32, (1 << bit) if bit < 31 else -(1 << 31)
 
 
-def unpack_block(words, scl, block, dst):
+def unpack_blocks(words, scl, blocks, dst):
     def one(owner, carry):
-        unpack_owner(words, scl, block, dst, owner)
+        for block in blocks:
+            unpack_owner(words, scl, block, dst, owner)
         return carry
 
     lax.fori_loop(0, 8, one, 0)
@@ -626,7 +627,11 @@
         loads[half][3].wait()
     slot_lane = lax.broadcasted_iota(jnp.int32, (8, 128), 1)
 
-    def scale_rows(group):
+    def scale_rows(pair):
+        for part in range(2):
+            scale_group(pl.multiple_of(pair + part * 8, 8))
+
+    def scale_group(group):
         tile = jnp.zeros((8, 128), f32)
         for half in range(2):
             rows = pl.ds(pl.multiple_of(192 + half * BLOCK + group, 8), 8)
@@ -645,7 +650,7 @@
                 tile = jnp.where(slot_lane == index * 2 + half, mean / math.sqrt(fan), tile)
         spread[pl.ds(group, 8), :] = tile
 
-    loop(12, 8, scale_rows)
+    loop(6, 16, scale_rows)
     spread[BLOCK:128, :] = jnp.zeros((128 - BLOCK, 128), f32)
     small[me, 0:16, :] = spread[...].T[0:16, :]
     small[me, 16:32, :] = jnp.zeros((16, 128), f32)
@@ -669,8 +674,8 @@
     col = lax.broadcasted_iota(jnp.int32, (256, 256), 1)
     key_ok = col < seq[0, 0]
     query_ok = row < seq[0, 0] * live[0, 0]
-    valid[0] = jnp.where(key_ok, 1.0, 0.0)
-    pair[0] = jnp.where(key_ok & query_ok, 1.0, 0.0)
+    valid[0] = jnp.where(key_ok, 1.0, 0.0).astype(bf16)
+    pair[0] = jnp.where(key_ok & query_ok, 1.0, 0.0).astype(bf16)
 
     def in_slots(at):
         mid = (at < 128) & (at < seq[0, 1])
@@ -685,8 +690,8 @@
     live_one = row * 0 + live[0, 2] > 0
     live_two = row * 0 + live[0, 2] > 1
     query_ok = (qm & live_mid) | (qo & live_one) | (qt & live_two)
-    valid[1] = jnp.where(key_ok, 1.0, 0.0)
-    pair[1] = jnp.where(key_ok & query_ok, 1.0, 0.0)
+    valid[1] = jnp.where(key_ok, 1.0, 0.0).astype(bf16)
+    pair[1] = jnp.where(key_ok & query_ok, 1.0, 0.0).astype(bf16)
     ones = jnp.where(query_ok, 1.0, 0.0)
 
     def clip_in(r):
@@ -695,7 +700,8 @@
         low[pl.ds(r, 128), :] = lo
 
     hid_load.wait()
-    loop(4, 128, clip_in)
+    for r in range(0, ROWS, 128):
+        clip_in(r)
     pass_on(3)
     all_here(3)
     total = jnp.zeros((16, D), f32)
@@ -752,20 +758,21 @@
         for c in range(0, D, 128):
             rs = slice(g * 256, (g + 1) * 256)
             q, k, v = (qkv[rs, at + c : at + c + 128] for at in (0, D, 2 * D))
-            ok = valid[g] > 0.5
+            ok = valid[g].astype(f32) > 0.5
             parts = []
             for j in range(2):
                 s, p = softmax(q, k, ok, j)
                 parts.append(dot_nn(p.astype(bf16), v))
             ctx[rs, c : c + 128] = jnp.where(first, parts[0], parts[1])
     pass_on(1)
-    unpack_block(words, scl, 3, wm)
+    unpack_blocks(words, scl, (3,), wm)
 
     def clip_ctx(r):
         lo = (c1 * jnp.tanh(ctx[pl.ds(r, 128), :] * i1)).astype(bf16)
         low[pl.ds(r, 128), :] = lo
 
-    loop(4, 128, clip_ctx)
+    for r in range(0, ROWS, 128):
+        clip_ctx(r)
 
     for part in range(3):
         cs = slice(part * 256, (part + 1) * 256)
@@ -784,13 +791,13 @@
     loop(4, 128, norm_one)
     all_here(1)
     pass_on(2)
-    for block in range(4, 8):
-        unpack_block(words, scl, block, ww)
+    unpack_blocks(words, scl, range(4, 8), ww)
     all_here(2)
-    for block in range(8, 12):
-        unpack_block(words, scl, block, wn)
 
     for t in range(8):
+        for owner in ((0, 1), (2,), (3,), (4,), (5,), (6,), (7,), ())[t]:
+            for block in range(8, 12):
+                unpack_owner(words, scl, block, wn, owner)
         if t < 6:
             cs = slice(t * 512, (t + 1) * 512)
             widened[:, cs] = dot_nn(low[...], ww[:, cs]) + wbias[0:1, cs]
@@ -908,8 +915,8 @@
         k = qkv[rs, pl.ds(k0, 128)]
         v = qkv[rs, pl.ds(v0, 128)]
         cg = cgrad[rs, pl.ds(q0, 128)]
-        ok = valid[g] > 0.5
-        pairs = pair[g] > 0.5
+        ok = valid[g].astype(f32) > 0.5
+        pairs = pair[g].astype(f32) > 0.5
         dq, dk, dv = [], [], []
         for j in range(2):
             s, p = softmax(q, k, ok, j)
@@ -1366,8 +1373,8 @@
             pltpu.VMEM((ROWS, FF), bf16),
             pltpu.VMEM((ROWS, D), f32),
             pltpu.VMEM((ROWS, D), bf16),
-            pltpu.VMEM((2, 256, 256), f32),
-            pltpu.VMEM((2, 256, 256), f32),
+            pltpu.VMEM((2, 256, 256), bf16),
+            pltpu.VMEM((2, 256, 256), bf16),
             pltpu.VMEM((D, ROWS), bf16),
             pltpu.VMEM((D, ROWS), bf16),
             pltpu.VMEM((D, ROWS), bf16),
@@ -1396,8 +1403,8 @@
 
 
 def finish_kernel(
-    count, small, kept, fin, tg, mg, wg, ng, tb, mb, wb, nb, gain, shift, clips, loss,
-    fbuf, turned, tout, mout, wout, nout, fsem, osem,
+    count, small, kept, fin, out_in, grad_in, out, grad, tg, mg, wg, ng, tb, mb, wb, nb, gain, shift, clips, loss,
+    fbuf, turned, tout, mout, wout, nout, obuf, gbuf, fsem, osem, psem,
 ):
     fcopies = [pltpu.make_async_copy(fin.at[i], fbuf.at[i], fsem.at[i]) for i in range(3)]
     ocopies = []
@@ -1407,6 +1414,16 @@
             ocopies.append(pltpu.make_async_copy(src.at[half], dst.at[half], osem.at[at]))
     for index in (1, 2, 0):
         fcopies[index].start()
+    arrive = [
+        pltpu.make_async_copy(out_in, obuf, psem.at[0]),
+        pltpu.make_async_copy(grad_in, gbuf, psem.at[1]),
+    ]
+    depart = [
+        pltpu.make_async_copy(obuf, out, psem.at[2]),
+        pltpu.make_async_copy(gbuf, grad, psem.at[3]),
+    ]
+    for copy in arrive:
+        copy.start()
     me = lax.axis_index("fsdp")
     z = lax.div(me, 2)
     core = lax.rem(me, 2)
@@ -1424,7 +1441,7 @@
     lane = lax.broadcasted_iota(jnp.int32, (1, D), 1)
     for spot in range(4):
         clips[spot] = jnp.sum(jnp.where(lane == spot, line, 0.0))
-    loss[0] = jnp.sum(jnp.where(lane == 4, line, 0.0)) * count[0]
+    loss[...] = jnp.sum(jnp.where(lane == 4, line, 0.0)) * count[0]
 
     def keep(block, half, group, total, fan):
         word, bit = plane_of(block, half, group)
@@ -1453,6 +1470,9 @@
     for half in range(2):
         spread_out(range(3, 4), half, mout, fbuf.at[2], 0)
         leave(2, half)
+    for index in range(2):
+        arrive[index].wait()
+        depart[index].start()
     fcopies[0].wait()
     for j in range(3):
         for i in range(2):
@@ -1466,11 +1486,11 @@
                 rows = slice((block - 8) * BLOCK + group * 8, (block - 8) * BLOCK + group * 8 + 8)
                 nout[half, rows, :] = keep(block, half, group, turned[rows, :], FF)
         leave(0, half)
-    for copy in ocopies:
+    for copy in depart + ocopies:
         copy.wait()
 
 
-def finish(count, small, kept, fin):
+def finish(count, small, kept, fin, out, grad):
     vm = pl.BlockSpec(memory_space=pltpu.VMEM)
     sm = pl.BlockSpec(memory_space=pltpu.SMEM)
     hbm = pl.BlockSpec(memory_space=pl.ANY)
@@ -1479,20 +1499,22 @@
     dma = pltpu.SemaphoreType.DMA
     return pl.pallas_call(
         finish_kernel,
-        out_shape=[sds(v, f32) for v in shapes]
+        out_shape=[sds((ROWS, D), bf16), sds((ROWS, D), f32)]
+        + [sds(v, f32) for v in shapes]
         + [
             sds((3, BLOCK), f32), sds((1, BLOCK), f32), sds((1, 4 * BLOCK), f32),
             sds((1, BLOCK), f32), sds((2, BLOCK), f32), sds((2, BLOCK), f32),
-            sds((4,), f32), sds((1,), f32),
+            sds((4,), f32), sds((), f32),
         ],
-        in_specs=[sm, vm, vm, hbm],
-        out_specs=[hbm] * 4 + [vm] * 6 + [sm] * 2,
+        in_specs=[sm, vm, vm, hbm, hbm, hbm],
+        out_specs=[hbm] * 6 + [vm] * 6 + [sm] * 2,
         scratch_shapes=[pltpu.VMEM((3, BLOCK, FF), f32), pltpu.VMEM((4 * BLOCK, D), f32)]
         + [pltpu.VMEM(v, f32) for v in shapes]
-        + [dma((3,)), dma((8,))],
+        + [pltpu.VMEM((ROWS, D), bf16), pltpu.VMEM((ROWS, D), f32)]
+        + [dma((3,)), dma((8,)), dma((4,))],
         compiler_params=pltpu.CompilerParams(vmem_limit_bytes=VMEM_CAP),
         name="finish",
-    )(count, small, kept, fin)
+    )(count, small, kept, fin, out, grad)
 
 
 def on_device_fast(
@@ -1509,11 +1531,11 @@
     fin = fin.reshape(3, BLOCK, FF)
     tokens = hidden_in.shape[0] * lax.axis_size("dp") * lax.axis_size("fsdp")
     count = jnp.full((1,), 1.0 / (tokens * D), f32)
-    tg, mg, wg, ng, tb, mb, wb, nb, gain, shift, clips, loss = finish(
-        count, small_sum, kept, fin
+    out, input_grad, tg, mg, wg, ng, tb, mb, wb, nb, gain, shift, clips, loss = finish(
+        count, small_sum, kept, fin, out, input_grad
     )
     return (
-        out, loss[0], input_grad, tg, mg, wg, ng, tb, mb.reshape(BLOCK),
+        out, loss, input_grad, tg, mg, wg, ng, tb, mb.reshape(BLOCK),
         wb.reshape(4 * BLOCK), nb.reshape(BLOCK), gain, shift, clips,
     )
 

time: 209 us -> 203 us (0.971)
  Pallas kernels: 205 us -> 201 us
    pallas_call x1, Pallas kernels: 199 us -> 194 us  [layer(): pl.pallas_call(layer_kernel, out_shape=(sds((ROWS, D), bf16), sds((ROWS,...]
where the time goes in v6:
time: 203 us
  Pallas kernels  201 us (99%)
    pallas_call x1, Pallas kernels, layer(): pl.pallas_call(layer_kernel, out_shape=(sds((ROWS, D), bf16), sds((ROWS,...  194 us
    pallas_call x1, Pallas kernels, finish(): pl.pallas_call(finish_kernel, out_shape=[sds((ROWS, D), bf16), sds((ROWS,...  7.07 us

profile of v6, /device:TPU:0, one launch (start us, length us, event | category | flops | bytes accessed | tf_op | source)
XLA Modules:
  0.0 202.5 jit_solution(17991422576851213716)
XLA Ops:
  0.7 193.5 %layer.1 = (bf16[512,768]{1,0:T(8,128)(2,1)}, f32[512,768]{1,0:T(8,128)}, f32[3,2,2,24,3072]{4,3,2,1,0:T(8,128)}, s32[72,768]{1,0:T(8,128)}, f32[16,768]{1,0:T(8,128)}) custom-call(s32[1,4]{1,0:T(1,128)} %seq.1, s32[1,3]{1,0:T(1,128)} %live.1, f32[4]{0:T(128)} %level.1, f32[3,96]{1,0:T(4,128)} %tb.1, f32[1,96]{1,0:T(1,128)} %bitcast.8, f32[384]{0:T(512)} %wb.1, ...), custom_call_target="tpu_custom_call" | custom-call | tf_op jit(solution)/shard_map/layer/pallas_call | solution.py:1338
  194.2 7.1 %finish.1 = (bf16[512,768]{1,0:T(8,128)(2,1)}, f32[512,768]{1,0:T(8,128)}, f32[2,96,2304]{2,1,0:T(8,128)}, f32[2,96,768]{2,1,0:T(8,128)}, f32[2,96,3072]{2,1,0:T...) custom-call(f32[1]{0:T(128)} %constant.0.clone.1.count, ...), custom_call_target="tpu_custom_call" | custom-call | tf_op jit(solution)/shard_map/finish/pallas_call | solution.py:1500
  201.3 1.3 reduce

commit v7 on v6

--- a/solution.py
+++ b/solution.py
@@ -553,11 +553,9 @@
                 nl.at[half], (ctx if half == 0 else sgrad).at[0 : 4 * BLOCK, :], lsem.at[half, 3]
             ),
         ])
-    for index in range(4):
+    for index in range(2):
         for half in range(2):
             loads[half][index].start()
-    hid_load.start()
-    teach_load.start()
 
     def latent_piece(block, half, group):
         if block < 4:
@@ -618,6 +616,11 @@
     for half in range(2):
         loads[half][0].wait()
         loads[half][1].wait()
+    for index in range(2, 4):
+        for half in range(2):
+            loads[half][index].start()
+    hid_load.start()
+    teach_load.start()
     for word in range(3):
         pack(word)
     pl.semaphore_wait(greet, 6)

time: 203 us -> 203 us (level)
  no operation moved by 1% of the time
where the time goes in v7:
time: 203 us
  Pallas kernels  201 us (99%)
    pallas_call x1, Pallas kernels, layer(): pl.pallas_call(layer_kernel, out_shape=(sds((ROWS, D), bf16), sds((ROWS,...  193 us
    pallas_call x1, Pallas kernels, finish(): pl.pallas_call(finish_kernel, out_shape=[sds((ROWS, D), bf16), sds((ROWS,...  7.07 us

profile of v7, /device:TPU:0, one launch (start us, length us, event | category | flops | bytes accessed | tf_op | source)
XLA Modules:
  0.0 202.5 jit_solution(2691212100501388618)
XLA Ops:
  0.7 193.5 %layer.1 = (bf16[512,768]{1,0:T(8,128)(2,1)}, f32[512,768]{1,0:T(8,128)}, f32[3,2,2,24,3072]{4,3,2,1,0:T(8,128)}, s32[72,768]{1,0:T(8,128)}, f32[16,768]{1,0:T(8,128)}) custom-call(s32[1,4]{1,0:T(1,128)} %seq.1, s32[1,3]{1,0:T(1,128)} %live.1, f32[4]{0:T(128)} %level.1, f32[3,96]{1,0:T(4,128)} %tb.1, f32[1,96]{1,0:T(1,128)} %bitcast.8, f32[384]{0:T(512)} %wb.1, ...), custom_call_target="tpu_custom_call" | custom-call | tf_op jit(solution)/shard_map/layer/pallas_call | solution.py:1341
  194.1 7.1 %finish.1 = (bf16[512,768]{1,0:T(8,128)(2,1)}, f32[512,768]{1,0:T(8,128)}, f32[2,96,2304]{2,1,0:T(8,128)}, f32[2,96,768]{2,1,0:T(8,128)}, f32[2,96,3072]{2,1,0:T...) custom-call(f32[1]{0:T(128)} %constant.0.clone.1.count, ...), custom_call_target="tpu_custom_call" | custom-call | tf_op jit(solution)/shard_map/finish/pallas_call | solution.py:1503
  201.2 1.3 reduce

commit v8 on v6

--- a/solution.py
+++ b/solution.py
@@ -1422,8 +1422,6 @@
         pltpu.make_async_copy(obuf, out, psem.at[2]),
         pltpu.make_async_copy(gbuf, grad, psem.at[3]),
     ]
-    for copy in arrive:
-        copy.start()
     me = lax.axis_index("fsdp")
     z = lax.div(me, 2)
     core = lax.rem(me, 2)
@@ -1460,6 +1458,8 @@
         ocopies[index + 4 * half].start()
 
     fcopies[1].wait()
+    for copy in arrive:
+        copy.start()
     for half in range(2):
         spread_out(range(4, 8), half, wout, fbuf.at[1], 0)
         leave(1, half)

time: 203 us -> 204 us (level)
  no operation moved by 1% of the time
where the time goes in v8:
time: 204 us
  Pallas kernels  202 us (99%)
    pallas_call x1, Pallas kernels, layer(): pl.pallas_call(layer_kernel, out_shape=(sds((ROWS, D), bf16), sds((ROWS,...  194 us
    pallas_call x1, Pallas kernels, finish(): pl.pallas_call(finish_kernel, out_shape=[sds((ROWS, D), bf16), sds((ROWS,...  8.57 us

profile of v8, /device:TPU:0, one launch (start us, length us, event | category | flops | bytes accessed | tf_op | source)
XLA Modules:
  0.0 204.0 jit_solution(1800000680568949219)
XLA Ops:
  0.7 193.5 %layer.1 = (bf16[512,768]{1,0:T(8,128)(2,1)}, f32[512,768]{1,0:T(8,128)}, f32[3,2,2,24,3072]{4,3,2,1,0:T(8,128)}, s32[72,768]{1,0:T(8,128)}, f32[16,768]{1,0:T(8,128)}) custom-call(s32[1,4]{1,0:T(1,128)} %seq.1, s32[1,3]{1,0:T(1,128)} %live.1, f32[4]{0:T(128)} %level.1, f32[3,96]{1,0:T(4,128)} %tb.1, f32[1,96]{1,0:T(1,128)} %bitcast.8, f32[384]{0:T(512)} %wb.1, ...), custom_call_target="tpu_custom_call" | custom-call | tf_op jit(solution)/shard_map/layer/pallas_call | solution.py:1338
  194.2 8.6 %finish.1 = (bf16[512,768]{1,0:T(8,128)(2,1)}, f32[512,768]{1,0:T(8,128)}, f32[2,96,2304]{2,1,0:T(8,128)}, f32[2,96,768]{2,1,0:T(8,128)}, f32[2,96,3072]{2,1,0:T...) custom-call(f32[1]{0:T(128)} %constant.0.clone.1.count, ...), custom_call_target="tpu_custom_call" | custom-call | tf_op jit(solution)/shard_map/finish/pallas_call | solution.py:1500
  202.8 1.3 reduce
